TPU v7x, 128 devices: a whole 4x4x4 slice. The times are simulated.
128 devices in a mesh: row: 8 (over y, core), col: 16 (over x, z).
Axes of the slice: x: 4, y: 4, z: 4, core: 2. Of those that a mesh axis runs over, the one named last changes fastest.
Arguments:
- amp_tiles: bfloat16 [2048, 128, 128], P(('row', 'col')), may hold values from -6 to 6
- owner_col: int32 [2048, 1], P(('row', 'col')), may hold values from 0 to 15; in each aligned block of 16 rows (0 to 15, 16 to 31, ...) at most 2 rows name the same one
- local_pair: int32 [2048], P(('row', 'col')), may hold values from 0 to 31
- occ_pair: int32 [2048], P(('row', 'col')), may hold values from 0 to 15
- integrals: bfloat16 [65536, 8192], P('col', 'row'), may hold values from -0.046875 to 0.046875
Outputs:
- ladder: bfloat16 [2048, 8192], P('col', 'row')
Inputs may be any that keep to these rules, and one draw needn't show every extreme that they name: `owner_col`: among the 16 tiles of one device, at most 2 name the same owner, and in every draw some device sends exactly 2 tiles to some owner.
All inputs are finite; a program needn't handle non-finite values.
Results may differ from a plain program's by a relative error of at most 0.018.
Values may be sent and summed in bfloat16 or wider, within the bound.
No kernel may reach another device: no remote copies, remote signals or barrier semaphores. Data moves between devices by JAX's collectives and lax.ppermute only.
A program may use at most 128 MiB of HBM per device.

v0:
```python
import jax
import jax.numpy as jnp
from jax import lax
from jax.sharding import PartitionSpec as P

CAP = 2
CD_DEV = 32
OT_DEV = 1


def per_device(amp_tiles, owner_col, local_pair, occ_pair, integrals):
    ncol = lax.axis_size("col")
    count = amp_tiles.shape[0]
    side = amp_tiles.shape[1]
    occ_total = OT_DEV * ncol
    positions = occ_total * CD_DEV
    owners = owner_col[:, 0]
    order_ids = jnp.arange(count, dtype=jnp.int32)
    same = (owners[:, None] == owners[None, :]) & (order_ids[None, :] < order_ids[:, None])
    rank = jnp.sum(same.astype(jnp.int32), axis=1)
    slot = owners * CAP + rank
    target = occ_pair * CD_DEV + local_pair
    send_tiles = jnp.zeros((ncol * CAP, side, side), jnp.bfloat16).at[slot].set(amp_tiles)
    send_codes = jnp.full((ncol * CAP,), positions, jnp.int32).at[slot].set(target)
    got_tiles, got_codes = (
        lax.all_to_all(send_tiles, "col", split_axis=0, concat_axis=0, tiled=True),
        lax.all_to_all(send_codes, "col", split_axis=0, concat_axis=0, tiled=True),
    )
    all_tiles, all_codes = (
        lax.all_gather(got_tiles, "row", axis=0, tiled=True),
        lax.all_gather(got_codes, "row", axis=0, tiled=True),
    )
    placed = (
        jnp.zeros((positions, side, side), jnp.float32)
        .at[all_codes]
        .add(all_tiles.astype(jnp.float32), mode="drop")
    )
    matrix = placed.astype(jnp.bfloat16).reshape(occ_total, CD_DEV, side, side)
    matrix = matrix.transpose(0, 2, 1, 3).reshape(occ_total * side, CD_DEV * side)
    return lax.psum_scatter(
        jnp.dot(matrix, integrals, preferred_element_type=jnp.float32).astype(jnp.bfloat16),
        "col",
        scatter_dimension=0,
        tiled=True,
    )


def solution(mesh):
    return jax.shard_map(
        per_device,
        mesh=mesh,
        in_specs=(
            P(("row", "col"), None, None),
            P(("row", "col"), None),
            P(("row", "col")),
            P(("row", "col")),
            P("col", "row"),
        ),
        out_specs=P("col", "row"),
        check_vma=False,
    )
```

profile of v0, /device:TPU:1, one launch (start us, length us, event | category | flops | bytes accessed | tf_op | source)
XLA Modules:
  0.0 318.1 jit_solution(4286979656401644608)
XLA Ops:
  6.5 0.9 convert_reduce_fusion
  7.4 0.7 fusion.7
  8.1 0.2 broadcast_in_dim.19
  8.3 2.1 scatter_fusion
  10.4 24.2 %all_to_all.17 = bf16[32,128,128]{2,1,0:T(8,128)(2,1)} all-to-all(bf16[32,128,128]{2,1,0:T(8,128)(2,1)S(1)} %scatter_fusion), channel_id=1, replica_groups=mesh['row'=8,'col'=16] {'col'}, dimensions={0} | all-to-all | bytes 2097152 | tf_op jit(solution)/shard_map/all_to_all | solution.py:26
  34.7 0.7 multiply_add_fusion
  35.3 0.6 scatter_custom_fusion
  36.0 0.7 all_to_all.11
  36.6 3.6 %all-to-all-start = ((s32[16,2,1]{1,2,0:T(1,128)}), s32[16,2,1]{1,2,0:T(1,128)S(1)}, u32[]{:S(2)}, u32[]{:S(2)}) async-start(s32[16,2,1]{1,2,0:T(1,128)} %bitcast.3), calls=%async_computation | async-start | bytes 16384 | tf_op jit(solution)/shard_map/all_to_all | solution.py:27
  40.3 1.3 dynamic-slice
  42.3 4.4 %all-to-all-done = s32[16,2,1]{1,2,0:T(1,128)S(1)} async-done(((s32[16,2,1]{1,2,0:T(1,128)}), s32[16,2,1]{1,2,0:T(1,128)S(1)}, u32[]{:S(2)}, u32[]{:S(2)}) %all-to-all-start) | async-done | bytes 160 | tf_op jit(solution)/shard_map/all_to_all | solution.py:27
  46.6 0.5 broadcast.27
  47.1 0.7 reduce.3
  47.8 0.1 reshape.37
  47.9 0.2 dynamic-update-slice
  48.2 11.1 %all-reduce = s32[256]{0:T(256)S(1)} all-reduce(s32[256]{0:T(256)S(1)} %dynamic-update-slice), channel_id=1, replica_groups=mesh['row'=8,'col'=16] {'row'}, use_global_device_ids=true, to_apply=%add | all-reduce | flops 256 | bytes 2048
  59.3 25.4 %all-gather.2.cloned.1.call-done = bf16[256,128,128]{2,1,0:T(8,128)(2,1)} async-done(((bf16[32,128,128]{2,1,0:T(8,128)(2,1)}), bf16[256,128,128]{2,1,0:T(8,128)(2,1)}) %all-gather.2.cloned.1.call-update) | async-done | bytes 8388624 | tf_op jit(solution)/shard_map/all_gather | solution.py:30
  84.7 11.2 %convert_element_type.13 = f32[256,128,128]{2,1,0:T(8,128)} convert(bf16[256,128,128]{2,1,0:T(8,128)(2,1)} %all-gather.2.cloned.1.call-done) | non-fusion elementwise | flops 4194304 | bytes 25165824 | tf_op jit(solution)/shard_map/convert_element_type | solution.py:36
  95.9 11.2 %broadcast_in_dim.16 = f32[512,128,128]{2,1,0:T(8,128)} broadcast(f32[]{:T(128)} %constant.6.clone.1), dimensions={} | broadcast | bytes 33554436 | tf_op jit(solution)/shard_map/broadcast_in_dim | solution.py:34
  107.1 52.2 %scatter_fusion.1 = f32[512,128,128]{2,1,0:T(8,128)} fusion(f32[512,128,128]{2,1,0:T(8,128)} %broadcast_in_dim.16, s32[256]{0:T(256)S(1)} %compare_select_fusion, f32[256,128,128]{2,1,0:T(8,128)} %convert_element_type.13), kind=kCustom, calls=%fused_computation.2 | custom fusion | flops 4194304 | bytes 50332672 | tf_op jit(solution)/shard_map/scatter-add | solution.py:36
  159.3 12.3 %convert_element_type.14 = bf16[512,128,128]{2,1,0:T(8,128)(2,1)S(1)} convert(f32[512,128,128]{2,1,0:T(8,128)} %scatter_fusion.1) | non-fusion elementwise | flops 8388608 | bytes 50331648 | tf_op jit(solution)/shard_map/convert_element_type | solution.py:38
  171.6 43.2 %copy.10 = bf16[16,128,32,128]{3,2,1,0:T(8,128)(2,1)S(1)} copy(bf16[16,128,32,128]{3,1,2,0:T(8,128)(2,1)S(1)} %bitcast.23) | data formatting | bytes 33554432 | tf_op jit(solution)/shard_map/transpose | solution.py:39
  214.8 22.6 %fusion.3 = bf16[2048,1024]{1,0:T(8,128)(2,1)} fusion(bf16[4096,1024]{1,0:T(8,128)(2,1)} %param.9, bf16[256,8,32,128]{3,2,1,0:T(8,128)(2,1)S(1)} %bitcast.24), kind=kOutput, calls=%fused_computation.6 | convolution fusion | flops 17181966336 | bytes 29360128 | tf_op jit(solution)/shard_map/dot_general | solution.py:41
  237.5 73.8 %reduce-scatter.2.cloned.1.call-done = bf16[128,1024]{1,0:T(8,128)(2,1)} async-done(((bf16[2048,1024]{1,0:T(8,128)(2,1)}), bf16[128,1024]{1,0:T(8,128)(2,1)}) %reduce-scatter.2.cloned.1.call-update) | async-done | bytes 262160 | tf_op jit(solution)/shard_map/reduce_scatter | solution.py:40
  (6 shorter events, 0.1 us)
Async XLA Ops:
  6.5 78.1 %all-gather.2.cloned.1.call-start = ((), (), s32[]{:S(2)}) async-start(), calls=%async_computation.3 | async-start | bytes 9437184 | tf_op jit(solution)/shard_map/all_gather | solution.py:30
  36.6 10.0 %all-to-all-start = ((s32[16,2,1]{1,2,0:T(1,128)}), s32[16,2,1]{1,2,0:T(1,128)S(1)}, u32[]{:S(2)}, u32[]{:S(2)}) async-start(s32[16,2,1]{1,2,0:T(1,128)} %bitcast.3), calls=%async_computation | async-start | bytes 16384 | tf_op jit(solution)/shard_map/all_to_all | solution.py:27
  40.3 271.0 %reduce-scatter.2.cloned.1.call-start = ((), (), s32[]{:S(2)}) async-start(), calls=%async_computation.4 | async-start | bytes 4456448 | tf_op jit(solution)/shard_map/reduce_scatter | solution.py:40
Sparse Core Ops, SparseCore 0:
  34.8 49.8 all-gather.1
  237.6 73.6 reduce-scatter.1
where the time goes:
time: 320 us; the launch traced here: 318 us
  waiting for transfers between devices  104 us (32%)
  other arithmetic  78.6 us (25%)
  local copies, waits for them, and re-layouts  60.2 us (19%)
  blocking collectives  35.3 us (11%)
  matrix products  22.6 us (7%)
  between operations  14.1 us (4%)
  starting transfers between devices  3.68 us (1%)
    reduce_scatter x1, waiting for transfers between devices, per_device(): lax.psum_scatter(jnp.dot(matrix, integrals, preferred_element_type=jnp.fl...  73.8 us
    scatter-add x1, other arithmetic, per_device(): placed = jnp.zeros((positions, side, side), jnp.float32).at[all_codes].ad...  52.2 us
    transpose x1, local copies, waits for them, and re-layouts, per_device(): matrix.transpose(0, 2, 1, 3).reshape(occ_total * side, CD_DEV * side)  43.2 us
    all_gather x1, waiting for transfers between devices, per_device(): lax.all_gather(got_tiles, 'row', axis=0, tiled=True)  25.4 us
    all_to_all x1, blocking collectives, per_device(): lax.all_to_all(send_tiles, 'col', split_axis=0, concat_axis=0, tiled=True)  24.2 us
    dot_general x1, matrix products, per_device(): jnp.dot(matrix, integrals, preferred_element_type=jnp.float32)  22.6 us
    convert_element_type x1, other arithmetic, per_device(): matrix = placed.astype(jnp.bfloat16).reshape(occ_total, CD_DEV, side, side)  12.3 us
    broadcast_in_dim x1, local copies, waits for them, and re-layouts, per_device(): jnp.zeros((positions, side, side), jnp.float32).at[all_codes]  11.2 us
  transfers between devices with their start and end apart: 3, of which 3 were waited for; matrix products, arithmetic and copies ran while one was open for 1% of the time, Pallas kernels for 0%

commit v1 on v0

v1 whole, which is shorter than its diff:
```python
import jax
import jax.numpy as jnp
from jax import lax
from jax.experimental import pallas as pl
from jax.experimental.pallas import tpu as pltpu
from jax.sharding import PartitionSpec as P

SIDE = 128
CAP = 2
RING = 4
SLOTS = RING * CAP
HEAD = 16
MSG = SLOTS * SIDE + HEAD
PIECE = RING * MSG
OCC = RING * RING
DUMMY = OCC
UNROLL = 8

VMEM = pl.BlockSpec(memory_space=pltpu.VMEM)
SMEM = pl.BlockSpec(memory_space=pltpu.SMEM)
F32, BF16, I32 = jnp.float32, jnp.bfloat16, jnp.int32


def row_perm(step):
    return [(r, (r + 2 * step) % (2 * RING)) for r in range(2 * RING)]


CORE_PERM = [(r, r ^ 1) for r in range(2 * RING)]


def plane_perm(step, second):
    pairs = []
    for r in range(2 * RING):
        for x in range(RING):
            for z in range(RING):
                along_x = (r % 2 == 0) != second
                nx, nz = ((x + step) % RING, z) if along_x else (x, (z + step) % RING)
                pairs.append((r * OCC + x * RING + z, r * OCC + nx * RING + nz))
    return pairs


def send_first(v, step):
    return lax.ppermute(v, ("row", "col"), plane_perm(step, False))


def send_second(v, step):
    return lax.ppermute(v, ("row", "col"), plane_perm(step, True))


def send_y(v, step):
    return lax.ppermute(v, "row", row_perm(step))


def send_core(v):
    return lax.ppermute(v, "row", CORE_PERM)


def place():
    core = lax.rem(lax.axis_index("row"), 2)
    col = lax.axis_index("col")
    x, z = col // RING, lax.rem(col, RING)
    first = core == 0
    return first, jnp.where(first, x, z), jnp.where(first, z, x)


def relative(index, first, a, b):
    x, z = index >> 2, index & 3
    return (jnp.where(first, x, z) - a) & 3, (jnp.where(first, z, x) - b) & 3


def params(mib):
    return pltpu.CompilerParams(vmem_limit_bytes=mib * 2**20)


def header(occ_row, loc_row):
    rows = lax.broadcasted_iota(I32, (HEAD, SIDE), 0)
    occ = jnp.broadcast_to(occ_row, (HEAD, SIDE))
    loc = jnp.broadcast_to(loc_row, (HEAD, SIDE))
    return jnp.where(rows == 0, occ, jnp.where(rows == 1, loc, 0.0)).astype(BF16)


def sort_tiles_kernel(meta, tiles, *refs):
    outs, seen = refs[:RING], refs[RING]
    first, a, b = place()
    count = tiles.shape[0]
    for o in range(OCC):
        seen[o] = 0
    rows = lax.broadcasted_iota(I32, (8, SIDE), 0)
    lanes = lax.broadcasted_iota(I32, (8, SIDE), 1)
    occ_of = jnp.zeros((8, SIDE), F32)
    loc_of = jnp.zeros((8, SIDE), F32)
    for k in range(count):
        owner, loc, occ = meta[k], meta[count + k], meta[2 * count + k]
        rank = seen[owner]
        seen[owner] = rank + 1
        da, db = relative(owner, first, a, b)
        slot = db * CAP + rank
        here = (rows == da) & (lanes == slot)
        occ_of = jnp.where(here, (occ + 1).astype(F32), occ_of)
        loc_of = jnp.where(here, loc.astype(F32), loc_of)
        at = pl.ds(pl.multiple_of(slot * SIDE, SIDE), SIDE)
        for d in range(RING):

            @pl.when(da == d)
            def _(d=d, k=k, at=at):
                outs[d][at, :] = tiles[k]

    for d in range(RING):
        outs[d][SLOTS * SIDE :, :] = header(occ_of[d : d + 1], loc_of[d : d + 1])


def sort_tiles(meta, tiles):
    return pl.pallas_call(
        sort_tiles_kernel,
        in_specs=[SMEM, VMEM],
        out_specs=[VMEM] * RING,
        out_shape=[jax.ShapeDtypeStruct((MSG, SIDE), BF16)] * RING,
        scratch_shapes=[pltpu.SMEM((OCC,), I32)],
        compiler_params=params(8),
        name="sort_tiles",
    )(meta, tiles)


def turn_kernel(*refs):
    ins, outs = refs[:RING], refs[RING:]
    lanes = lax.broadcasted_iota(I32, (HEAD, SIDE), 1)
    heads = [r[SLOTS * SIDE :, :].astype(F32) for r in ins]
    for db in range(RING):
        head = jnp.zeros((HEAD, SIDE), F32)
        for da in range(RING):
            outs[db][da * CAP * SIDE : (da + 1) * CAP * SIDE, :] = ins[da][db * CAP * SIDE : (db + 1) * CAP * SIDE, :]
            turned = pltpu.roll(heads[da], ((da - db) * CAP) % SIDE, 1)
            head = jnp.where((lanes >= da * CAP) & (lanes < (da + 1) * CAP), turned, head)
        outs[db][SLOTS * SIDE :, :] = head.astype(BF16)


def turn(parts):
    return pl.pallas_call(
        turn_kernel,
        in_specs=[VMEM] * RING,
        out_specs=[VMEM] * RING,
        out_shape=[jax.ShapeDtypeStruct((MSG, SIDE), BF16)] * RING,
        compiler_params=params(8),
        name="turn",
    )(*parts)


def multiply_tiles(pieces, ints, acc, head_v, head_s, row_s, code_s, block_of, dummy):
    first, a, b = place()
    n = len(pieces)
    heads = []
    for piece in pieces:
        for m in range(RING):
            at = m * MSG + SLOTS * SIDE
            heads.append(piece[at : at + HEAD, :].astype(F32)[0:8].astype(I32))
    for i, h in enumerate(heads):
        occ = jnp.broadcast_to(h[0:1], (8, SIDE)) - 1
        loc = jnp.broadcast_to(h[1:2], (8, SIDE))
        da, db = relative(occ, first, a, b)
        wanted, block = block_of(da, db)
        head_v[i * 8 : (i + 1) * 8, :] = jnp.where((occ >= 0) & wanted, block * 32 + loc, -1)
    pltpu.sync_copy(head_v, head_s)
    for p, piece in enumerate(pieces):
        count = jnp.int32(0)
        for m in range(RING):
            for s in range(SLOTS):
                code = head_s[(p * RING + m) * 8, s]
                row_s[count] = m * MSG + s * SIDE
                code_s[count] = code
                count = count + (code >= 0).astype(I32)
        for i in range(UNROLL):
            row_s[count + i] = 0
            code_s[count + i] = dummy * 32

        def step(k):
            code = code_s[k]
            at = pl.multiple_of(row_s[k], 16)
            block = pl.multiple_of((code >> 5) * SIDE, SIDE)
            rows = pl.multiple_of((code & 31) * SIDE, SIDE)
            acc[pl.ds(block, SIDE), :] += jnp.dot(
                piece[pl.ds(at, SIDE), :], ints[pl.ds(rows, SIDE), :], preferred_element_type=F32
            )

        def body(i, carry):
            for u in range(UNROLL):
                step(i * UNROLL + u)
            return carry

        lax.fori_loop(0, (count + UNROLL - 1) // UNROLL, body, 0)


def list_scratch(n):
    return [
        pltpu.VMEM((n * RING * 8, SIDE), I32),
        pltpu.SMEM((n * RING * 8, SIDE), I32),
        pltpu.SMEM((RING * SLOTS + UNROLL,), I32),
        pltpu.SMEM((RING * SLOTS + UNROLL,), I32),
    ]


def kept(v):
    return pltpu.with_memory_space_constraint(v, pltpu.VMEM)


def all_blocks(da, db):
    return da >= 0, da * RING + db


def accumulate(total, ints, pieces, flops):
    n = len(pieces)
    width = ints.shape[1]
    old = [] if total is None else [total]

    def kernel(*refs):
        refs = refs[len(old) :]
        ints_ref, piece_refs, acc, scratch = refs[0], refs[1 : 1 + n], refs[1 + n], refs[2 + n :]
        if not old:
            acc[...] = jnp.zeros_like(acc)
        multiply_tiles(piece_refs, ints_ref, acc, *scratch, all_blocks, DUMMY)

    return pl.pallas_call(
        kernel,
        in_specs=[VMEM] * (len(old) + 1 + n),
        out_specs=VMEM,
        out_shape=pltpu.VMEM(((OCC + 1) * SIDE, width), F32),
        scratch_shapes=list_scratch(n),
        input_output_aliases={0: 0} if old else {},
        compiler_params=params(14),
        cost_estimate=pl.CostEstimate(flops=flops, bytes_accessed=2**22, transcendentals=0),
        name="accumulate",
    )(*[kept(v) for v in old], kept(ints), *pieces)


def finish(total, ints, pieces, blocks, block_of, outs, flops):
    n = len(pieces)
    width = ints.shape[1]
    size = len(blocks)

    def kernel(*refs):
        total_ref, ints_ref, piece_refs = refs[0], refs[1], refs[2 : 2 + n]
        out_refs = refs[2 + n : 2 + n + len(outs)]
        acc, scratch = refs[2 + n + len(outs)], refs[3 + n + len(outs) :]
        for i, (da, db) in enumerate(blocks):
            at = (da * RING + db) * SIDE
            acc[i * SIDE : (i + 1) * SIDE, :] = total_ref[at : at + SIDE, :]
        multiply_tiles(piece_refs, ints_ref, acc, *scratch, block_of, size)
        for ref, (start, many, dtype) in zip(out_refs, outs):
            ref[...] = acc[start * SIDE : (start + many) * SIDE, :].astype(dtype)

    return pl.pallas_call(
        kernel,
        in_specs=[VMEM] * (2 + n),
        out_specs=[VMEM] * len(outs),
        out_shape=[jax.ShapeDtypeStruct((many * SIDE, width), dtype) for _, many, dtype in outs],
        scratch_shapes=[pltpu.VMEM(((size + 1) * SIDE, width), F32)] + list_scratch(n),
        compiler_params=params(20),
        cost_estimate=pl.CostEstimate(flops=flops, bytes_accessed=2**22, transcendentals=0),
        name="finish",
    )(kept(total), kept(ints), *pieces)


def to_owner(meta, tiles):
    parts = sort_tiles(meta, tiles)
    parts = [parts[0]] + [send_first(parts[d], d) for d in range(1, RING)]
    parts = turn(parts)
    parts = [parts[0]] + [send_second(parts[d], d) for d in range(1, RING)]
    return jnp.concatenate(parts, axis=0)


def per_device(amp_tiles, owner_col, local_pair, occ_pair, integrals):
    meta = jnp.concatenate([owner_col[:, 0], local_pair, occ_pair])
    far_tiles, far_meta = send_y(amp_tiles, 2), send_y(meta, 2)

    own = to_owner(meta, amp_tiles)
    up, down = send_y(own, 1), send_y(own, -1)
    far = to_owner(far_meta, far_tiles)
    total = accumulate(None, integrals, [own, send_core(own)], 2**32)
    total = accumulate(total, integrals, [far, send_core(far)], 2**32)
    late = [up, down, send_core(up), send_core(down)]

    (far_a,) = finish(
        total, integrals, late, [(2, 1), (2, 2), (2, 3)], lambda da, db: ((da == 2) & (db > 0), db - 1), [(0, 3, BF16)], 2**31
    )
    got = [send_first(far_a, 2)]
    sides = finish(
        total,
        integrals,
        late,
        [(1, 1), (1, 2), (1, 3), (3, 1), (3, 2), (3, 3)],
        lambda da, db: (((da == 1) | (da == 3)) & (db > 0), jnp.where(da == 3, 2, -1) + db),
        [(0, 3, BF16), (3, 3, BF16)],
        2**31,
    )
    got += [send_first(sides[0], 1), send_first(sides[1], -1)]
    lasts = finish(
        total,
        integrals,
        late,
        [(1, 0), (2, 0), (3, 0)],
        lambda da, db: ((da > 0) & (db == 0), da - 1),
        [(i, 1, BF16) for i in range(3)],
        2**31,
    )
    got_last = [send_first(lasts[1], 2), send_first(lasts[0], 1), send_first(lasts[2], -1)]
    own_last, own_rest = finish(
        total,
        integrals,
        late,
        [(0, 0), (0, 1), (0, 2), (0, 3)],
        lambda da, db: (da == 0, db),
        [(0, 1, F32), (1, 3, F32)],
        2**31,
    )
    rest = own_rest + got[0].astype(F32) + got[1].astype(F32) + got[2].astype(F32)
    rest = rest.astype(BF16).reshape(3, SIDE, -1)
    ladder = own_last
    for g in got_last:
        ladder = ladder + g.astype(F32)
    for d in (2, 1, 3):
        ladder = ladder + send_second(rest[d - 1], d).astype(F32)
    return ladder.astype(BF16)


def solution(mesh):
    return jax.shard_map(
        per_device,
        mesh=mesh,
        in_specs=(
            P(("row", "col"), None, None),
            P(("row", "col"), None),
            P(("row", "col")),
            P(("row", "col")),
            P("col", "row"),
        ),
        out_specs=P("col", "row"),
        check_vma=False,
    )
```

time: 320 us -> 129 us (0.40)
  other arithmetic: 78.6 us -> 2.26 us
  waiting for transfers between devices: 104 us -> 34.7 us
  local copies, waits for them, and re-layouts: 60.2 us -> 3.69 us
  starting transfers between devices: 3.68 us -> 55.3 us
  blocking collectives: 35.3 us -> 0 us
  Pallas kernels: 0 us -> 31.5 us
  matrix products: 22.6 us -> 0 us
  between operations: 14.1 us -> 0.24 us
    reduce_scatter x1 -> x0, waiting for transfers between devices: 73.8 us -> none  [per_device(): lax.psum_scatter(jnp.dot(matrix, integrals, preferred_element_type=jnp.fl...]
    ppermute x0 -> x29, starting transfers between devices: none -> 55.3 us  [the longest x9 23.2 us: send_second(): return lax.ppermute(v, ('row', 'col'), plane_perm(step, True))]
    scatter-add x1 -> x0, other arithmetic: 52.2 us -> none  [per_device(): placed = jnp.zeros((positions, side, side), jnp.float32).at[all_codes].ad...]
    transpose x1 -> x0, local copies, waits for them, and re-layouts: 43.2 us -> none  [per_device(): matrix.transpose(0, 2, 1, 3).reshape(occ_total * side, CD_DEV * side)]
    ppermute x0 -> x29, waiting for transfers between devices: none -> 34.7 us  [the longest x4 13.1 us: send_y(): return lax.ppermute(v, 'row', row_perm(step))]
    pallas_call x0 -> x10, Pallas kernels: none -> 31.5 us  [the longest x4 19.9 us: finish(): pl.pallas_call(kernel, in_specs=[VMEM] * (2 + n), out_specs=[VMEM] * len(...]
    all_gather x1 -> x0, waiting for transfers between devices: 25.4 us -> none  [per_device(): lax.all_gather(got_tiles, 'row', axis=0, tiled=True)]
    all_to_all x1 -> x0, blocking collectives: 24.2 us -> none  [per_device(): lax.all_to_all(send_tiles, 'col', split_axis=0, concat_axis=0, tiled=True)]
  transfers between devices with their start and end apart: 3 -> 29, of which waited for: 3 -> 9; matrix products, arithmetic and copies ran while one was open for 1% -> 1% of each run, Pallas kernels for 0% -> 20%
where the time goes in v1:
time: 129 us; the launch traced here: 128 us
  starting transfers between devices  55.3 us (43%)
  waiting for transfers between devices  34.7 us (27%)
  Pallas kernels  31.5 us (24%)
  local copies, waits for them, and re-layouts  3.69 us (3%)
  other arithmetic  2.26 us (2%)
    ppermute x9, starting transfers between devices, send_second(): return lax.ppermute(v, ('row', 'col'), plane_perm(step, True))  23.2 us
    pallas_call x4, Pallas kernels, finish(): pl.pallas_call(kernel, in_specs=[VMEM] * (2 + n), out_specs=[VMEM] * len(...  19.9 us
    ppermute x12, starting transfers between devices, send_first(): return lax.ppermute(v, ('row', 'col'), plane_perm(step, False))  18.5 us
    ppermute x4, waiting for transfers between devices, send_y(): return lax.ppermute(v, 'row', row_perm(step))  13.1 us
    ppermute x12, waiting for transfers between devices, send_first(): return lax.ppermute(v, ('row', 'col'), plane_perm(step, False))  11.9 us
    ppermute x9, waiting for transfers between devices, send_second(): return lax.ppermute(v, ('row', 'col'), plane_perm(step, True))  9.77 us
    pallas_call x2, Pallas kernels, accumulate(): pl.pallas_call(kernel, in_specs=[VMEM] * (len(old) + 1 + n), out_specs=VM...  8.9 us
    ppermute x4, starting transfers between devices, send_y(): return lax.ppermute(v, 'row', row_perm(step))  8.22 us
  transfers between devices with their start and end apart: 29, of which 9 were waited for; matrix products, arithmetic and copies ran while one was open for 1% of the time, Pallas kernels for 20%

profile of v1, /device:TPU:1, one launch (start us, length us, event | category | flops | bytes accessed | tf_op | source)
XLA Modules:
  0.0 127.8 jit_solution(1923412699488524018)
XLA Ops:
  2.3 2.5 %collective-permute-start = (bf16[1040,128]{1,0:T(8,128)(2,1)S(1)}, bf16[1040,128]{1,0:T(8,128)(2,1)S(1)}, u32[]{:S(2)}, u32[]{:S(2)}) collective-permute-start(bf16[1040,128]{1,0:T(8,128)(2,1)S(1)} %get-tuple-element.29), channel_id=1, source_target_pairs={{0,4},{1,5},{2,6},{3,7},{4,8},{5,9},{6,10},{7,11},{8,12},{9,13},{1... | collective-permute-start | bytes 798728 | tf_op jit(solution)/shard_map/ppermute | solution.py:43
  4.8 3.3 %collective-permute-start.1 = (bf16[1040,128]{1,0:T(8,128)(2,1)S(1)}, bf16[1040,128]{1,0:T(8,128)(2,1)S(1)}, u32[]{:S(2)}, u32[]{:S(2)}) collective-permute-start(bf16[1040,128]{1,0:T(8,128)(2,1)S(1)} %get-tuple-element.30), channel_id=1, source_target_pairs={{0,8},{1,9},{2,10},{3,11},{4,12},{5,13},{6,14},{7,15},{8,0},{9,1},... | collective-permute-start | bytes 798728 | tf_op jit(solution)/shard_map/ppermute | solution.py:43
  8.9 2.9 %collective-permute-start.8 = (bf16[16,128,128]{2,1,0:T(8,128)(2,1)}, bf16[16,128,128]{2,1,0:T(8,128)(2,1)S(1)}, u32[]{:S(2)}, u32[]{:S(2)}) collective-permute-start(bf16[16,128,128]{2,1,0:T(8,128)(2,1)} %tiles.1), channel_id=1, source_target_pairs={{0,64},{16,80},{32,96},{48,112},{64,0},{80,16},{96,32},{112,48},{1... | collective-permute-start | bytes 1572872 | tf_op jit(solution)/shard_map/ppermute | solution.py:51
  11.8 3.3 %collective-permute-done.1.refs_2_ = bf16[1040,128]{1,0:T(8,128)(2,1)S(1)} collective-permute-done((bf16[1040,128]{1,0:T(8,128)(2,1)S(1)}, bf16[1040,128]{1,0:T(8,128)(2,1)S(1)}, u32[]{:S(2)}, u32[]{:S(2)}) %collective-permute-start.1) | collective-permute-done | bytes 266272 | tf_op jit(solution)/shard_map/ppermute | solution.py:43
  16.5 2.6 %collective-permute-start.7 = (s32[48]{0:T(128)S(1)}, s32[48]{0:T(128)S(1)}, u32[]{:S(2)}, u32[]{:S(2)}) collective-permute-start(s32[48]{0:T(128)S(1)} %pad_add_fusion.meta), channel_id=1, source_target_pairs={{0,64},{16,80},{32,96},{48,112},{64,0},{80,16},{96,32},{112,48},{1... | collective-permute-start | bytes 584 | tf_op jit(solution)/shard_map/ppermute | solution.py:51
  19.1 2.5 %collective-permute-start.4 = (bf16[1040,128]{1,0:T(8,128)(2,1)S(1)}, bf16[1040,128]{1,0:T(8,128)(2,1)S(1)}, u32[]{:S(2)}, u32[]{:S(2)}) collective-permute-start(bf16[1040,128]{1,0:T(8,128)(2,1)S(1)} %get-tuple-element.34), channel_id=1, source_target_pairs={{0,2},{1,3},{2,0},{3,1},{4,6},{5,7},{6,4},{7,5},{8,10},{9,11},{10,... | collective-permute-start | bytes 798728 | tf_op jit(solution)/shard_map/ppermute | solution.py:47
  27.7 3.9 %collective-permute-done.10.refs_2_ = bf16[1040,128]{1,0:T(8,128)(2,1)S(1)} collective-permute-done((bf16[1040,128]{1,0:T(8,128)(2,1)S(1)}, bf16[1040,128]{1,0:T(8,128)(2,1)S(1)}, u32[]{:S(2)}, u32[]{:S(2)}) %collective-permute-start.10) | collective-permute-done | bytes 266272 | tf_op jit(solution)/shard_map/ppermute | solution.py:43
  31.6 4.7 %collective-permute-done.11.refs_3_ = bf16[1040,128]{1,0:T(8,128)(2,1)S(1)} collective-permute-done((bf16[1040,128]{1,0:T(8,128)(2,1)S(1)}, bf16[1040,128]{1,0:T(8,128)(2,1)S(1)}, u32[]{:S(2)}, u32[]{:S(2)}) %collective-permute-start.11) | collective-permute-done | bytes 266272 | tf_op jit(solution)/shard_map/ppermute | solution.py:43
  40.5 2.1 %collective-permute-start.17 = (bf16[4160,128]{1,0:T(8,128)(2,1)S(1)}, bf16[4160,128]{1,0:T(8,128)(2,1)S(1)}, u32[]{:S(2)}, u32[]{:S(2)}) collective-permute-start(bf16[4160,128]{1,0:T(8,128)(2,1)S(1)} %constant_dynamic-update-slice_fusion.refs_1_), channel_id=1, source_target_pairs={{0,96},{16,112},{32,0},{48,16},{64,32},{80,48},{96,64},{112,80},{1... | collective-permute-start | bytes 3194888 | tf_op jit(solution)/shard_map/ppermute | solution.py:51
  45.3 4.3 %collective-permute-done.13 = bf16[1040,128]{1,0:T(8,128)(2,1)S(1)} collective-permute-done((bf16[1040,128]{1,0:T(8,128)(2,1)S(1)}, bf16[1040,128]{1,0:T(8,128)(2,1)S(1)}, u32[]{:S(2)}, u32[]{:S(2)}) %collective-permute-start.13) | collective-permute-done | bytes 266272 | tf_op jit(solution)/shard_map/ppermute | solution.py:47
  51.0 2.7 %collective-permute-start.15 = (bf16[4160,128]{1,0:T(8,128)(2,1)S(1)}, bf16[4160,128]{1,0:T(8,128)(2,1)S(1)}, u32[]{:S(2)}, u32[]{:S(2)}) collective-permute-start(bf16[4160,128]{1,0:T(8,128)(2,1)S(1)} %constant_dynamic-update-slice_fusion.4.refs_2_), channel_id=1, source_target_pairs={{0,16},{16,0},{32,48},{48,32},{64,80},{80,64},{96,112},{112,96},{1... | collective-permute-start | bytes 3194888 | tf_op jit(solution)/shard_map/ppermute | solution.py:55
  53.7 12.5 %collective-permute-done.16.refs_2_ = bf16[4160,128]{1,0:T(8,128)(2,1)S(1)} collective-permute-done((bf16[4160,128]{1,0:T(8,128)(2,1)S(1)}, bf16[4160,128]{1,0:T(8,128)(2,1)S(1)}, u32[]{:S(2)}, u32[]{:S(2)}) %collective-permute-start.16) | collective-permute-done | bytes 1064992 | tf_op jit(solution)/shard_map/ppermute | solution.py:51
  67.1 3.4 %copy-done = bf16[4096,1024]{1,0:T(8,128)(2,1)S(1)} copy-done((bf16[4096,1024]{1,0:T(8,128)(2,1)S(1)}, bf16[4096,1024]{1,0:T(8,128)(2,1)}, u32[]{:S(2)}) %copy-start) | copy-done | bytes 8388632
  70.5 4.6 %accumulate.2.refs_0_ = f32[2176,1024]{1,0:T(8,128)S(1)} custom-call(bf16[4096,1024]{1,0:T(8,128)(2,1)S(1)} %copy-done, bf16[4160,128]{1,0:T(8,128)(2,1)S(1)} %constant_dynamic-update-slice_fusion.refs_1_, bf16[4160,128]{1,0:T(8,128)(2,1)S(1)} %collective-permute-done.6.refs_2_), custom_call_target="tpu_custom_call" | custom-call | flops 4294967296 | bytes 4194304 | tf_op jit(solution)/shard_map/accumulate/pallas_call | solution.py:221
  75.1 4.3 %accumulate.3.refs_0_ = f32[2176,1024]{1,0:T(8,128)S(1)} custom-call(f32[2176,1024]{1,0:T(8,128)S(1)} %accumulate.2.refs_0_, bf16[4096,1024]{1,0:T(8,128)(2,1)S(1)} %copy-done, bf16[4160,128]{1,0:T(8,128)(2,1)S(1)} %constant_dynamic-update-slice_fusion.4.refs_2_, bf16[4160,128]{1,0:T(8,128)(2,1)S(1)} %collective-permute-done.15.refs_3_), custom_call_target="tpu_custom_call", output_to_operand_aliasing={{}: (0, {})} | custom-call | flops 4294967296 | bytes 4194304 | tf_op jit(solution)/shard_map/accumulate/pallas_call | solution.py:221
  79.5 4.3 %finish.6 = bf16[384,1024]{1,0:T(8,128)(2,1)S(1)} custom-call(f32[2176,1024]{1,0:T(8,128)S(1)} %accumulate.3.refs_0_, bf16[4096,1024]{1,0:T(8,128)(2,1)S(1)} %bitcast.2, bf16[4160,128]{1,0:T(8,128)(2,1)S(1)} %collective-permute-done.16.refs_2_, bf16[4160,128]{1,0:T(8,128)(2,1)S(1)} %collective-permute-done.17.refs_3_, ...), custom_call_target="tpu_custom_call" | custom-call | flops 2147483648 | bytes 4194304 | tf_op jit(solution)/shard_map/finish/pallas_call | solution.py:250
  85.3 5.2 %finish.7 = (bf16[384,1024]{1,0:T(8,128)(2,1)S(1)}, bf16[384,1024]{1,0:T(8,128)(2,1)S(1)}) custom-call(f32[2176,1024]{1,0:T(8,128)S(1)} %accumulate.3.refs_0_, bf16[4096,1024]{1,0:T(8,128)(2,1)S(1)} %bitcast.2, bf16[4160,128]{1,0:T(8,128)(2,1)S(1)} %collective-permute-done.16.refs_2_, bf16[4160,128]{1,0:T(8,128)(2,1)S(1)} %collective-permute-done.17.refs_3_, ...), custom_call_target="tpu_custom_call" | custom-call | flops 2147483648 | bytes 4194304 | tf_op jit(solution)/shard_map/finish/pallas_call | solution.py:250
  90.6 2.5 %collective-permute-start.24 = (bf16[384,1024]{1,0:T(8,128)(2,1)S(1)}, bf16[384,1024]{1,0:T(8,128)(2,1)S(1)}, u32[]{:S(2)}, u32[]{:S(2)}) collective-permute-start(bf16[384,1024]{1,0:T(8,128)(2,1)S(1)} %get-tuple-element.49), channel_id=1, source_target_pairs={{0,4},{1,5},{2,6},{3,7},{4,8},{5,9},{6,10},{7,11},{8,12},{9,13},{1... | collective-permute-start | bytes 2359304 | tf_op jit(solution)/shard_map/ppermute | solution.py:43
  93.3 5.0 %finish.5 = (bf16[128,1024]{1,0:T(8,128)(2,1)S(1)}, bf16[128,1024]{1,0:T(8,128)(2,1)S(1)}, bf16[128,1024]{1,0:T(8,128)(2,1)S(1)}) custom-call(f32[2176,1024]{1,0:T(8,128)S(1)} %accumulate.3.refs_0_, bf16[4096,1024]{1,0:T(8,128)(2,1)S(1)} %bitcast.2, bf16[4160,128]{1,0:T(8,128)(2,1)S(1)} %collective-permute-done.16.refs_2_, ...), custom_call_target="tpu_custom_call" | custom-call | flops 2147483648 | bytes 4194304 | tf_op jit(solution)/shard_map/finish/pallas_call | solution.py:250
  100.0 5.3 %finish.4 = (f32[128,1024]{1,0:T(8,128)S(1)}, f32[384,1024]{1,0:T(8,128)S(1)}) custom-call(f32[2176,1024]{1,0:T(8,128)S(1)} %accumulate.3.refs_0_, bf16[4096,1024]{1,0:T(8,128)(2,1)S(1)} %bitcast.2, bf16[4160,128]{1,0:T(8,128)(2,1)S(1)} %collective-permute-done.16.refs_2_, bf16[4160,128]{1,0:T(8,128)(2,1)S(1)} %collective-permute-done.17.refs_3_, ...), custom_call_target="tpu_custom_call" | custom-call | flops 2147483648 | bytes 4194304 | tf_op jit(solution)/shard_map/finish/pallas_call | solution.py:250
  105.4 2.7 %collective-permute-start.22 = (bf16[128,1024]{1,0:T(8,128)(2,1)S(1)}, bf16[128,1024]{1,0:T(8,128)(2,1)S(1)}, u32[]{:S(2)}, u32[]{:S(2)}) collective-permute-start(bf16[128,1024]{1,0:T(8,128)(2,1)S(1)} %get-tuple-element.47), channel_id=1, source_target_pairs={{0,12},{1,13},{2,14},{3,15},{4,0},{5,1},{6,2},{7,3},{8,4},{9,5},{1... | collective-permute-start | bytes 786440 | tf_op jit(solution)/shard_map/ppermute | solution.py:43
  108.8 11.5 %collective-permute-start.27 = (bf16[128,1024]{1,0:T(8,128)(2,1)S(1)}, bf16[128,1024]{1,0:T(8,128)(2,1)S(1)}, u32[]{:S(2)}, u32[]{:S(2)}) collective-permute-start(bf16[128,1024]{1,0:T(8,128)(2,1)S(1)} %get-tuple-element.53), channel_id=1, source_target_pairs={{0,1},{1,2},{2,3},{3,0},{4,5},{5,6},{6,7},{7,4},{8,9},{9,10},{10,1... | collective-permute-start | bytes 786440 | tf_op jit(solution)/shard_map/ppermute | solution.py:47
  120.3 2.3 %collective-permute-start.28 = (bf16[128,1024]{1,0:T(8,128)(2,1)S(1)}, bf16[128,1024]{1,0:T(8,128)(2,1)S(1)}, u32[]{:S(2)}, u32[]{:S(2)}) collective-permute-start(bf16[128,1024]{1,0:T(8,128)(2,1)S(1)} %get-tuple-element.52), channel_id=1, source_target_pairs={{0,3},{1,0},{2,1},{3,2},{4,7},{5,4},{6,5},{7,6},{8,11},{9,8},{10,9... | collective-permute-start | bytes 786440 | tf_op jit(solution)/shard_map/ppermute | solution.py:47
  122.6 3.7 %collective-permute-done.27 = bf16[128,1024]{1,0:T(8,128)(2,1)S(1)} collective-permute-done((bf16[128,1024]{1,0:T(8,128)(2,1)S(1)}, bf16[128,1024]{1,0:T(8,128)(2,1)S(1)}, u32[]{:S(2)}, u32[]{:S(2)}) %collective-permute-start.27) | collective-permute-done | bytes 262176 | tf_op jit(solution)/shard_map/ppermute | solution.py:47
  (63 shorter events, 25.3 us)
Async XLA Ops:
  2.3 9.5 %collective-permute-start = (bf16[1040,128]{1,0:T(8,128)(2,1)S(1)}, bf16[1040,128]{1,0:T(8,128)(2,1)S(1)}, u32[]{:S(2)}, u32[]{:S(2)}) collective-permute-start(bf16[1040,128]{1,0:T(8,128)(2,1)S(1)} %get-tuple-element.29), channel_id=1, source_target_pairs={{0,4},{1,5},{2,6},{3,7},{4,8},{5,9},{6,10},{7,11},{8,12},{9,13},{1... | collective-permute-start | bytes 798728 | tf_op jit(solution)/shard_map/ppermute | solution.py:43
  4.8 10.3 %collective-permute-start.1 = (bf16[1040,128]{1,0:T(8,128)(2,1)S(1)}, bf16[1040,128]{1,0:T(8,128)(2,1)S(1)}, u32[]{:S(2)}, u32[]{:S(2)}) collective-permute-start(bf16[1040,128]{1,0:T(8,128)(2,1)S(1)} %get-tuple-element.30), channel_id=1, source_target_pairs={{0,8},{1,9},{2,10},{3,11},{4,12},{5,13},{6,14},{7,15},{8,0},{9,1},... | collective-permute-start | bytes 798728 | tf_op jit(solution)/shard_map/ppermute | solution.py:43
  8.9 14.5 %collective-permute-start.8 = (bf16[16,128,128]{2,1,0:T(8,128)(2,1)}, bf16[16,128,128]{2,1,0:T(8,128)(2,1)S(1)}, u32[]{:S(2)}, u32[]{:S(2)}) collective-permute-start(bf16[16,128,128]{2,1,0:T(8,128)(2,1)} %tiles.1), channel_id=1, source_target_pairs={{0,64},{16,80},{32,96},{48,112},{64,0},{80,16},{96,32},{112,48},{1... | collective-permute-start | bytes 1572872 | tf_op jit(solution)/shard_map/ppermute | solution.py:51
  15.2 12.4 %collective-permute-start.3 = (bf16[1040,128]{1,0:T(8,128)(2,1)S(1)}, bf16[1040,128]{1,0:T(8,128)(2,1)S(1)}, u32[]{:S(2)}, u32[]{:S(2)}) collective-permute-start(bf16[1040,128]{1,0:T(8,128)(2,1)S(1)} %get-tuple-element.33), channel_id=1, source_target_pairs={{0,1},{1,2},{2,3},{3,0},{4,5},{5,6},{6,7},{7,4},{8,9},{9,10},{10,1... | collective-permute-start | bytes 798728 | tf_op jit(solution)/shard_map/ppermute | solution.py:47
  19.1 8.6 %collective-permute-start.4 = (bf16[1040,128]{1,0:T(8,128)(2,1)S(1)}, bf16[1040,128]{1,0:T(8,128)(2,1)S(1)}, u32[]{:S(2)}, u32[]{:S(2)}) collective-permute-start(bf16[1040,128]{1,0:T(8,128)(2,1)S(1)} %get-tuple-element.34), channel_id=1, source_target_pairs={{0,2},{1,3},{2,0},{3,1},{4,6},{5,7},{6,4},{7,5},{8,10},{9,11},{10,... | collective-permute-start | bytes 798728 | tf_op jit(solution)/shard_map/ppermute | solution.py:47
  21.6 16.5 %collective-permute-start.5 = (bf16[1040,128]{1,0:T(8,128)(2,1)S(1)}, bf16[1040,128]{1,0:T(8,128)(2,1)S(1)}, u32[]{:S(2)}, u32[]{:S(2)}) collective-permute-start(bf16[1040,128]{1,0:T(8,128)(2,1)S(1)} %get-tuple-element.35), channel_id=1, source_target_pairs={{0,3},{1,0},{2,1},{3,2},{4,7},{5,4},{6,5},{7,6},{8,11},{9,8},{10,9... | collective-permute-start | bytes 798728 | tf_op jit(solution)/shard_map/ppermute | solution.py:47
  24.4 7.1 %collective-permute-start.10 = (bf16[1040,128]{1,0:T(8,128)(2,1)S(1)}, bf16[1040,128]{1,0:T(8,128)(2,1)S(1)}, u32[]{:S(2)}, u32[]{:S(2)}) collective-permute-start(bf16[1040,128]{1,0:T(8,128)(2,1)S(1)} %get-tuple-element.38), channel_id=1, source_target_pairs={{0,8},{1,9},{2,10},{3,11},{4,12},{5,13},{6,14},{7,15},{8,0},{9,1},... | collective-permute-start | bytes 798728 | tf_op jit(solution)/shard_map/ppermute | solution.py:43
  26.1 10.1 %collective-permute-start.11 = (bf16[1040,128]{1,0:T(8,128)(2,1)S(1)}, bf16[1040,128]{1,0:T(8,128)(2,1)S(1)}, u32[]{:S(2)}, u32[]{:S(2)}) collective-permute-start(bf16[1040,128]{1,0:T(8,128)(2,1)S(1)} %get-tuple-element.39), channel_id=1, source_target_pairs={{0,12},{1,13},{2,14},{3,15},{4,0},{5,1},{6,2},{7,3},{8,4},{9,5},{1... | collective-permute-start | bytes 798728 | tf_op jit(solution)/shard_map/ppermute | solution.py:43
  27.5 8.7 %collective-permute-start.9 = (bf16[1040,128]{1,0:T(8,128)(2,1)S(1)}, bf16[1040,128]{1,0:T(8,128)(2,1)S(1)}, u32[]{:S(2)}, u32[]{:S(2)}) collective-permute-start(bf16[1040,128]{1,0:T(8,128)(2,1)S(1)} %get-tuple-element.37), channel_id=1, source_target_pairs={{0,4},{1,5},{2,6},{3,7},{4,8},{5,9},{6,10},{7,11},{8,12},{9,13},{1... | collective-permute-start | bytes 798728 | tf_op jit(solution)/shard_map/ppermute | solution.py:43
  36.3 7.5 %collective-permute-start.12 = (bf16[1040,128]{1,0:T(8,128)(2,1)S(1)}, bf16[1040,128]{1,0:T(8,128)(2,1)S(1)}, u32[]{:S(2)}, u32[]{:S(2)}) collective-permute-start(bf16[1040,128]{1,0:T(8,128)(2,1)S(1)} %get-tuple-element.41), channel_id=1, source_target_pairs={{0,1},{1,2},{2,3},{3,0},{4,5},{5,6},{6,7},{7,4},{8,9},{9,10},{10,1... | collective-permute-start | bytes 798728 | tf_op jit(solution)/shard_map/ppermute | solution.py:47
  38.1 29.0 %collective-permute-start.6 = (bf16[4160,128]{1,0:T(8,128)(2,1)S(1)}, bf16[4160,128]{1,0:T(8,128)(2,1)S(1)}, u32[]{:S(2)}, u32[]{:S(2)}) collective-permute-start(bf16[4160,128]{1,0:T(8,128)(2,1)S(1)} %constant_dynamic-update-slice_fusion.refs_1_), channel_id=1, source_target_pairs={{0,16},{16,0},{32,48},{48,32},{64,80},{80,64},{96,112},{112,96},{1... | collective-permute-start | bytes 3194888 | tf_op jit(solution)/shard_map/ppermute | solution.py:55
  39.9 26.3 %collective-permute-start.16 = (bf16[4160,128]{1,0:T(8,128)(2,1)S(1)}, bf16[4160,128]{1,0:T(8,128)(2,1)S(1)}, u32[]{:S(2)}, u32[]{:S(2)}) collective-permute-start(bf16[4160,128]{1,0:T(8,128)(2,1)S(1)} %constant_dynamic-update-slice_fusion.refs_1_), channel_id=1, source_target_pairs={{0,32},{16,48},{32,64},{48,80},{64,96},{80,112},{96,0},{112,16},{1... | collective-permute-start | bytes 3194888 | tf_op jit(solution)/shard_map/ppermute | solution.py:51
  40.5 26.6 %collective-permute-start.17 = (bf16[4160,128]{1,0:T(8,128)(2,1)S(1)}, bf16[4160,128]{1,0:T(8,128)(2,1)S(1)}, u32[]{:S(2)}, u32[]{:S(2)}) collective-permute-start(bf16[4160,128]{1,0:T(8,128)(2,1)S(1)} %constant_dynamic-update-slice_fusion.refs_1_), channel_id=1, source_target_pairs={{0,96},{16,112},{32,0},{48,16},{64,32},{80,48},{96,64},{112,80},{1... | collective-permute-start | bytes 3194888 | tf_op jit(solution)/shard_map/ppermute | solution.py:51
  51.0 24.1 %collective-permute-start.15 = (bf16[4160,128]{1,0:T(8,128)(2,1)S(1)}, bf16[4160,128]{1,0:T(8,128)(2,1)S(1)}, u32[]{:S(2)}, u32[]{:S(2)}) collective-permute-start(bf16[4160,128]{1,0:T(8,128)(2,1)S(1)} %constant_dynamic-update-slice_fusion.4.refs_2_), channel_id=1, source_target_pairs={{0,16},{16,0},{32,48},{48,32},{64,80},{80,64},{96,112},{112,96},{1... | collective-permute-start | bytes 3194888 | tf_op jit(solution)/shard_map/ppermute | solution.py:55
  66.2 13.2 %collective-permute-start.18 = (bf16[4160,128]{1,0:T(8,128)(2,1)S(1)}, bf16[4160,128]{1,0:T(8,128)(2,1)S(1)}, u32[]{:S(2)}, u32[]{:S(2)}) collective-permute-start(bf16[4160,128]{1,0:T(8,128)(2,1)S(1)} %collective-permute-done.16.refs_2_), channel_id=1, source_target_pairs={{0,16},{16,0},{32,48},{48,32},{64,80},{80,64},{96,112},{112,96},{1... | collective-permute-start | bytes 3194888 | tf_op jit(solution)/shard_map/ppermute | solution.py:55
  67.1 12.3 %collective-permute-start.19 = (bf16[4160,128]{1,0:T(8,128)(2,1)S(1)}, bf16[4160,128]{1,0:T(8,128)(2,1)S(1)}, u32[]{:S(2)}, u32[]{:S(2)}) collective-permute-start(bf16[4160,128]{1,0:T(8,128)(2,1)S(1)} %collective-permute-done.17.refs_3_), channel_id=1, source_target_pairs={{0,16},{16,0},{32,48},{48,32},{64,80},{80,64},{96,112},{112,96},{1... | collective-permute-start | bytes 3194888 | tf_op jit(solution)/shard_map/ppermute | solution.py:55
  83.8 21.6 %collective-permute-start.23 = (bf16[384,1024]{1,0:T(8,128)(2,1)S(1)}, bf16[384,1024]{1,0:T(8,128)(2,1)S(1)}, u32[]{:S(2)}, u32[]{:S(2)}) collective-permute-start(bf16[384,1024]{1,0:T(8,128)(2,1)S(1)} %finish.6), channel_id=1, source_target_pairs={{0,8},{1,9},{2,10},{3,11},{4,12},{5,13},{6,14},{7,15},{8,0},{9,1},... | collective-permute-start | bytes 2359304 | tf_op jit(solution)/shard_map/ppermute | solution.py:43
  90.6 17.6 %collective-permute-start.24 = (bf16[384,1024]{1,0:T(8,128)(2,1)S(1)}, bf16[384,1024]{1,0:T(8,128)(2,1)S(1)}, u32[]{:S(2)}, u32[]{:S(2)}) collective-permute-start(bf16[384,1024]{1,0:T(8,128)(2,1)S(1)} %get-tuple-element.49), channel_id=1, source_target_pairs={{0,4},{1,5},{2,6},{3,7},{4,8},{5,9},{6,10},{7,11},{8,12},{9,13},{1... | collective-permute-start | bytes 2359304 | tf_op jit(solution)/shard_map/ppermute | solution.py:43
  93.0 15.1 %collective-permute-start.25 = (bf16[384,1024]{1,0:T(8,128)(2,1)S(1)}, bf16[384,1024]{1,0:T(8,128)(2,1)S(1)}, u32[]{:S(2)}, u32[]{:S(2)}) collective-permute-start(bf16[384,1024]{1,0:T(8,128)(2,1)S(1)} %get-tuple-element.50), channel_id=1, source_target_pairs={{0,12},{1,13},{2,14},{3,15},{4,0},{5,1},{6,2},{7,3},{8,4},{9,5},{1... | collective-permute-start | bytes 2359304 | tf_op jit(solution)/shard_map/ppermute | solution.py:43
  98.3 22.0 %collective-permute-start.20 = (bf16[128,1024]{1,0:T(8,128)(2,1)S(1)}, bf16[128,1024]{1,0:T(8,128)(2,1)S(1)}, u32[]{:S(2)}, u32[]{:S(2)}) collective-permute-start(bf16[128,1024]{1,0:T(8,128)(2,1)S(1)} %get-tuple-element.45), channel_id=1, source_target_pairs={{0,8},{1,9},{2,10},{3,11},{4,12},{5,13},{6,14},{7,15},{8,0},{9,1},... | collective-permute-start | bytes 786440 | tf_op jit(solution)/shard_map/ppermute | solution.py:43
  100.0 22.6 %collective-permute-start.21 = (bf16[128,1024]{1,0:T(8,128)(2,1)S(1)}, bf16[128,1024]{1,0:T(8,128)(2,1)S(1)}, u32[]{:S(2)}, u32[]{:S(2)}) collective-permute-start(bf16[128,1024]{1,0:T(8,128)(2,1)S(1)} %get-tuple-element.46), channel_id=1, source_target_pairs={{0,4},{1,5},{2,6},{3,7},{4,8},{5,9},{6,10},{7,11},{8,12},{9,13},{1... | collective-permute-start | bytes 786440 | tf_op jit(solution)/shard_map/ppermute | solution.py:43
  105.4 17.3 %collective-permute-start.22 = (bf16[128,1024]{1,0:T(8,128)(2,1)S(1)}, bf16[128,1024]{1,0:T(8,128)(2,1)S(1)}, u32[]{:S(2)}, u32[]{:S(2)}) collective-permute-start(bf16[128,1024]{1,0:T(8,128)(2,1)S(1)} %get-tuple-element.47), channel_id=1, source_target_pairs={{0,12},{1,13},{2,14},{3,15},{4,0},{5,1},{6,2},{7,3},{8,4},{9,5},{1... | collective-permute-start | bytes 786440 | tf_op jit(solution)/shard_map/ppermute | solution.py:43
  108.7 13.9 %collective-permute-start.26 = (bf16[128,1024]{1,0:T(8,128)(2,1)S(1)}, bf16[128,1024]{1,0:T(8,128)(2,1)S(1)}, u32[]{:S(2)}, u32[]{:S(2)}) collective-permute-start(bf16[128,1024]{1,0:T(8,128)(2,1)S(1)} %get-tuple-element.51), channel_id=1, source_target_pairs={{0,2},{1,3},{2,0},{3,1},{4,6},{5,7},{6,4},{7,5},{8,10},{9,11},{10,... | collective-permute-start | bytes 786440 | tf_op jit(solution)/shard_map/ppermute | solution.py:47
  108.8 17.6 %collective-permute-start.27 = (bf16[128,1024]{1,0:T(8,128)(2,1)S(1)}, bf16[128,1024]{1,0:T(8,128)(2,1)S(1)}, u32[]{:S(2)}, u32[]{:S(2)}) collective-permute-start(bf16[128,1024]{1,0:T(8,128)(2,1)S(1)} %get-tuple-element.53), channel_id=1, source_target_pairs={{0,1},{1,2},{2,3},{3,0},{4,5},{5,6},{6,7},{7,4},{8,9},{9,10},{10,1... | collective-permute-start | bytes 786440 | tf_op jit(solution)/shard_map/ppermute | solution.py:47
  (8 other events, 51.2 us)

commit v2 on v0

v2 whole, which is shorter than its diff:
```python
import jax
import jax.numpy as jnp
from jax import lax
from jax.experimental import pallas as pl
from jax.experimental.pallas import tpu as pltpu
from jax.sharding import PartitionSpec as P

SIDE = 128
CAP = 2
RING = 4
SLOTS = RING * CAP
HEAD = 16
MSG = SLOTS * SIDE + HEAD
PIECE = RING * MSG
OCC = RING * RING
DUMMY = OCC
UNROLL = 4
INFO = 32

VMEM = pl.BlockSpec(memory_space=pltpu.VMEM)
SMEM = pl.BlockSpec(memory_space=pltpu.SMEM)
ANY = pl.BlockSpec(memory_space=pl.ANY)
HBM = pl.BlockSpec(memory_space=pltpu.HBM)
F32, BF16, I32 = jnp.float32, jnp.bfloat16, jnp.int32


def row_perm(step):
    return [(r, (r + 2 * step) % (2 * RING)) for r in range(2 * RING)]


CORE_PERM = [(r, r ^ 1) for r in range(2 * RING)]


def plane_perm(step, second):
    pairs = []
    for r in range(2 * RING):
        for x in range(RING):
            for z in range(RING):
                along_x = (r % 2 == 0) != second
                nx, nz = ((x + step) % RING, z) if along_x else (x, (z + step) % RING)
                pairs.append((r * OCC + x * RING + z, r * OCC + nx * RING + nz))
    return pairs


def send_first(v, step):
    return lax.ppermute(v, ("row", "col"), plane_perm(step, False))


def send_second(v, step):
    return lax.ppermute(v, ("row", "col"), plane_perm(step, True))


def send_y(v, step):
    return lax.ppermute(v, "row", row_perm(step))


def send_core(v):
    return lax.ppermute(v, "row", CORE_PERM)


def place():
    core = lax.rem(lax.axis_index("row"), 2)
    col = lax.axis_index("col")
    x, z = col // RING, lax.rem(col, RING)
    first = core == 0
    return first, jnp.where(first, x, z), jnp.where(first, z, x)


def relative(index, first, a, b):
    x, z = index >> 2, index & 3
    return (jnp.where(first, x, z) - a) & 3, (jnp.where(first, z, x) - b) & 3


def params(mib):
    return pltpu.CompilerParams(vmem_limit_bytes=mib * 2**20)


def kept(v):
    return pltpu.with_memory_space_constraint(v, pltpu.VMEM)


def in_hbm(v):
    return pltpu.with_memory_space_constraint(v, pltpu.HBM)


def header(lines):
    rows = lax.broadcasted_iota(I32, (HEAD, SIDE), 0)
    head = jnp.zeros((HEAD, SIDE), F32)
    for i, line in enumerate(lines):
        head = jnp.where(rows == i, jnp.broadcast_to(line, (HEAD, SIDE)), head)
    return head.astype(BF16)


def sort_tiles_body(owner_of, loc_at, occ_at, tile_at, count, outs, seen):
    first, a, b = place()
    for o in range(OCC):
        seen[o] = 0
    rows = lax.broadcasted_iota(I32, (8, SIDE), 0)
    lanes = lax.broadcasted_iota(I32, (8, SIDE), 1)
    occ_of = jnp.zeros((8, SIDE), F32)
    loc_of = jnp.zeros((8, SIDE), F32)
    for k in range(count):
        owner = owner_of(k)
        rank = seen[owner]
        seen[owner] = rank + 1
        da, db = relative(owner, first, a, b)
        slot = db * CAP + rank
        here = (rows == da) & (lanes == slot)
        occ_of = jnp.where(here, (occ_at(k) + 1).astype(F32), occ_of)
        loc_of = jnp.where(here, loc_at(k).astype(F32), loc_of)
        at = pl.ds(pl.multiple_of(slot * SIDE, SIDE), SIDE)
        for d in range(RING):

            @pl.when(da == d)
            def _(d=d, k=k, at=at):
                outs[d][at, :] = tile_at(k)

    for d in range(RING):
        outs[d][SLOTS * SIDE :, :] = header([occ_of[d : d + 1], loc_of[d : d + 1]])


def sort_own(owner, loc, occ, tiles):
    count = tiles.shape[0]

    def kernel(owner_hbm, loc_hbm, occ_hbm, tiles_hbm, *refs):
        outs, raw, seen = refs[:RING], refs[RING], refs[RING + 1]
        owner_ref, loc_ref, occ_ref, sems = refs[RING + 2 :]
        pairs = [(owner_hbm, owner_ref), (loc_hbm, loc_ref), (occ_hbm, occ_ref)]
        pairs += [(tiles_hbm.at[k], raw.at[pl.ds(k * SIDE, SIDE), :]) for k in range(count)]
        copies = [pltpu.make_async_copy(src, dst, sems.at[i]) for i, (src, dst) in enumerate(pairs)]
        for copy in copies:
            copy.start()
        for copy in copies:
            copy.wait()
        sort_tiles_body(
            lambda k: owner_ref[k],
            lambda k: loc_ref[k],
            lambda k: occ_ref[k],
            lambda k: raw[k * SIDE : (k + 1) * SIDE, :],
            count,
            outs,
            seen,
        )
        lanes = lax.broadcasted_iota(I32, (8, SIDE), 1)
        rows = []
        for ref in (owner_ref, loc_ref, occ_ref):
            row = jnp.zeros((8, SIDE), F32)
            for k in range(count):
                row = jnp.where(lanes == k, ref[k].astype(F32), row)
            rows.append(row[0:1])
        raw[count * SIDE :, :] = header(rows)

    return pl.pallas_call(
        kernel,
        in_specs=[HBM] * 4,
        out_specs=[VMEM] * (RING + 1),
        out_shape=[pltpu.VMEM((MSG, SIDE), BF16)] * RING + [pltpu.VMEM((count * SIDE + HEAD, SIDE), BF16)],
        scratch_shapes=[pltpu.SMEM((OCC,), I32)]
        + [pltpu.SMEM((count,), I32)] * 3
        + [pltpu.SemaphoreType.DMA((3 + count,))],
        compiler_params=params(8),
        name="sort_own",
    )(*[in_hbm(v) for v in (owner, loc, occ, tiles)])


def sort_far(raw, after):
    count = (raw.shape[0] - HEAD) // SIDE

    def kernel(raw_ref, after_ref, *refs):
        outs, seen, head_v, head_s = refs[:RING], refs[RING], refs[RING + 1], refs[RING + 2]
        head_v[...] = raw_ref[count * SIDE :, :].astype(F32)[0:8].astype(I32)
        pltpu.sync_copy(head_v, head_s)
        sort_tiles_body(
            lambda k: head_s[0, k],
            lambda k: head_s[1, k],
            lambda k: head_s[2, k],
            lambda k: raw_ref[k * SIDE : (k + 1) * SIDE, :],
            count,
            outs,
            seen,
        )

    return pl.pallas_call(
        kernel,
        in_specs=[VMEM, ANY],
        out_specs=[VMEM] * RING,
        out_shape=[pltpu.VMEM((MSG, SIDE), BF16)] * RING,
        scratch_shapes=[pltpu.SMEM((OCC,), I32), pltpu.VMEM((8, SIDE), I32), pltpu.SMEM((8, SIDE), I32)],
        compiler_params=params(8),
        name="sort_far",
    )(kept(raw), after)


def turn_kernel(after, *refs):
    ins, outs = refs[:RING], refs[RING:]
    lanes = lax.broadcasted_iota(I32, (HEAD, SIDE), 1)
    heads = [r[SLOTS * SIDE :, :].astype(F32) for r in ins]
    for db in range(RING):
        head = jnp.zeros((HEAD, SIDE), F32)
        for da in range(RING):
            outs[db][da * CAP * SIDE : (da + 1) * CAP * SIDE, :] = ins[da][db * CAP * SIDE : (db + 1) * CAP * SIDE, :]
            turned = pltpu.roll(heads[da], ((da - db) * CAP) % SIDE, 1)
            head = jnp.where((lanes >= da * CAP) & (lanes < (da + 1) * CAP), turned, head)
        outs[db][SLOTS * SIDE :, :] = head.astype(BF16)


def turn(parts, after):
    return pl.pallas_call(
        turn_kernel,
        in_specs=[ANY] + [VMEM] * RING,
        out_specs=[VMEM] * RING,
        out_shape=[pltpu.VMEM((MSG, SIDE), BF16)] * RING,
        compiler_params=params(8),
        name="turn",
    )(after, *[kept(v) for v in parts])


def order(da, db):
    travels = jnp.where(da == 2, 0, jnp.where(da == 1, 3, 6)) + db - 1
    return jnp.where(da == 0, 12 + db, jnp.where(db == 0, 8 + da, travels))


def group(pieces, info_v, info_s, packed):
    first, a, b = place()
    n = len(pieces) * RING * SLOTS
    lanes = lax.broadcasted_iota(I32, (8, SIDE), 1)
    head = jnp.zeros((8, SIDE), F32)
    for i in range(len(pieces) * RING):
        at = (i % RING) * MSG + SLOTS * SIDE
        one = pieces[i // RING][at : at + HEAD, :].astype(F32)[0:8]
        here = (lanes >= i * SLOTS) & (lanes < (i + 1) * SLOTS)
        head = jnp.where(here, pltpu.roll(one, i * SLOTS, 1) if i else one, head)
    occ = jnp.broadcast_to(head[0:1], (8, SIDE)).astype(I32) - 1
    loc = jnp.broadcast_to(head[1:2], (8, SIDE)).astype(I32)
    da, db = relative(occ, first, a, b)
    block = jnp.where(occ >= 0, order(da, db), DUMMY)
    rows = lax.broadcasted_iota(I32, (SIDE, SIDE), 0)
    cols = lax.broadcasted_iota(I32, (SIDE, SIDE), 1)
    hot = (rows == jnp.broadcast_to(block[0:1], (SIDE, SIDE))) & (rows < OCC)
    hot = jnp.where(hot, 1.0, 0.0)
    count = jnp.broadcast_to(jnp.sum(hot, axis=1, keepdims=True), (SIDE, SIDE)).astype(I32)
    padded = (((count + 1) >> 1) << 1).astype(F32)
    below = jnp.where(cols < rows, 1.0, 0.0).astype(BF16)
    above = jnp.where(rows < cols, 1.0, 0.0).astype(BF16)
    start = jnp.dot(below, padded.astype(BF16), preferred_element_type=F32)
    rank = jnp.dot(hot.astype(BF16), above, preferred_element_type=F32)
    spot = jnp.broadcast_to(jnp.sum(hot * (start + rank), axis=0, keepdims=True), (8, SIDE)).astype(I32)
    spot = jnp.where(occ >= 0, spot, n + OCC)
    rows8 = lax.broadcasted_iota(I32, (8, SIDE), 0)
    info_v[0:8, :] = jnp.where(rows8 == 0, spot, jnp.where(rows8 == 1, loc, block))
    start = start.astype(I32)
    info_v[8:INFO, :] = jnp.where(cols == 0, start, start + count)[0 : INFO - 8, :]
    pltpu.sync_copy(info_v, info_s)
    for i in range(OCC):
        free = pl.multiple_of(info_s[8 + i, 1] * SIDE, SIDE)
        packed[pl.ds(free, SIDE), :] = jnp.zeros((SIDE, SIDE), BF16)
    for i in range(n):
        to = pl.multiple_of(info_s[0, i] * SIDE, SIDE)
        at = (i // SLOTS % RING) * MSG + (i % SLOTS) * SIDE
        packed[pl.ds(to, SIDE), :] = pieces[i // (RING * SLOTS)][at : at + SIDE, :]


def read_lists(n, info_s, loc_s, block_s):
    for i in range(OCC):
        loc_s[info_s[8 + i, 1]] = 0
    for i in range(n):
        to = info_s[0, i]
        loc_s[to] = info_s[1, i]
        block_s[to] = info_s[2, i]


def multiply(blocks, info_s, loc_s, block_s, packed, ints, total):
    begin = info_s[8 + blocks[0], 0] >> 1
    end = info_s[8 + blocks[1], 0] >> 1

    def body(i, carry):
        for u in range(UNROLL):
            pair = begin + i * UNROLL + u
            k = jnp.minimum(pair, end - 1) * 2
            block = jnp.where(pair < end, block_s[k], DUMMY)
            at = pl.multiple_of(block * SIDE, SIDE)
            tiles = [packed[pl.ds(pl.multiple_of((k + j) * SIDE, SIDE), SIDE), :] for j in range(2)]
            rows = [ints[pl.ds(pl.multiple_of(loc_s[k + j] * SIDE, SIDE), SIDE), :] for j in range(2)]
            total[pl.ds(at, SIDE), :] += jnp.dot(
                jnp.concatenate(tiles, axis=1), jnp.concatenate(rows, axis=0), preferred_element_type=F32
            )
        return carry

    lax.fori_loop(0, (end - begin + UNROLL - 1) // UNROLL, body, 0)


def spots(n):
    return n * RING * SLOTS + OCC + 2


def list_scratch(n):
    return [pltpu.SMEM((INFO, SIDE), I32), pltpu.SMEM((spots(n),), I32), pltpu.SMEM((spots(n),), I32)]


def cost(flops):
    return pl.CostEstimate(flops=flops, bytes_accessed=2**12, transcendentals=0)


def accumulate(total, ints, pieces):
    n = len(pieces)
    old = [] if total is None else [total]

    def kernel(*refs):
        refs = refs[len(old) :]
        ints_ref, piece_refs, acc = refs[0], refs[1 : 1 + n], refs[1 + n]
        packed, info_v, info_s, loc_s, block_s = refs[2 + n :]
        if not old:
            acc[...] = jnp.zeros_like(acc)
        group(piece_refs, info_v, info_s, packed)
        read_lists(n * RING * SLOTS, info_s, loc_s, block_s)
        multiply((0, OCC), info_s, loc_s, block_s, packed, ints_ref, acc)

    return pl.pallas_call(
        kernel,
        in_specs=[VMEM] * (len(old) + 1 + n),
        out_specs=VMEM,
        out_shape=pltpu.VMEM(((OCC + 1) * SIDE, ints.shape[1]), F32),
        scratch_shapes=[pltpu.VMEM((spots(n) * SIDE, SIDE), BF16), pltpu.VMEM((INFO, SIDE), I32)] + list_scratch(n),
        input_output_aliases={0: 0} if old else {},
        compiler_params=params(14),
        cost_estimate=cost(2**20),
        name="accumulate",
    )(*[kept(v) for v in old], kept(ints), *[kept(v) for v in pieces])


def finish(total, ints, late, blocks, outs, flops):
    n = RING
    width = ints.shape[1]
    new = len(late) == n
    given = [pltpu.VMEM((spots(n) * SIDE, SIDE), BF16), pltpu.VMEM((INFO, SIDE), I32)] if new else []

    def kernel(total_in, ints_ref, *refs):
        late_refs, acc, out_refs, rest = refs[: len(late)], refs[len(late)], refs[len(late) + 1 :][: len(outs)], refs[len(late) + 1 + len(outs) :]
        if new:
            packed, info_v, info_s, loc_s, block_s = rest
            group(late_refs, info_v, info_s, packed)
        else:
            packed, info_v = late_refs
            info_s, loc_s, block_s = rest
            pltpu.sync_copy(info_v, info_s)
        read_lists(n * RING * SLOTS, info_s, loc_s, block_s)
        multiply(blocks, info_s, loc_s, block_s, packed, ints_ref, acc)
        for ref, (start, many) in zip(out_refs, outs):
            ref[...] = acc[start * SIDE : (start + many) * SIDE, :].astype(BF16)

    total, *results = pl.pallas_call(
        kernel,
        in_specs=[VMEM] * (2 + len(late)),
        out_specs=[VMEM] * (1 + len(outs) + len(given)),
        out_shape=[pltpu.VMEM(total.shape, F32)] + [pltpu.VMEM((many * SIDE, width), BF16) for _, many in outs] + given,
        scratch_shapes=list_scratch(n),
        input_output_aliases={0: 0},
        compiler_params=params(8),
        cost_estimate=cost(flops),
        name="finish",
    )(kept(total), kept(ints), *[kept(v) for v in late])
    return total, results[: len(outs)], results[len(outs) :] if new else late


def fold(total, start, many, others, cut, dtype, space):
    width = total.shape[1]
    rows = many * SIDE // cut

    def kernel(total_ref, *refs):
        ins, outs = refs[: len(others)], refs[len(others) :]
        for c, out in enumerate(outs):
            value = total_ref[start * SIDE + c * rows : start * SIDE + (c + 1) * rows, :]
            for ref in ins:
                value = value + ref[c * rows : (c + 1) * rows, :].astype(F32)
            out[...] = value.astype(dtype)

    return pl.pallas_call(
        kernel,
        in_specs=[VMEM] * (1 + len(others)),
        out_specs=[VMEM] * cut,
        out_shape=[space((rows, width), dtype)] * cut,
        compiler_params=params(8),
        cost_estimate=cost(2**20),
        name="fold",
    )(kept(total), *[kept(v) for v in others])


def first_steps(parts):
    return [parts[0]] + [send_first(parts[d], d) for d in (1, 2, 3)]


def second_steps(parts):
    return jnp.concatenate([parts[0]] + [send_second(parts[d], d) for d in (1, 2, 3)], axis=0)


def per_device(amp_tiles, owner_col, local_pair, occ_pair, integrals):
    *parts, raw = sort_own(owner_col[:, 0], local_pair, occ_pair, amp_tiles)
    far_raw = send_y(raw, 2)
    parts = first_steps(parts)
    turned = turn(parts, parts[0])
    own = second_steps(turned)
    up, down, own_other = send_y(own, 1), send_y(own, -1), send_core(own)
    far_parts = sort_far(far_raw, turned[0])
    far = second_steps(turn(first_steps(far_parts), own))
    total = accumulate(None, integrals, [own, own_other])
    up, down, total = lax.optimization_barrier((up, down, total))
    late = [up, down, send_core(up), send_core(down)]
    total = accumulate(total, integrals, [far, send_core(far)])

    total, (to_2,), late = finish(total, integrals, late, (0, 3), [(0, 3)], 2**31)
    got = [send_first(to_2, 2)]
    total, (to_1, to_3), late = finish(total, integrals, late, (3, 9), [(3, 3), (6, 3)], 2**31)
    got += [send_first(to_1, 1), send_first(to_3, -1)]
    total, lasts, late = finish(total, integrals, late, (9, 12), [(9, 1), (10, 1), (11, 1)], 2**31)
    got_last = [send_first(lasts[1], 2), send_first(lasts[0], 1), send_first(lasts[2], -1)]
    total, _, late = finish(total, integrals, late, (12, 16), [], 2**31)
    rest = fold(total, 13, 3, got, 3, BF16, pltpu.VMEM)
    got_last += [send_second(rest[d - 1], d) for d in (2, 1, 3)]
    return fold(total, 12, 1, got_last, 1, BF16, jax.ShapeDtypeStruct)[0]


def solution(mesh):
    return jax.shard_map(
        per_device,
        mesh=mesh,
        in_specs=(
            P(("row", "col"), None, None),
            P(("row", "col"), None),
            P(("row", "col")),
            P(("row", "col")),
            P("col", "row"),
        ),
        out_specs=P("col", "row"),
        check_vma=False,
    )
```

time: 320 us -> 103 us (0.32)
  other arithmetic: 78.6 us -> 0 us
  waiting for transfers between devices: 104 us -> 33.4 us
  local copies, waits for them, and re-layouts: 60.2 us -> 0.26 us
  starting transfers between devices: 3.68 us -> 47.1 us
  blocking collectives: 35.3 us -> 0 us
  matrix products: 22.6 us -> 0 us
  Pallas kernels: 0 us -> 21.4 us
  between operations: 14.1 us -> 0.19 us
    reduce_scatter x1 -> x0, waiting for transfers between devices: 73.8 us -> none  [per_device(): lax.psum_scatter(jnp.dot(matrix, integrals, preferred_element_type=jnp.fl...]
    scatter-add x1 -> x0, other arithmetic: 52.2 us -> none  [per_device(): placed = jnp.zeros((positions, side, side), jnp.float32).at[all_codes].ad...]
    ppermute x0 -> x28, starting transfers between devices: none -> 47.1 us  [the longest x12 15.5 us: send_first(): return lax.ppermute(v, ('row', 'col'), plane_perm(step, False))]
    transpose x1 -> x0, local copies, waits for them, and re-layouts: 43.2 us -> none  [per_device(): matrix.transpose(0, 2, 1, 3).reshape(occ_total * side, CD_DEV * side)]
    ppermute x0 -> x28, waiting for transfers between devices: none -> 33.4 us  [the longest x9 15.1 us: send_second(): return lax.ppermute(v, ('row', 'col'), plane_perm(step, True))]
    all_gather x1 -> x0, waiting for transfers between devices: 25.4 us -> none  [per_device(): lax.all_gather(got_tiles, 'row', axis=0, tiled=True)]
    all_to_all x1 -> x0, blocking collectives: 24.2 us -> none  [per_device(): lax.all_to_all(send_tiles, 'col', split_axis=0, concat_axis=0, tiled=True)]
    convert_element_type x2 -> x0, other arithmetic: 23.5 us -> none  [the longest x1 12.3 us: per_device(): matrix = placed.astype(jnp.bfloat16).reshape(occ_total, CD_DEV, side, side)]
  transfers between devices with their start and end apart: 3 -> 28, of which waited for: 3 -> 14; matrix products, arithmetic and copies ran while one was open for 1% -> 0% of each run, Pallas kernels for 0% -> 16%
where the time goes in v2:
time: 103 us; the launch traced here: 102 us
  starting transfers between devices  47.1 us (46%)
  waiting for transfers between devices  33.4 us (32%)
  Pallas kernels  21.4 us (21%)
    ppermute x12, starting transfers between devices, send_first(): return lax.ppermute(v, ('row', 'col'), plane_perm(step, False))  15.5 us
    ppermute x9, waiting for transfers between devices, send_second(): return lax.ppermute(v, ('row', 'col'), plane_perm(step, True))  15.1 us
    ppermute x12, waiting for transfers between devices, send_first(): return lax.ppermute(v, ('row', 'col'), plane_perm(step, False))  14.7 us
    ppermute x9, starting transfers between devices, send_second(): return lax.ppermute(v, ('row', 'col'), plane_perm(step, True))  12.4 us
    ppermute x4, starting transfers between devices, send_core(): return lax.ppermute(v, 'row', CORE_PERM)  12.2 us
    pallas_call x4, Pallas kernels, finish(): pl.pallas_call(kernel, in_specs=[VMEM] * (2 + len(late)), out_specs=[VMEM...  9.37 us
    pallas_call x2, Pallas kernels, accumulate(): pl.pallas_call(kernel, in_specs=[VMEM] * (len(old) + 1 + n), out_specs=VM...  7.94 us
    ppermute x3, starting transfers between devices, send_y(): return lax.ppermute(v, 'row', row_perm(step))  7 us
  transfers between devices with their start and end apart: 28, of which 14 were waited for; matrix products, arithmetic and copies ran while one was open for 0% of the time, Pallas kernels for 16%

profile of v2, /device:TPU:1, one launch (start us, length us, event | category | flops | bytes accessed | tf_op | source)
XLA Modules:
  0.0 102.3 jit_solution(17962138779879793072)
XLA Ops:
  1.6 2.5 %collective-permute-start = (bf16[1040,128]{1,0:T(8,128)(2,1)S(1)}, bf16[1040,128]{1,0:T(8,128)(2,1)S(1)}, u32[]{:S(2)}, u32[]{:S(2)}) collective-permute-start(bf16[1040,128]{1,0:T(8,128)(2,1)S(1)} %get-tuple-element.40), channel_id=1, source_target_pairs={{0,4},{1,5},{2,6},{3,7},{4,8},{5,9},{6,10},{7,11},{8,12},{9,13},{1... | collective-permute-start | bytes 798728 | tf_op jit(solution)/shard_map/ppermute | solution.py:46
  4.2 3.3 %collective-permute-start.1 = (bf16[1040,128]{1,0:T(8,128)(2,1)S(1)}, bf16[1040,128]{1,0:T(8,128)(2,1)S(1)}, u32[]{:S(2)}, u32[]{:S(2)}) collective-permute-start(bf16[1040,128]{1,0:T(8,128)(2,1)S(1)} %get-tuple-element.41), channel_id=1, source_target_pairs={{0,8},{1,9},{2,10},{3,11},{4,12},{5,13},{6,14},{7,15},{8,0},{9,1},... | collective-permute-start | bytes 798728 | tf_op jit(solution)/shard_map/ppermute | solution.py:46
  8.2 2.9 %collective-permute-start.9 = (bf16[2064,128]{1,0:T(8,128)(2,1)S(1)}, bf16[2064,128]{1,0:T(8,128)(2,1)S(1)}, u32[]{:S(2)}, u32[]{:S(2)}) collective-permute-start(bf16[2064,128]{1,0:T(8,128)(2,1)S(1)} %get-tuple-element.48), channel_id=1, source_target_pairs={{0,64},{16,80},{32,96},{48,112},{64,0},{80,16},{96,32},{112,48},{1... | collective-permute-start | bytes 1585160 | tf_op jit(solution)/shard_map/ppermute | solution.py:54
  11.1 3.3 %collective-permute-done.1.refs_2_ = bf16[1040,128]{1,0:T(8,128)(2,1)S(1)} collective-permute-done((bf16[1040,128]{1,0:T(8,128)(2,1)S(1)}, bf16[1040,128]{1,0:T(8,128)(2,1)S(1)}, u32[]{:S(2)}, u32[]{:S(2)}) %collective-permute-start.1) | collective-permute-done | bytes 266272 | tf_op jit(solution)/shard_map/ppermute | solution.py:46
  15.8 2.5 %collective-permute-start.4 = (bf16[1040,128]{1,0:T(8,128)(2,1)S(1)}, bf16[1040,128]{1,0:T(8,128)(2,1)S(1)}, u32[]{:S(2)}, u32[]{:S(2)}) collective-permute-start(bf16[1040,128]{1,0:T(8,128)(2,1)S(1)} %get-tuple-element.45), channel_id=1, source_target_pairs={{0,2},{1,3},{2,0},{3,1},{4,6},{5,7},{6,4},{7,5},{8,10},{9,11},{10,... | collective-permute-start | bytes 798728 | tf_op jit(solution)/shard_map/ppermute | solution.py:50
  19.4 3.2 %collective-permute-done.9.raw_ref = bf16[2064,128]{1,0:T(8,128)(2,1)S(1)} collective-permute-done((bf16[2064,128]{1,0:T(8,128)(2,1)S(1)}, bf16[2064,128]{1,0:T(8,128)(2,1)S(1)}, u32[]{:S(2)}, u32[]{:S(2)}) %collective-permute-start.9) | collective-permute-done | bytes 528416 | tf_op jit(solution)/shard_map/ppermute | solution.py:54
  23.9 2.6 %collective-permute-start.12 = (bf16[1040,128]{1,0:T(8,128)(2,1)S(1)}, bf16[1040,128]{1,0:T(8,128)(2,1)S(1)}, u32[]{:S(2)}, u32[]{:S(2)}) collective-permute-start(bf16[1040,128]{1,0:T(8,128)(2,1)S(1)} %get-tuple-element.52), channel_id=1, source_target_pairs={{0,12},{1,13},{2,14},{3,15},{4,0},{5,1},{6,2},{7,3},{8,4},{9,5},{1... | collective-permute-start | bytes 798728 | tf_op jit(solution)/shard_map/ppermute | solution.py:46
  26.6 3.4 %collective-permute-start.8 = (bf16[4160,128]{1,0:T(8,128)(2,1)S(1)}, bf16[4160,128]{1,0:T(8,128)(2,1)S(1)}, u32[]{:S(2)}, u32[]{:S(2)}) collective-permute-start(bf16[4160,128]{1,0:T(8,128)(2,1)S(1)} %constant_dynamic-update-slice_fusion.refs_1_.after), channel_id=1, source_target_pairs={{0,16},{16,0},{32,48},{48,32},{64,80},{80,64},{96,112},{112,96},{1... | collective-permute-start | bytes 3194888 | tf_op jit(solution)/shard_map/ppermute | solution.py:58
  30.0 2.7 %collective-permute-start.7 = (bf16[4160,128]{1,0:T(8,128)(2,1)S(1)}, bf16[4160,128]{1,0:T(8,128)(2,1)S(1)}, u32[]{:S(2)}, u32[]{:S(2)}) collective-permute-start(bf16[4160,128]{1,0:T(8,128)(2,1)S(1)} %constant_dynamic-update-slice_fusion.refs_1_.after), channel_id=1, source_target_pairs={{0,96},{16,112},{32,0},{48,16},{64,32},{80,48},{96,64},{112,80},{1... | collective-permute-start | bytes 3194888 | tf_op jit(solution)/shard_map/ppermute | solution.py:54
  35.7 2.2 %collective-permute-start.13 = (bf16[1040,128]{1,0:T(8,128)(2,1)S(1)}, bf16[1040,128]{1,0:T(8,128)(2,1)S(1)}, u32[]{:S(2)}, u32[]{:S(2)}) collective-permute-start(bf16[1040,128]{1,0:T(8,128)(2,1)S(1)} %get-tuple-element.54), channel_id=1, source_target_pairs={{0,1},{1,2},{2,3},{3,0},{4,5},{5,6},{6,7},{7,4},{8,9},{9,10},{10,1... | collective-permute-start | bytes 798728 | tf_op jit(solution)/shard_map/ppermute | solution.py:50
  38.8 3.8 %collective-permute-done.13 = bf16[1040,128]{1,0:T(8,128)(2,1)S(1)} collective-permute-done((bf16[1040,128]{1,0:T(8,128)(2,1)S(1)}, bf16[1040,128]{1,0:T(8,128)(2,1)S(1)}, u32[]{:S(2)}, u32[]{:S(2)}) %collective-permute-start.13) | collective-permute-done | bytes 266272 | tf_op jit(solution)/shard_map/ppermute | solution.py:50
  43.2 2.5 %collective-permute-done.14 = bf16[1040,128]{1,0:T(8,128)(2,1)S(1)} collective-permute-done((bf16[1040,128]{1,0:T(8,128)(2,1)S(1)}, bf16[1040,128]{1,0:T(8,128)(2,1)S(1)}, u32[]{:S(2)}, u32[]{:S(2)}) %collective-permute-start.14) | collective-permute-done | bytes 266272 | tf_op jit(solution)/shard_map/ppermute | solution.py:50
  45.7 2.4 %collective-permute-done.15 = bf16[1040,128]{1,0:T(8,128)(2,1)S(1)} collective-permute-done((bf16[1040,128]{1,0:T(8,128)(2,1)S(1)}, bf16[1040,128]{1,0:T(8,128)(2,1)S(1)}, u32[]{:S(2)}, u32[]{:S(2)}) %collective-permute-start.15) | collective-permute-done | bytes 266272 | tf_op jit(solution)/shard_map/ppermute | solution.py:50
  48.2 6.4 %collective-permute-start.16 = (bf16[4160,128]{1,0:T(8,128)(2,1)S(1)}, bf16[4160,128]{1,0:T(8,128)(2,1)S(1)}, u32[]{:S(2)}, u32[]{:S(2)}) collective-permute-start(bf16[4160,128]{1,0:T(8,128)(2,1)S(1)} %constant_dynamic-update-slice_fusion.4.refs_2_), channel_id=1, source_target_pairs={{0,16},{16,0},{32,48},{48,32},{64,80},{80,64},{96,112},{112,96},{1... | collective-permute-start | bytes 3194888 | tf_op jit(solution)/shard_map/ppermute | solution.py:58
  54.5 4.2 %accumulate.2.refs_0_ = f32[2176,1024]{1,0:T(8,128)S(1)} custom-call(bf16[4096,1024]{1,0:T(8,128)(2,1)S(1)} %copy-done, bf16[4160,128]{1,0:T(8,128)(2,1)S(1)} %constant_dynamic-update-slice_fusion.refs_1_.after, bf16[4160,128]{1,0:T(8,128)(2,1)S(1)} %collective-permute-done.8.refs_2_), custom_call_target="tpu_custom_call" | custom-call | flops 1048576 | bytes 4096 | tf_op jit(solution)/shard_map/accumulate/pallas_call | solution.py:318
  59.1 2.4 %collective-permute-start.17 = (bf16[4160,128]{1,0:T(8,128)(2,1)S(1)}, bf16[4160,128]{1,0:T(8,128)(2,1)S(1)}, u32[]{:S(2)}, u32[]{:S(2)}) collective-permute-start(bf16[4160,128]{1,0:T(8,128)(2,1)S(1)} %collective-permute-done.6.refs_0_), channel_id=1, source_target_pairs={{0,16},{16,0},{32,48},{48,32},{64,80},{80,64},{96,112},{112,96},{1... | collective-permute-start | bytes 3194888 | tf_op jit(solution)/shard_map/ppermute | solution.py:58
  61.5 3.8 %accumulate.3.total_in = f32[2176,1024]{1,0:T(8,128)S(1)} custom-call(f32[2176,1024]{1,0:T(8,128)S(1)} %accumulate.2.refs_0_, bf16[4096,1024]{1,0:T(8,128)(2,1)S(1)} %copy-done, bf16[4160,128]{1,0:T(8,128)(2,1)S(1)} %constant_dynamic-update-slice_fusion.4.refs_2_, bf16[4160,128]{1,0:T(8,128)(2,1)S(1)} %collective-permute-done.16.refs_3_), custom_call_target="tpu_custom_call", output_to_operand_aliasing={{}: (0, {})} | custom-call | flops 1048576 | bytes 4096 | tf_op jit(solution)/shard_map/accumulate/pallas_call | solution.py:318
  65.3 2.7 %finish.4 = (f32[2176,1024]{1,0:T(8,128)S(1)}, bf16[384,1024]{1,0:T(8,128)(2,1)S(1)}, bf16[18688,128]{1,0:T(8,128)(2,1)S(1)}, s32[32,128]{1,0:T(8,128)S(1)}) custom-call(f32[2176,1024]{1,0:T(8,128)S(1)} %accumulate.3.total_in, bf16[4096,1024]{1,0:T(8,128)(2,1)S(1)} %copy-done, ...), custom_call_target="tpu_custom_call", output_to_operand_aliasing={{0}: (0, {})} | custom-call | flops 2147483648 | bytes 4096 | tf_op jit(solution)/shard_map/finish/pallas_call | solution.py:351
  68.9 2.6 %finish.5 = (f32[2176,1024]{1,0:T(8,128)S(1)}, bf16[384,1024]{1,0:T(8,128)(2,1)S(1)}, bf16[384,1024]{1,0:T(8,128)(2,1)S(1)}) custom-call(f32[2176,1024]{1,0:T(8,128)S(1)} %get-tuple-element.59.total_in, bf16[4096,1024]{1,0:T(8,128)(2,1)S(1)} %copy-done, bf16[18688,128]{1,0:T(8,128)(2,1)S(1)} %get-tuple-element.60.refs_0_, ...), custom_call_target="tpu_custom_call", output_to_operand_aliasing={{0}: (0, {})} | custom-call | flops 2147483648 | bytes 4096 | tf_op jit(solution)/shard_map/finish/pallas_call | solution.py:351
  71.6 2.7 %collective-permute-start.24 = (bf16[384,1024]{1,0:T(8,128)(2,1)S(1)}, bf16[384,1024]{1,0:T(8,128)(2,1)S(1)}, u32[]{:S(2)}, u32[]{:S(2)}) collective-permute-start(bf16[384,1024]{1,0:T(8,128)(2,1)S(1)} %get-tuple-element.69), channel_id=1, source_target_pairs={{0,12},{1,13},{2,14},{3,15},{4,0},{5,1},{6,2},{7,3},{8,4},{9,5},{1... | collective-permute-start | bytes 2359304 | tf_op jit(solution)/shard_map/ppermute | solution.py:46
  74.3 2.1 %finish.6 = (f32[2176,1024]{1,0:T(8,128)S(1)}, bf16[128,1024]{1,0:T(8,128)(2,1)S(1)}, bf16[128,1024]{1,0:T(8,128)(2,1)S(1)}, bf16[128,1024]{1,0:T(8,128)(2,1)S(1)}) custom-call(f32[2176,1024]{1,0:T(8,128)S(1)} %get-tuple-element.62.total_in, bf16[4096,1024]{1,0:T(8,128)(2,1)S(1)} %copy-done, ...), custom_call_target="tpu_custom_call", output_to_operand_aliasing={{0}: (0, {})} | custom-call | flops 2147483648 | bytes 4096 | tf_op jit(solution)/shard_map/finish/pallas_call | solution.py:351
  82.3 7.1 %collective-permute-done.23.refs_1_ = bf16[384,1024]{1,0:T(8,128)(2,1)S(1)} collective-permute-done((bf16[384,1024]{1,0:T(8,128)(2,1)S(1)}, bf16[384,1024]{1,0:T(8,128)(2,1)S(1)}, u32[]{:S(2)}, u32[]{:S(2)}) %collective-permute-start.23) | collective-permute-done | bytes 786464 | tf_op jit(solution)/shard_map/ppermute | solution.py:46
  95.0 3.6 %collective-permute-done.25.refs_3_ = bf16[128,1024]{1,0:T(8,128)(2,1)S(1)} collective-permute-done((bf16[128,1024]{1,0:T(8,128)(2,1)S(1)}, bf16[128,1024]{1,0:T(8,128)(2,1)S(1)}, u32[]{:S(2)}, u32[]{:S(2)}) %collective-permute-start.25) | collective-permute-done | bytes 262176 | tf_op jit(solution)/shard_map/ppermute | solution.py:50
  98.6 2.8 %collective-permute-done.26.refs_4_ = bf16[128,1024]{1,0:T(8,128)(2,1)S(1)} collective-permute-done((bf16[128,1024]{1,0:T(8,128)(2,1)S(1)}, bf16[128,1024]{1,0:T(8,128)(2,1)S(1)}, u32[]{:S(2)}, u32[]{:S(2)}) %collective-permute-start.26) | collective-permute-done | bytes 262176 | tf_op jit(solution)/shard_map/ppermute | solution.py:50
  (54 shorter events, 24.6 us)
Async XLA Ops:
  1.6 9.5 %collective-permute-start = (bf16[1040,128]{1,0:T(8,128)(2,1)S(1)}, bf16[1040,128]{1,0:T(8,128)(2,1)S(1)}, u32[]{:S(2)}, u32[]{:S(2)}) collective-permute-start(bf16[1040,128]{1,0:T(8,128)(2,1)S(1)} %get-tuple-element.40), channel_id=1, source_target_pairs={{0,4},{1,5},{2,6},{3,7},{4,8},{5,9},{6,10},{7,11},{8,12},{9,13},{1... | collective-permute-start | bytes 798728 | tf_op jit(solution)/shard_map/ppermute | solution.py:46
  4.2 10.2 %collective-permute-start.1 = (bf16[1040,128]{1,0:T(8,128)(2,1)S(1)}, bf16[1040,128]{1,0:T(8,128)(2,1)S(1)}, u32[]{:S(2)}, u32[]{:S(2)}) collective-permute-start(bf16[1040,128]{1,0:T(8,128)(2,1)S(1)} %get-tuple-element.41), channel_id=1, source_target_pairs={{0,8},{1,9},{2,10},{3,11},{4,12},{5,13},{6,14},{7,15},{8,0},{9,1},... | collective-permute-start | bytes 798728 | tf_op jit(solution)/shard_map/ppermute | solution.py:46
  7.5 7.0 %collective-permute-start.2 = (bf16[1040,128]{1,0:T(8,128)(2,1)S(1)}, bf16[1040,128]{1,0:T(8,128)(2,1)S(1)}, u32[]{:S(2)}, u32[]{:S(2)}) collective-permute-start(bf16[1040,128]{1,0:T(8,128)(2,1)S(1)} %get-tuple-element.42), channel_id=1, source_target_pairs={{0,12},{1,13},{2,14},{3,15},{4,0},{5,1},{6,2},{7,3},{8,4},{9,5},{1... | collective-permute-start | bytes 798728 | tf_op jit(solution)/shard_map/ppermute | solution.py:46
  8.2 14.4 %collective-permute-start.9 = (bf16[2064,128]{1,0:T(8,128)(2,1)S(1)}, bf16[2064,128]{1,0:T(8,128)(2,1)S(1)}, u32[]{:S(2)}, u32[]{:S(2)}) collective-permute-start(bf16[2064,128]{1,0:T(8,128)(2,1)S(1)} %get-tuple-element.48), channel_id=1, source_target_pairs={{0,64},{16,80},{32,96},{48,112},{64,0},{80,16},{96,32},{112,48},{1... | collective-permute-start | bytes 1585160 | tf_op jit(solution)/shard_map/ppermute | solution.py:54
  14.5 9.4 %collective-permute-start.3 = (bf16[1040,128]{1,0:T(8,128)(2,1)S(1)}, bf16[1040,128]{1,0:T(8,128)(2,1)S(1)}, u32[]{:S(2)}, u32[]{:S(2)}) collective-permute-start(bf16[1040,128]{1,0:T(8,128)(2,1)S(1)} %get-tuple-element.44), channel_id=1, source_target_pairs={{0,1},{1,2},{2,3},{3,0},{4,5},{5,6},{6,7},{7,4},{8,9},{9,10},{10,1... | collective-permute-start | bytes 798728 | tf_op jit(solution)/shard_map/ppermute | solution.py:50
  15.8 10.7 %collective-permute-start.4 = (bf16[1040,128]{1,0:T(8,128)(2,1)S(1)}, bf16[1040,128]{1,0:T(8,128)(2,1)S(1)}, u32[]{:S(2)}, u32[]{:S(2)}) collective-permute-start(bf16[1040,128]{1,0:T(8,128)(2,1)S(1)} %get-tuple-element.45), channel_id=1, source_target_pairs={{0,2},{1,3},{2,0},{3,1},{4,6},{5,7},{6,4},{7,5},{8,10},{9,11},{10,... | collective-permute-start | bytes 798728 | tf_op jit(solution)/shard_map/ppermute | solution.py:50
  18.3 8.3 %collective-permute-start.5 = (bf16[1040,128]{1,0:T(8,128)(2,1)S(1)}, bf16[1040,128]{1,0:T(8,128)(2,1)S(1)}, u32[]{:S(2)}, u32[]{:S(2)}) collective-permute-start(bf16[1040,128]{1,0:T(8,128)(2,1)S(1)} %get-tuple-element.46), channel_id=1, source_target_pairs={{0,3},{1,0},{2,1},{3,2},{4,7},{5,4},{6,5},{7,6},{8,11},{9,8},{10,9... | collective-permute-start | bytes 798728 | tf_op jit(solution)/shard_map/ppermute | solution.py:50
  23.7 10.6 %collective-permute-start.10 = (bf16[1040,128]{1,0:T(8,128)(2,1)S(1)}, bf16[1040,128]{1,0:T(8,128)(2,1)S(1)}, u32[]{:S(2)}, u32[]{:S(2)}) collective-permute-start(bf16[1040,128]{1,0:T(8,128)(2,1)S(1)} %get-tuple-element.50), channel_id=1, source_target_pairs={{0,4},{1,5},{2,6},{3,7},{4,8},{5,9},{6,10},{7,11},{8,12},{9,13},{1... | collective-permute-start | bytes 798728 | tf_op jit(solution)/shard_map/ppermute | solution.py:46
  23.8 11.9 %collective-permute-start.11 = (bf16[1040,128]{1,0:T(8,128)(2,1)S(1)}, bf16[1040,128]{1,0:T(8,128)(2,1)S(1)}, u32[]{:S(2)}, u32[]{:S(2)}) collective-permute-start(bf16[1040,128]{1,0:T(8,128)(2,1)S(1)} %get-tuple-element.51), channel_id=1, source_target_pairs={{0,8},{1,9},{2,10},{3,11},{4,12},{5,13},{6,14},{7,15},{8,0},{9,1},... | collective-permute-start | bytes 798728 | tf_op jit(solution)/shard_map/ppermute | solution.py:46
  23.9 11.8 %collective-permute-start.12 = (bf16[1040,128]{1,0:T(8,128)(2,1)S(1)}, bf16[1040,128]{1,0:T(8,128)(2,1)S(1)}, u32[]{:S(2)}, u32[]{:S(2)}) collective-permute-start(bf16[1040,128]{1,0:T(8,128)(2,1)S(1)} %get-tuple-element.52), channel_id=1, source_target_pairs={{0,12},{1,13},{2,14},{3,15},{4,0},{5,1},{6,2},{7,3},{8,4},{9,5},{1... | collective-permute-start | bytes 798728 | tf_op jit(solution)/shard_map/ppermute | solution.py:46
  26.6 27.9 %collective-permute-start.8 = (bf16[4160,128]{1,0:T(8,128)(2,1)S(1)}, bf16[4160,128]{1,0:T(8,128)(2,1)S(1)}, u32[]{:S(2)}, u32[]{:S(2)}) collective-permute-start(bf16[4160,128]{1,0:T(8,128)(2,1)S(1)} %constant_dynamic-update-slice_fusion.refs_1_.after), channel_id=1, source_target_pairs={{0,16},{16,0},{32,48},{48,32},{64,80},{80,64},{96,112},{112,96},{1... | collective-permute-start | bytes 3194888 | tf_op jit(solution)/shard_map/ppermute | solution.py:58
  30.0 28.8 %collective-permute-start.7 = (bf16[4160,128]{1,0:T(8,128)(2,1)S(1)}, bf16[4160,128]{1,0:T(8,128)(2,1)S(1)}, u32[]{:S(2)}, u32[]{:S(2)}) collective-permute-start(bf16[4160,128]{1,0:T(8,128)(2,1)S(1)} %constant_dynamic-update-slice_fusion.refs_1_.after), channel_id=1, source_target_pairs={{0,96},{16,112},{32,0},{48,16},{64,32},{80,48},{96,64},{112,80},{1... | collective-permute-start | bytes 3194888 | tf_op jit(solution)/shard_map/ppermute | solution.py:54
  34.3 24.8 %collective-permute-start.6 = (bf16[4160,128]{1,0:T(8,128)(2,1)S(1)}, bf16[4160,128]{1,0:T(8,128)(2,1)S(1)}, u32[]{:S(2)}, u32[]{:S(2)}) collective-permute-start(bf16[4160,128]{1,0:T(8,128)(2,1)S(1)} %constant_dynamic-update-slice_fusion.refs_1_.after), channel_id=1, source_target_pairs={{0,32},{16,48},{32,64},{48,80},{64,96},{80,112},{96,0},{112,16},{1... | collective-permute-start | bytes 3194888 | tf_op jit(solution)/shard_map/ppermute | solution.py:54
  37.9 7.8 %collective-permute-start.14 = (bf16[1040,128]{1,0:T(8,128)(2,1)S(1)}, bf16[1040,128]{1,0:T(8,128)(2,1)S(1)}, u32[]{:S(2)}, u32[]{:S(2)}) collective-permute-start(bf16[1040,128]{1,0:T(8,128)(2,1)S(1)} %get-tuple-element.55), channel_id=1, source_target_pairs={{0,2},{1,3},{2,0},{3,1},{4,6},{5,7},{6,4},{7,5},{8,10},{9,11},{10,... | collective-permute-start | bytes 798728 | tf_op jit(solution)/shard_map/ppermute | solution.py:50
  48.2 13.3 %collective-permute-start.16 = (bf16[4160,128]{1,0:T(8,128)(2,1)S(1)}, bf16[4160,128]{1,0:T(8,128)(2,1)S(1)}, u32[]{:S(2)}, u32[]{:S(2)}) collective-permute-start(bf16[4160,128]{1,0:T(8,128)(2,1)S(1)} %constant_dynamic-update-slice_fusion.4.refs_2_), channel_id=1, source_target_pairs={{0,16},{16,0},{32,48},{48,32},{64,80},{80,64},{96,112},{112,96},{1... | collective-permute-start | bytes 3194888 | tf_op jit(solution)/shard_map/ppermute | solution.py:58
  68.0 12.9 %collective-permute-start.22 = (bf16[384,1024]{1,0:T(8,128)(2,1)S(1)}, bf16[384,1024]{1,0:T(8,128)(2,1)S(1)}, u32[]{:S(2)}, u32[]{:S(2)}) collective-permute-start(bf16[384,1024]{1,0:T(8,128)(2,1)S(1)} %get-tuple-element.67), channel_id=1, source_target_pairs={{0,8},{1,9},{2,10},{3,11},{4,12},{5,13},{6,14},{7,15},{8,0},{9,1},... | collective-permute-start | bytes 2359304 | tf_op jit(solution)/shard_map/ppermute | solution.py:46
  71.5 17.8 %collective-permute-start.23 = (bf16[384,1024]{1,0:T(8,128)(2,1)S(1)}, bf16[384,1024]{1,0:T(8,128)(2,1)S(1)}, u32[]{:S(2)}, u32[]{:S(2)}) collective-permute-start(bf16[384,1024]{1,0:T(8,128)(2,1)S(1)} %get-tuple-element.68), channel_id=1, source_target_pairs={{0,4},{1,5},{2,6},{3,7},{4,8},{5,9},{6,10},{7,11},{8,12},{9,13},{1... | collective-permute-start | bytes 2359304 | tf_op jit(solution)/shard_map/ppermute | solution.py:46
  71.6 17.7 %collective-permute-start.24 = (bf16[384,1024]{1,0:T(8,128)(2,1)S(1)}, bf16[384,1024]{1,0:T(8,128)(2,1)S(1)}, u32[]{:S(2)}, u32[]{:S(2)}) collective-permute-start(bf16[384,1024]{1,0:T(8,128)(2,1)S(1)} %get-tuple-element.69), channel_id=1, source_target_pairs={{0,12},{1,13},{2,14},{3,15},{4,0},{5,1},{6,2},{7,3},{8,4},{9,5},{1... | collective-permute-start | bytes 2359304 | tf_op jit(solution)/shard_map/ppermute | solution.py:46
  76.3 15.9 %collective-permute-start.19 = (bf16[128,1024]{1,0:T(8,128)(2,1)S(1)}, bf16[128,1024]{1,0:T(8,128)(2,1)S(1)}, u32[]{:S(2)}, u32[]{:S(2)}) collective-permute-start(bf16[128,1024]{1,0:T(8,128)(2,1)S(1)} %get-tuple-element.64), channel_id=1, source_target_pairs={{0,8},{1,9},{2,10},{3,11},{4,12},{5,13},{6,14},{7,15},{8,0},{9,1},... | collective-permute-start | bytes 786440 | tf_op jit(solution)/shard_map/ppermute | solution.py:46
  77.5 17.4 %collective-permute-start.20 = (bf16[128,1024]{1,0:T(8,128)(2,1)S(1)}, bf16[128,1024]{1,0:T(8,128)(2,1)S(1)}, u32[]{:S(2)}, u32[]{:S(2)}) collective-permute-start(bf16[128,1024]{1,0:T(8,128)(2,1)S(1)} %get-tuple-element.65), channel_id=1, source_target_pairs={{0,4},{1,5},{2,6},{3,7},{4,8},{5,9},{6,10},{7,11},{8,12},{9,13},{1... | collective-permute-start | bytes 786440 | tf_op jit(solution)/shard_map/ppermute | solution.py:46
  81.0 14.0 %collective-permute-start.21 = (bf16[128,1024]{1,0:T(8,128)(2,1)S(1)}, bf16[128,1024]{1,0:T(8,128)(2,1)S(1)}, u32[]{:S(2)}, u32[]{:S(2)}) collective-permute-start(bf16[128,1024]{1,0:T(8,128)(2,1)S(1)} %get-tuple-element.66), channel_id=1, source_target_pairs={{0,12},{1,13},{2,14},{3,15},{4,0},{5,1},{6,2},{7,3},{8,4},{9,5},{1... | collective-permute-start | bytes 786440 | tf_op jit(solution)/shard_map/ppermute | solution.py:46
  89.7 8.9 %collective-permute-start.25 = (bf16[128,1024]{1,0:T(8,128)(2,1)S(1)}, bf16[128,1024]{1,0:T(8,128)(2,1)S(1)}, u32[]{:S(2)}, u32[]{:S(2)}) collective-permute-start(bf16[128,1024]{1,0:T(8,128)(2,1)S(1)} %get-tuple-element.70), channel_id=1, source_target_pairs={{0,2},{1,3},{2,0},{3,1},{4,6},{5,7},{6,4},{7,5},{8,10},{9,11},{10,... | collective-permute-start | bytes 786440 | tf_op jit(solution)/shard_map/ppermute | solution.py:50
  91.0 10.4 %collective-permute-start.26 = (bf16[128,1024]{1,0:T(8,128)(2,1)S(1)}, bf16[128,1024]{1,0:T(8,128)(2,1)S(1)}, u32[]{:S(2)}, u32[]{:S(2)}) collective-permute-start(bf16[128,1024]{1,0:T(8,128)(2,1)S(1)} %get-tuple-element.71), channel_id=1, source_target_pairs={{0,1},{1,2},{2,3},{3,0},{4,5},{5,6},{6,7},{7,4},{8,9},{9,10},{10,1... | collective-permute-start | bytes 786440 | tf_op jit(solution)/shard_map/ppermute | solution.py:50
  92.3 9.1 %collective-permute-start.27 = (bf16[128,1024]{1,0:T(8,128)(2,1)S(1)}, bf16[128,1024]{1,0:T(8,128)(2,1)S(1)}, u32[]{:S(2)}, u32[]{:S(2)}) collective-permute-start(bf16[128,1024]{1,0:T(8,128)(2,1)S(1)} %get-tuple-element.72), channel_id=1, source_target_pairs={{0,3},{1,0},{2,1},{3,2},{4,7},{5,4},{6,5},{7,6},{8,11},{9,8},{10,9... | collective-permute-start | bytes 786440 | tf_op jit(solution)/shard_map/ppermute | solution.py:50
  (5 other events, 62.5 us)

commit v3 on v2

--- a/solution.py
+++ b/solution.py
@@ -216,18 +216,24 @@
 
 
 def order(da, db):
-    travels = jnp.where(da == 2, 0, jnp.where(da == 1, 3, 6)) + db - 1
-    return jnp.where(da == 0, 12 + db, jnp.where(db == 0, 8 + da, travels))
+    ahead = jnp.where(db >= 2, 2 + db, 8 + db)
+    behind = jnp.where(db >= 2, 8 + db, 6 + db)
+    return jnp.where(da == 0, 12 + db, jnp.where(da == 2, db, jnp.where(da == 1, ahead, behind)))
+
+
+def message_places(pieces):
+    return [(piece, m * MSG) for piece in pieces for m in range(piece.shape[0] // MSG)]
 
 
 def group(pieces, info_v, info_s, packed):
     first, a, b = place()
-    n = len(pieces) * RING * SLOTS
+    messages = message_places(pieces)
+    n = len(messages) * SLOTS
     lanes = lax.broadcasted_iota(I32, (8, SIDE), 1)
     head = jnp.zeros((8, SIDE), F32)
-    for i in range(len(pieces) * RING):
-        at = (i % RING) * MSG + SLOTS * SIDE
-        one = pieces[i // RING][at : at + HEAD, :].astype(F32)[0:8]
+    for i, (piece, at) in enumerate(messages):
+        at += SLOTS * SIDE
+        one = piece[at : at + HEAD, :].astype(F32)[0:8]
         here = (lanes >= i * SLOTS) & (lanes < (i + 1) * SLOTS)
         head = jnp.where(here, pltpu.roll(one, i * SLOTS, 1) if i else one, head)
     occ = jnp.broadcast_to(head[0:1], (8, SIDE)).astype(I32) - 1
@@ -256,8 +262,9 @@
         packed[pl.ds(free, SIDE), :] = jnp.zeros((SIDE, SIDE), BF16)
     for i in range(n):
         to = pl.multiple_of(info_s[0, i] * SIDE, SIDE)
-        at = (i // SLOTS % RING) * MSG + (i % SLOTS) * SIDE
-        packed[pl.ds(to, SIDE), :] = pieces[i // (RING * SLOTS)][at : at + SIDE, :]
+        piece, at = messages[i // SLOTS]
+        at += i % SLOTS * SIDE
+        packed[pl.ds(to, SIDE), :] = piece[at : at + SIDE, :]
 
 
 def read_lists(n, info_s, loc_s, block_s):
@@ -290,7 +297,7 @@
 
 
 def spots(n):
-    return n * RING * SLOTS + OCC + 2
+    return n + OCC + 2
 
 
 def list_scratch(n):
@@ -302,22 +309,23 @@
 
 
 def accumulate(total, ints, pieces):
-    n = len(pieces)
+    many = len(pieces)
+    n = len(message_places(pieces)) * SLOTS
     old = [] if total is None else [total]
 
     def kernel(*refs):
         refs = refs[len(old) :]
-        ints_ref, piece_refs, acc = refs[0], refs[1 : 1 + n], refs[1 + n]
-        packed, info_v, info_s, loc_s, block_s = refs[2 + n :]
+        ints_ref, piece_refs, acc = refs[0], refs[1 : 1 + many], refs[1 + many]
+        packed, info_v, info_s, loc_s, block_s = refs[2 + many :]
         if not old:
             acc[...] = jnp.zeros_like(acc)
         group(piece_refs, info_v, info_s, packed)
-        read_lists(n * RING * SLOTS, info_s, loc_s, block_s)
+        read_lists(n, info_s, loc_s, block_s)
         multiply((0, OCC), info_s, loc_s, block_s, packed, ints_ref, acc)
 
     return pl.pallas_call(
         kernel,
-        in_specs=[VMEM] * (len(old) + 1 + n),
+        in_specs=[VMEM] * (len(old) + 1 + many),
         out_specs=VMEM,
         out_shape=pltpu.VMEM(((OCC + 1) * SIDE, ints.shape[1]), F32),
         scratch_shapes=[pltpu.VMEM((spots(n) * SIDE, SIDE), BF16), pltpu.VMEM((INFO, SIDE), I32)] + list_scratch(n),
@@ -329,9 +337,9 @@
 
 
 def finish(total, ints, late, blocks, outs, flops):
-    n = RING
+    new = late[1].dtype == BF16
+    n = len(message_places(late)) * SLOTS if new else late[0].shape[0] // SIDE - OCC - 2
     width = ints.shape[1]
-    new = len(late) == n
     given = [pltpu.VMEM((spots(n) * SIDE, SIDE), BF16), pltpu.VMEM((INFO, SIDE), I32)] if new else []
 
     def kernel(total_in, ints_ref, *refs):
@@ -343,7 +351,7 @@
             packed, info_v = late_refs
             info_s, loc_s, block_s = rest
             pltpu.sync_copy(info_v, info_s)
-        read_lists(n * RING * SLOTS, info_s, loc_s, block_s)
+        read_lists(n, info_s, loc_s, block_s)
         multiply(blocks, info_s, loc_s, block_s, packed, ints_ref, acc)
         for ref, (start, many) in zip(out_refs, outs):
             ref[...] = acc[start * SIDE : (start + many) * SIDE, :].astype(BF16)
@@ -362,23 +370,21 @@
     return total, results[: len(outs)], results[len(outs) :] if new else late
 
 
-def fold(total, start, many, others, cut, dtype, space):
+def fold(total, others, outs, dtype, space):
     width = total.shape[1]
-    rows = many * SIDE // cut
 
     def kernel(total_ref, *refs):
-        ins, outs = refs[: len(others)], refs[len(others) :]
-        for c, out in enumerate(outs):
-            value = total_ref[start * SIDE + c * rows : start * SIDE + (c + 1) * rows, :]
-            for ref in ins:
-                value = value + ref[c * rows : (c + 1) * rows, :].astype(F32)
+        for (start, many, terms), out in zip(outs, refs[len(others) :]):
+            value = total_ref[start * SIDE : (start + many) * SIDE, :]
+            for which, at in terms:
+                value = value + refs[which][at * SIDE : (at + many) * SIDE, :].astype(F32)
             out[...] = value.astype(dtype)
 
     return pl.pallas_call(
         kernel,
         in_specs=[VMEM] * (1 + len(others)),
-        out_specs=[VMEM] * cut,
-        out_shape=[space((rows, width), dtype)] * cut,
+        out_specs=[VMEM] * len(outs),
+        out_shape=[space((many * SIDE, width), dtype) for _, many, _ in outs],
         compiler_params=params(8),
         cost_estimate=cost(2**20),
         name="fold",
@@ -390,33 +396,93 @@
 
 
 def second_steps(parts):
-    return jnp.concatenate([parts[0]] + [send_second(parts[d], d) for d in (1, 2, 3)], axis=0)
+    return [parts[0]] + [send_second(parts[d], d) for d in (1, 2, 3)]
+
+
+def join(parts, after):
+    sizes = [v.shape[0] for v in parts]
+
+    def kernel(after_ref, *refs):
+        at = 0
+        for ref, size in zip(refs, sizes):
+            refs[-1][at : at + size, :] = ref[...]
+            at += size
+
+    return pl.pallas_call(
+        kernel,
+        in_specs=[ANY] + [VMEM] * len(parts),
+        out_specs=VMEM,
+        out_shape=pltpu.VMEM((sum(sizes), SIDE), BF16),
+        compiler_params=params(8),
+        cost_estimate=cost(2**20),
+        name="join",
+    )(after, *[kept(v) for v in parts])
+
+
+def hold(parts, after):
+    def kernel(after_ref, *refs):
+        for src, dst in zip(refs, refs[len(parts) :]):
+            dst[...] = src[...]
+
+    return pl.pallas_call(
+        kernel,
+        in_specs=[ANY] + [VMEM] * len(parts),
+        out_specs=[VMEM] * len(parts),
+        out_shape=[pltpu.VMEM(v.shape, BF16) for v in parts],
+        compiler_params=params(8),
+        cost_estimate=cost(2**20),
+        name="hold",
+    )(after, *[kept(v) for v in parts])
+
+
+def load(ints):
+    def kernel(src, dst, sem):
+        copy = pltpu.make_async_copy(src, dst, sem)
+        copy.start()
+        copy.wait()
+
+    return pl.pallas_call(
+        kernel,
+        in_specs=[HBM],
+        out_specs=VMEM,
+        out_shape=pltpu.VMEM(ints.shape, ints.dtype),
+        scratch_shapes=[pltpu.SemaphoreType.DMA],
+        compiler_params=params(8),
+        cost_estimate=cost(2**20),
+        name="load",
+    )(in_hbm(ints))
 
 
 def per_device(amp_tiles, owner_col, local_pair, occ_pair, integrals):
     *parts, raw = sort_own(owner_col[:, 0], local_pair, occ_pair, amp_tiles)
     far_raw = send_y(raw, 2)
-    parts = first_steps(parts)
-    turned = turn(parts, parts[0])
-    own = second_steps(turned)
-    up, down, own_other = send_y(own, 1), send_y(own, -1), send_core(own)
+    ints = load(integrals)
+    turned = turn(first_steps(parts), ints)
+    near = second_steps(turned)
+    own = jnp.concatenate(near, axis=0)
+    up, down = send_y(own, 1), send_y(own, -1)
     far_parts = sort_far(far_raw, turned[0])
-    far = second_steps(turn(first_steps(far_parts), own))
-    total = accumulate(None, integrals, [own, own_other])
+    far_turned = turn(first_steps(far_parts), own)
+    far = second_steps(far_turned)
+    total = accumulate(None, ints, [own] + [send_core(v) for v in near])
+    far_other = [send_core(v) for v in [join(far[:1], total)] + far[1:]]
+    total = accumulate(total, ints, far + far_other)
     up, down, total = lax.optimization_barrier((up, down, total))
-    late = [up, down, send_core(up), send_core(down)]
-    total = accumulate(total, integrals, [far, send_core(far)])
-
-    total, (to_2,), late = finish(total, integrals, late, (0, 3), [(0, 3)], 2**31)
-    got = [send_first(to_2, 2)]
-    total, (to_1, to_3), late = finish(total, integrals, late, (3, 9), [(3, 3), (6, 3)], 2**31)
-    got += [send_first(to_1, 1), send_first(to_3, -1)]
-    total, lasts, late = finish(total, integrals, late, (9, 12), [(9, 1), (10, 1), (11, 1)], 2**31)
-    got_last = [send_first(lasts[1], 2), send_first(lasts[0], 1), send_first(lasts[2], -1)]
-    total, _, late = finish(total, integrals, late, (12, 16), [], 2**31)
-    rest = fold(total, 13, 3, got, 3, BF16, pltpu.VMEM)
-    got_last += [send_second(rest[d - 1], d) for d in (2, 1, 3)]
-    return fold(total, 12, 1, got_last, 1, BF16, jax.ShapeDtypeStruct)[0]
+    late = [send_core(up), send_core(down)]
+    total = accumulate(total, ints, [up, down])
+
+    total, (two_ahead, two_behind), late = finish(total, ints, late, (0, 4), [(0, 2), (2, 2)], 2**31)
+    from_behind, from_ahead = send_first(two_ahead, 1), send_first(two_behind, -1)
+    total, (ahead, behind), late = finish(total, ints, late, (4, 8), [(4, 2), (6, 2)], 2**31)
+    got = [send_first(behind, -1), send_first(ahead, 1)]
+    total, _, late = finish(total, ints, late, (8, 12), [], 2**31)
+    ahead, behind = fold(total, [from_behind, from_ahead], [(8, 2, [(0, 0)]), (10, 2, [(1, 0)])], BF16, pltpu.VMEM)
+    got += [send_first(ahead, 1), send_first(behind, -1)]
+    total, _, late = finish(total, ints, late, (12, 16), [], 2**31)
+    outs = [(13, 1, [(0, 1), (2, 1)]), (14, 1, [(1, 0), (3, 0)]), (15, 1, [(1, 1), (3, 1)])]
+    rest = fold(total, got, outs, BF16, pltpu.VMEM)
+    last = [got[0], got[2]] + [send_second(rest[d - 1], d) for d in (2, 1, 3)]
+    return fold(total, last, [(12, 1, [(i, 0) for i in range(5)])], BF16, jax.ShapeDtypeStruct)[0]
 
 
 def solution(mesh):

time: 103 us -> 101 us (0.981)
  waiting for transfers between devices: 33.4 us -> 21.1 us
  Pallas kernels: 21.4 us -> 27.5 us
  starting transfers between devices: 47.1 us -> 51.2 us
    ppermute x9, waiting for transfers between devices: 15.1 us -> 6.1 us  [send_second(): return lax.ppermute(v, ('row', 'col'), plane_perm(step, True))]
    pallas_call x2 -> x5, Pallas kernels: 7.94 us -> 15.6 us  [the longest x3 12.2 us: accumulate(): pl.pallas_call(kernel, in_specs=[VMEM] * (len(old) + 1 + many), out_specs...]
    ppermute x12, waiting for transfers between devices: 14.7 us -> 8.33 us  [send_first(): return lax.ppermute(v, ('row', 'col'), plane_perm(step, False))]
    ppermute x4 -> x10, starting transfers between devices: 12.2 us -> 16.6 us  [send_core(): return lax.ppermute(v, 'row', CORE_PERM)]
    ppermute x4 -> x10, waiting for transfers between devices: 0.06 us -> 2.16 us  [send_core(): return lax.ppermute(v, 'row', CORE_PERM)]
    pallas_call x4, Pallas kernels: 9.37 us -> 7.71 us  [finish(): pl.pallas_call(kernel, in_specs=[VMEM] * (2 + len(late)), out_specs=[VMEM...]
    ppermute x12, starting transfers between devices: 15.5 us -> 16.8 us  [send_first(): return lax.ppermute(v, ('row', 'col'), plane_perm(step, False))]
    ppermute x3, starting transfers between devices: 7 us -> 5.72 us  [send_y(): return lax.ppermute(v, 'row', row_perm(step))]
  transfers between devices with their start and end apart: 28 -> 34, of which waited for: 14 -> 12; matrix products, arithmetic and copies ran while one was open for 0% -> 0% of each run, Pallas kernels for 16% -> 22%
where the time goes in v3:
time: 101 us; the launch traced here: 100 us
  starting transfers between devices  51.2 us (51%)
  Pallas kernels  27.5 us (27%)
  waiting for transfers between devices  21.1 us (21%)
    ppermute x12, starting transfers between devices, send_first(): return lax.ppermute(v, ('row', 'col'), plane_perm(step, False))  16.8 us
    ppermute x10, starting transfers between devices, send_core(): return lax.ppermute(v, 'row', CORE_PERM)  16.6 us
    pallas_call x3, Pallas kernels, accumulate(): pl.pallas_call(kernel, in_specs=[VMEM] * (len(old) + 1 + many), out_specs...  12.2 us
    ppermute x9, starting transfers between devices, send_second(): return lax.ppermute(v, ('row', 'col'), plane_perm(step, True))  12 us
    ppermute x12, waiting for transfers between devices, send_first(): return lax.ppermute(v, ('row', 'col'), plane_perm(step, False))  8.33 us
    pallas_call x4, Pallas kernels, finish(): pl.pallas_call(kernel, in_specs=[VMEM] * (2 + len(late)), out_specs=[VMEM...  7.71 us
    ppermute x9, waiting for transfers between devices, send_second(): return lax.ppermute(v, ('row', 'col'), plane_perm(step, True))  6.1 us
    ppermute x3, starting transfers between devices, send_y(): return lax.ppermute(v, 'row', row_perm(step))  5.72 us
  transfers between devices with their start and end apart: 34, of which 12 were waited for; matrix products, arithmetic and copies ran while one was open for 0% of the time, Pallas kernels for 22%

profile of v3, /device:TPU:1, one launch (start us, length us, event | category | flops | bytes accessed | tf_op | source)
XLA Modules:
  0.0 100.1 jit_solution(9806759448320930995)
XLA Ops:
  1.6 2.5 %collective-permute-start = (bf16[1040,128]{1,0:T(8,128)(2,1)S(1)}, bf16[1040,128]{1,0:T(8,128)(2,1)S(1)}, u32[]{:S(2)}, u32[]{:S(2)}) collective-permute-start(bf16[1040,128]{1,0:T(8,128)(2,1)S(1)} %get-tuple-element.39), channel_id=1, source_target_pairs={{0,4},{1,5},{2,6},{3,7},{4,8},{5,9},{6,10},{7,11},{8,12},{9,13},{1... | collective-permute-start | bytes 798728 | tf_op jit(solution)/shard_map/ppermute | solution.py:46
  4.2 3.3 %collective-permute-start.1 = (bf16[1040,128]{1,0:T(8,128)(2,1)S(1)}, bf16[1040,128]{1,0:T(8,128)(2,1)S(1)}, u32[]{:S(2)}, u32[]{:S(2)}) collective-permute-start(bf16[1040,128]{1,0:T(8,128)(2,1)S(1)} %get-tuple-element.40), channel_id=1, source_target_pairs={{0,8},{1,9},{2,10},{3,11},{4,12},{5,13},{6,14},{7,15},{8,0},{9,1},... | collective-permute-start | bytes 798728 | tf_op jit(solution)/shard_map/ppermute | solution.py:46
  8.2 2.9 %collective-permute-start.12 = (bf16[2064,128]{1,0:T(8,128)(2,1)S(1)}, bf16[2064,128]{1,0:T(8,128)(2,1)S(1)}, u32[]{:S(2)}, u32[]{:S(2)}) collective-permute-start(bf16[2064,128]{1,0:T(8,128)(2,1)S(1)} %get-tuple-element.46), channel_id=1, source_target_pairs={{0,64},{16,80},{32,96},{48,112},{64,0},{80,16},{96,32},{112,48},{1... | collective-permute-start | bytes 1585160 | tf_op jit(solution)/shard_map/ppermute | solution.py:54
  11.1 3.4 %load.1.after.refs_0_.refs_1_.ints_ref = bf16[4096,1024]{1,0:T(8,128)(2,1)S(1)} custom-call(bf16[4096,1024]{1,0:T(8,128)(2,1)} %src.1), custom_call_target="tpu_custom_call" | custom-call | flops 1048576 | bytes 4096 | tf_op jit(solution)/shard_map/load/pallas_call | solution.py:444
  15.9 2.5 %collective-permute-start.4 = (bf16[1040,128]{1,0:T(8,128)(2,1)S(1)}, bf16[1040,128]{1,0:T(8,128)(2,1)S(1)}, u32[]{:S(2)}, u32[]{:S(2)}) collective-permute-start(bf16[1040,128]{1,0:T(8,128)(2,1)S(1)} %get-tuple-element.44), channel_id=1, source_target_pairs={{0,2},{1,3},{2,0},{3,1},{4,6},{5,7},{6,4},{7,5},{8,10},{9,11},{10,... | collective-permute-start | bytes 798728 | tf_op jit(solution)/shard_map/ppermute | solution.py:50
  18.4 2.8 %collective-permute-start.8 = (bf16[1040,128]{1,0:T(8,128)(2,1)S(1)}, bf16[1040,128]{1,0:T(8,128)(2,1)S(1)}, u32[]{:S(2)}, u32[]{:S(2)}) collective-permute-start(bf16[1040,128]{1,0:T(8,128)(2,1)S(1)} %get-tuple-element.42.after_ref), channel_id=1, source_target_pairs={{0,16},{16,0},{32,48},{48,32},{64,80},{80,64},{96,112},{112,96},{1... | collective-permute-start | bytes 798728 | tf_op jit(solution)/shard_map/ppermute | solution.py:58
  27.1 4.8 %collective-permute-start.9 = (bf16[1040,128]{1,0:T(8,128)(2,1)S(1)}, bf16[1040,128]{1,0:T(8,128)(2,1)S(1)}, u32[]{:S(2)}, u32[]{:S(2)}) collective-permute-start(bf16[1040,128]{1,0:T(8,128)(2,1)S(1)} %collective-permute-done.3), channel_id=1, source_target_pairs={{0,16},{16,0},{32,48},{48,32},{64,80},{80,64},{96,112},{112,96},{1... | collective-permute-start | bytes 798728 | tf_op jit(solution)/shard_map/ppermute | solution.py:58
  32.0 2.8 %collective-permute-start.7 = (bf16[4160,128]{1,0:T(8,128)(2,1)S(1)}, bf16[4160,128]{1,0:T(8,128)(2,1)S(1)}, u32[]{:S(2)}, u32[]{:S(2)}) collective-permute-start(bf16[4160,128]{1,0:T(8,128)(2,1)S(1)} %constant_dynamic-update-slice_fusion.refs_1_.after), channel_id=1, source_target_pairs={{0,96},{16,112},{32,0},{48,16},{64,32},{80,48},{96,64},{112,80},{1... | collective-permute-start | bytes 3194888 | tf_op jit(solution)/shard_map/ppermute | solution.py:54
  34.8 2.6 %collective-permute-start.10 = (bf16[1040,128]{1,0:T(8,128)(2,1)S(1)}, bf16[1040,128]{1,0:T(8,128)(2,1)S(1)}, u32[]{:S(2)}, u32[]{:S(2)}) collective-permute-start(bf16[1040,128]{1,0:T(8,128)(2,1)S(1)} %collective-permute-done.4), channel_id=1, source_target_pairs={{0,16},{16,0},{32,48},{48,32},{64,80},{80,64},{96,112},{112,96},{1... | collective-permute-start | bytes 798728 | tf_op jit(solution)/shard_map/ppermute | solution.py:58
  38.5 2.0 %collective-permute-start.17 = (bf16[1040,128]{1,0:T(8,128)(2,1)S(1)}, bf16[1040,128]{1,0:T(8,128)(2,1)S(1)}, u32[]{:S(2)}, u32[]{:S(2)}) collective-permute-start(bf16[1040,128]{1,0:T(8,128)(2,1)S(1)} %get-tuple-element.53), channel_id=1, source_target_pairs={{0,2},{1,3},{2,0},{3,1},{4,6},{5,7},{6,4},{7,5},{8,10},{9,11},{10,... | collective-permute-start | bytes 798728 | tf_op jit(solution)/shard_map/ppermute | solution.py:50
  41.1 4.2 %accumulate.3.after_ref.refs_0_ = f32[2176,1024]{1,0:T(8,128)S(1)} custom-call(bf16[4096,1024]{1,0:T(8,128)(2,1)S(1)} %load.1.after.refs_0_.refs_1_.ints_ref, bf16[4160,128]{1,0:T(8,128)(2,1)S(1)} %constant_dynamic-update-slice_fusion.refs_1_.after, bf16[1040,128]{1,0:T(8,128)(2,1)S(1)} %collective-permute-done.8.refs_2_, ...), custom_call_target="tpu_custom_call" | custom-call | flops 1048576 | bytes 4096 | tf_op jit(solution)/shard_map/accumulate/pallas_call | solution.py:326
  45.4 3.2 %collective-permute-start.19 = (bf16[1040,128]{1,0:T(8,128)(2,1)S(1)}, bf16[1040,128]{1,0:T(8,128)(2,1)S(1)}, u32[]{:S(2)}, u32[]{:S(2)}) collective-permute-start(bf16[1040,128]{1,0:T(8,128)(2,1)S(1)} %join.1), channel_id=1, source_target_pairs={{0,16},{16,0},{32,48},{48,32},{64,80},{80,64},{96,112},{112,96},{1... | collective-permute-start | bytes 798728 | tf_op jit(solution)/shard_map/ppermute | solution.py:58
  51.2 4.2 %accumulate.4.refs_0_ = f32[2176,1024]{1,0:T(8,128)S(1)} custom-call(f32[2176,1024]{1,0:T(8,128)S(1)} %accumulate.3.after_ref.refs_0_, bf16[4096,1024]{1,0:T(8,128)(2,1)S(1)} %load.1.after.refs_0_.refs_1_.ints_ref, bf16[1040,128]{1,0:T(8,128)(2,1)S(1)} %get-tuple-element.51.refs_0_.refs_2_, ...), custom_call_target="tpu_custom_call", output_to_operand_aliasing={{}: (0, {})} | custom-call | flops 1048576 | bytes 4096 | tf_op jit(solution)/shard_map/accumulate/pallas_call | solution.py:326
  55.5 2.2 %collective-permute-done.7.refs_3_ = bf16[4160,128]{1,0:T(8,128)(2,1)S(1)} collective-permute-done((bf16[4160,128]{1,0:T(8,128)(2,1)S(1)}, bf16[4160,128]{1,0:T(8,128)(2,1)S(1)}, u32[]{:S(2)}, u32[]{:S(2)}) %collective-permute-start.7) | collective-permute-done | bytes 1064992 | tf_op jit(solution)/shard_map/ppermute | solution.py:54
  57.7 2.3 %collective-permute-done.6.refs_2_ = bf16[4160,128]{1,0:T(8,128)(2,1)S(1)} collective-permute-done((bf16[4160,128]{1,0:T(8,128)(2,1)S(1)}, bf16[4160,128]{1,0:T(8,128)(2,1)S(1)}, u32[]{:S(2)}, u32[]{:S(2)}) %collective-permute-start.6) | collective-permute-done | bytes 1064992 | tf_op jit(solution)/shard_map/ppermute | solution.py:54
  61.9 3.8 %accumulate.5.total_in = f32[2176,1024]{1,0:T(8,128)S(1)} custom-call(f32[2176,1024]{1,0:T(8,128)S(1)} %accumulate.4.refs_0_, bf16[4096,1024]{1,0:T(8,128)(2,1)S(1)} %load.1.after.refs_0_.refs_1_.ints_ref, bf16[4160,128]{1,0:T(8,128)(2,1)S(1)} %collective-permute-done.6.refs_2_, ...), custom_call_target="tpu_custom_call", output_to_operand_aliasing={{}: (0, {})} | custom-call | flops 1048576 | bytes 4096 | tf_op jit(solution)/shard_map/accumulate/pallas_call | solution.py:326
  65.7 2.5 %finish.4 = (f32[2176,1024]{1,0:T(8,128)S(1)}, bf16[256,1024]{1,0:T(8,128)(2,1)S(1)}, bf16[256,1024]{1,0:T(8,128)(2,1)S(1)}, bf16[10496,128]{1,0:T(8,128)(2,1)S(1)}, s32[32,128]{1,0:T(8,128)S(1)}) custom-call(f32[2176,1024]{1,0:T(8,128)S(1)} %accumulate.5.total_in, ...), custom_call_target="tpu_custom_call", output_to_operand_aliasing={{0}: (0, {})} | custom-call | flops 2147483648 | bytes 4096 | tf_op jit(solution)/shard_map/finish/pallas_call | solution.py:359
  68.3 2.7 %collective-permute-start.27 = (bf16[256,1024]{1,0:T(8,128)(2,1)S(1)}, bf16[256,1024]{1,0:T(8,128)(2,1)S(1)}, u32[]{:S(2)}, u32[]{:S(2)}) collective-permute-start(bf16[256,1024]{1,0:T(8,128)(2,1)S(1)} %get-tuple-element.64), channel_id=1, source_target_pairs={{0,12},{1,13},{2,14},{3,15},{4,0},{5,1},{6,2},{7,3},{8,4},{9,5},{1... | collective-permute-start | bytes 1572872 | tf_op jit(solution)/shard_map/ppermute | solution.py:46
  71.0 2.0 %finish.5 = (f32[2176,1024]{1,0:T(8,128)S(1)}, bf16[256,1024]{1,0:T(8,128)(2,1)S(1)}, bf16[256,1024]{1,0:T(8,128)(2,1)S(1)}) custom-call(f32[2176,1024]{1,0:T(8,128)S(1)} %get-tuple-element.58.total_in, bf16[4096,1024]{1,0:T(8,128)(2,1)S(1)} %load.1.after.refs_0_.refs_1_.ints_ref, ...), custom_call_target="tpu_custom_call", output_to_operand_aliasing={{0}: (0, {})} | custom-call | flops 2147483648 | bytes 4096 | tf_op jit(solution)/shard_map/finish/pallas_call | solution.py:359
  78.1 2.7 %collective-permute-start.30 = (bf16[256,1024]{1,0:T(8,128)(2,1)S(1)}, bf16[256,1024]{1,0:T(8,128)(2,1)S(1)}, u32[]{:S(2)}, u32[]{:S(2)}) collective-permute-start(bf16[256,1024]{1,0:T(8,128)(2,1)S(1)} %get-tuple-element.67), channel_id=1, source_target_pairs={{0,12},{1,13},{2,14},{3,15},{4,0},{5,1},{6,2},{7,3},{8,4},{9,5},{1... | collective-permute-start | bytes 1572872 | tf_op jit(solution)/shard_map/ppermute | solution.py:46
  83.5 5.6 %collective-permute-done.28.refs_2_.refs_1_ = bf16[256,1024]{1,0:T(8,128)(2,1)S(1)} collective-permute-done((bf16[256,1024]{1,0:T(8,128)(2,1)S(1)}, bf16[256,1024]{1,0:T(8,128)(2,1)S(1)}, u32[]{:S(2)}, u32[]{:S(2)}) %collective-permute-start.28) | collective-permute-done | bytes 524320 | tf_op jit(solution)/shard_map/ppermute | solution.py:46
  90.8 2.4 %collective-permute-start.33 = (bf16[128,1024]{1,0:T(8,128)(2,1)S(1)}, bf16[128,1024]{1,0:T(8,128)(2,1)S(1)}, u32[]{:S(2)}, u32[]{:S(2)}) collective-permute-start(bf16[128,1024]{1,0:T(8,128)(2,1)S(1)} %get-tuple-element.70), channel_id=1, source_target_pairs={{0,3},{1,0},{2,1},{3,2},{4,7},{5,4},{6,5},{7,6},{8,11},{9,8},{10,9... | collective-permute-start | bytes 786440 | tf_op jit(solution)/shard_map/ppermute | solution.py:50
  93.2 3.3 %collective-permute-done.31.refs_2_ = bf16[128,1024]{1,0:T(8,128)(2,1)S(1)} collective-permute-done((bf16[128,1024]{1,0:T(8,128)(2,1)S(1)}, bf16[128,1024]{1,0:T(8,128)(2,1)S(1)}, u32[]{:S(2)}, u32[]{:S(2)}) %collective-permute-start.31) | collective-permute-done | bytes 262176 | tf_op jit(solution)/shard_map/ppermute | solution.py:50
  96.5 2.8 %collective-permute-done.32.refs_3_ = bf16[128,1024]{1,0:T(8,128)(2,1)S(1)} collective-permute-done((bf16[128,1024]{1,0:T(8,128)(2,1)S(1)}, bf16[128,1024]{1,0:T(8,128)(2,1)S(1)}, u32[]{:S(2)}, u32[]{:S(2)}) %collective-permute-start.32) | collective-permute-done | bytes 262176 | tf_op jit(solution)/shard_map/ppermute | solution.py:50
  (64 shorter events, 26.5 us)
Async XLA Ops:
  1.6 12.9 %collective-permute-start = (bf16[1040,128]{1,0:T(8,128)(2,1)S(1)}, bf16[1040,128]{1,0:T(8,128)(2,1)S(1)}, u32[]{:S(2)}, u32[]{:S(2)}) collective-permute-start(bf16[1040,128]{1,0:T(8,128)(2,1)S(1)} %get-tuple-element.39), channel_id=1, source_target_pairs={{0,4},{1,5},{2,6},{3,7},{4,8},{5,9},{6,10},{7,11},{8,12},{9,13},{1... | collective-permute-start | bytes 798728 | tf_op jit(solution)/shard_map/ppermute | solution.py:46
  4.2 10.4 %collective-permute-start.1 = (bf16[1040,128]{1,0:T(8,128)(2,1)S(1)}, bf16[1040,128]{1,0:T(8,128)(2,1)S(1)}, u32[]{:S(2)}, u32[]{:S(2)}) collective-permute-start(bf16[1040,128]{1,0:T(8,128)(2,1)S(1)} %get-tuple-element.40), channel_id=1, source_target_pairs={{0,8},{1,9},{2,10},{3,11},{4,12},{5,13},{6,14},{7,15},{8,0},{9,1},... | collective-permute-start | bytes 798728 | tf_op jit(solution)/shard_map/ppermute | solution.py:46
  8.2 14.5 %collective-permute-start.12 = (bf16[2064,128]{1,0:T(8,128)(2,1)S(1)}, bf16[2064,128]{1,0:T(8,128)(2,1)S(1)}, u32[]{:S(2)}, u32[]{:S(2)}) collective-permute-start(bf16[2064,128]{1,0:T(8,128)(2,1)S(1)} %get-tuple-element.46), channel_id=1, source_target_pairs={{0,64},{16,80},{32,96},{48,112},{64,0},{80,16},{96,32},{112,48},{1... | collective-permute-start | bytes 1585160 | tf_op jit(solution)/shard_map/ppermute | solution.py:54
  14.6 9.2 %collective-permute-start.3 = (bf16[1040,128]{1,0:T(8,128)(2,1)S(1)}, bf16[1040,128]{1,0:T(8,128)(2,1)S(1)}, u32[]{:S(2)}, u32[]{:S(2)}) collective-permute-start(bf16[1040,128]{1,0:T(8,128)(2,1)S(1)} %get-tuple-element.43), channel_id=1, source_target_pairs={{0,1},{1,2},{2,3},{3,0},{4,5},{5,6},{6,7},{7,4},{8,9},{9,10},{10,1... | collective-permute-start | bytes 798728 | tf_op jit(solution)/shard_map/ppermute | solution.py:50
  15.9 9.9 %collective-permute-start.4 = (bf16[1040,128]{1,0:T(8,128)(2,1)S(1)}, bf16[1040,128]{1,0:T(8,128)(2,1)S(1)}, u32[]{:S(2)}, u32[]{:S(2)}) collective-permute-start(bf16[1040,128]{1,0:T(8,128)(2,1)S(1)} %get-tuple-element.44), channel_id=1, source_target_pairs={{0,2},{1,3},{2,0},{3,1},{4,6},{5,7},{6,4},{7,5},{8,10},{9,11},{10,... | collective-permute-start | bytes 798728 | tf_op jit(solution)/shard_map/ppermute | solution.py:50
  18.4 13.6 %collective-permute-start.8 = (bf16[1040,128]{1,0:T(8,128)(2,1)S(1)}, bf16[1040,128]{1,0:T(8,128)(2,1)S(1)}, u32[]{:S(2)}, u32[]{:S(2)}) collective-permute-start(bf16[1040,128]{1,0:T(8,128)(2,1)S(1)} %get-tuple-element.42.after_ref), channel_id=1, source_target_pairs={{0,16},{16,0},{32,48},{48,32},{64,80},{80,64},{96,112},{112,96},{1... | collective-permute-start | bytes 798728 | tf_op jit(solution)/shard_map/ppermute | solution.py:58
  23.8 11.0 %collective-permute-start.13 = (bf16[1040,128]{1,0:T(8,128)(2,1)S(1)}, bf16[1040,128]{1,0:T(8,128)(2,1)S(1)}, u32[]{:S(2)}, u32[]{:S(2)}) collective-permute-start(bf16[1040,128]{1,0:T(8,128)(2,1)S(1)} %get-tuple-element.48), channel_id=1, source_target_pairs={{0,4},{1,5},{2,6},{3,7},{4,8},{5,9},{6,10},{7,11},{8,12},{9,13},{1... | collective-permute-start | bytes 798728 | tf_op jit(solution)/shard_map/ppermute | solution.py:46
  23.9 10.9 %collective-permute-start.14 = (bf16[1040,128]{1,0:T(8,128)(2,1)S(1)}, bf16[1040,128]{1,0:T(8,128)(2,1)S(1)}, u32[]{:S(2)}, u32[]{:S(2)}) collective-permute-start(bf16[1040,128]{1,0:T(8,128)(2,1)S(1)} %get-tuple-element.49), channel_id=1, source_target_pairs={{0,8},{1,9},{2,10},{3,11},{4,12},{5,13},{6,14},{7,15},{8,0},{9,1},... | collective-permute-start | bytes 798728 | tf_op jit(solution)/shard_map/ppermute | solution.py:46
  25.8 11.5 %collective-permute-start.15 = (bf16[1040,128]{1,0:T(8,128)(2,1)S(1)}, bf16[1040,128]{1,0:T(8,128)(2,1)S(1)}, u32[]{:S(2)}, u32[]{:S(2)}) collective-permute-start(bf16[1040,128]{1,0:T(8,128)(2,1)S(1)} %get-tuple-element.50), channel_id=1, source_target_pairs={{0,12},{1,13},{2,14},{3,15},{4,0},{5,1},{6,2},{7,3},{8,4},{9,5},{1... | collective-permute-start | bytes 798728 | tf_op jit(solution)/shard_map/ppermute | solution.py:46
  27.1 10.5 %collective-permute-start.9 = (bf16[1040,128]{1,0:T(8,128)(2,1)S(1)}, bf16[1040,128]{1,0:T(8,128)(2,1)S(1)}, u32[]{:S(2)}, u32[]{:S(2)}) collective-permute-start(bf16[1040,128]{1,0:T(8,128)(2,1)S(1)} %collective-permute-done.3), channel_id=1, source_target_pairs={{0,16},{16,0},{32,48},{48,32},{64,80},{80,64},{96,112},{112,96},{1... | collective-permute-start | bytes 798728 | tf_op jit(solution)/shard_map/ppermute | solution.py:58
  32.0 25.7 %collective-permute-start.7 = (bf16[4160,128]{1,0:T(8,128)(2,1)S(1)}, bf16[4160,128]{1,0:T(8,128)(2,1)S(1)}, u32[]{:S(2)}, u32[]{:S(2)}) collective-permute-start(bf16[4160,128]{1,0:T(8,128)(2,1)S(1)} %constant_dynamic-update-slice_fusion.refs_1_.after), channel_id=1, source_target_pairs={{0,96},{16,112},{32,0},{48,16},{64,32},{80,48},{96,64},{112,80},{1... | collective-permute-start | bytes 3194888 | tf_op jit(solution)/shard_map/ppermute | solution.py:54
  34.8 25.2 %collective-permute-start.6 = (bf16[4160,128]{1,0:T(8,128)(2,1)S(1)}, bf16[4160,128]{1,0:T(8,128)(2,1)S(1)}, u32[]{:S(2)}, u32[]{:S(2)}) collective-permute-start(bf16[4160,128]{1,0:T(8,128)(2,1)S(1)} %constant_dynamic-update-slice_fusion.refs_1_.after), channel_id=1, source_target_pairs={{0,32},{16,48},{32,64},{48,80},{64,96},{80,112},{96,0},{112,16},{1... | collective-permute-start | bytes 3194888 | tf_op jit(solution)/shard_map/ppermute | solution.py:54
  37.5 7.8 %collective-permute-start.16 = (bf16[1040,128]{1,0:T(8,128)(2,1)S(1)}, bf16[1040,128]{1,0:T(8,128)(2,1)S(1)}, u32[]{:S(2)}, u32[]{:S(2)}) collective-permute-start(bf16[1040,128]{1,0:T(8,128)(2,1)S(1)} %get-tuple-element.52), channel_id=1, source_target_pairs={{0,1},{1,2},{2,3},{3,0},{4,5},{5,6},{6,7},{7,4},{8,9},{9,10},{10,1... | collective-permute-start | bytes 798728 | tf_op jit(solution)/shard_map/ppermute | solution.py:50
  38.5 10.0 %collective-permute-start.17 = (bf16[1040,128]{1,0:T(8,128)(2,1)S(1)}, bf16[1040,128]{1,0:T(8,128)(2,1)S(1)}, u32[]{:S(2)}, u32[]{:S(2)}) collective-permute-start(bf16[1040,128]{1,0:T(8,128)(2,1)S(1)} %get-tuple-element.53), channel_id=1, source_target_pairs={{0,2},{1,3},{2,0},{3,1},{4,6},{5,7},{6,4},{7,5},{8,10},{9,11},{10,... | collective-permute-start | bytes 798728 | tf_op jit(solution)/shard_map/ppermute | solution.py:50
  40.5 8.0 %collective-permute-start.18 = (bf16[1040,128]{1,0:T(8,128)(2,1)S(1)}, bf16[1040,128]{1,0:T(8,128)(2,1)S(1)}, u32[]{:S(2)}, u32[]{:S(2)}) collective-permute-start(bf16[1040,128]{1,0:T(8,128)(2,1)S(1)} %get-tuple-element.54), channel_id=1, source_target_pairs={{0,3},{1,0},{2,1},{3,2},{4,7},{5,4},{6,5},{7,6},{8,11},{9,8},{10,9... | collective-permute-start | bytes 798728 | tf_op jit(solution)/shard_map/ppermute | solution.py:50
  68.2 9.6 %collective-permute-start.26 = (bf16[256,1024]{1,0:T(8,128)(2,1)S(1)}, bf16[256,1024]{1,0:T(8,128)(2,1)S(1)}, u32[]{:S(2)}, u32[]{:S(2)}) collective-permute-start(bf16[256,1024]{1,0:T(8,128)(2,1)S(1)} %get-tuple-element.63), channel_id=1, source_target_pairs={{0,4},{1,5},{2,6},{3,7},{4,8},{5,9},{6,10},{7,11},{8,12},{9,13},{1... | collective-permute-start | bytes 1572872 | tf_op jit(solution)/shard_map/ppermute | solution.py:46
  68.3 9.5 %collective-permute-start.27 = (bf16[256,1024]{1,0:T(8,128)(2,1)S(1)}, bf16[256,1024]{1,0:T(8,128)(2,1)S(1)}, u32[]{:S(2)}, u32[]{:S(2)}) collective-permute-start(bf16[256,1024]{1,0:T(8,128)(2,1)S(1)} %get-tuple-element.64), channel_id=1, source_target_pairs={{0,12},{1,13},{2,14},{3,15},{4,0},{5,1},{6,2},{7,3},{8,4},{9,5},{1... | collective-permute-start | bytes 1572872 | tf_op jit(solution)/shard_map/ppermute | solution.py:46
  73.0 9.8 %collective-permute-start.25 = (bf16[256,1024]{1,0:T(8,128)(2,1)S(1)}, bf16[256,1024]{1,0:T(8,128)(2,1)S(1)}, u32[]{:S(2)}, u32[]{:S(2)}) collective-permute-start(bf16[256,1024]{1,0:T(8,128)(2,1)S(1)} %get-tuple-element.62), channel_id=1, source_target_pairs={{0,12},{1,13},{2,14},{3,15},{4,0},{5,1},{6,2},{7,3},{8,4},{9,5},{1... | collective-permute-start | bytes 1572872 | tf_op jit(solution)/shard_map/ppermute | solution.py:46
  73.3 10.1 %collective-permute-start.29 = (bf16[256,1024]{1,0:T(8,128)(2,1)S(1)}, bf16[256,1024]{1,0:T(8,128)(2,1)S(1)}, u32[]{:S(2)}, u32[]{:S(2)}) collective-permute-start(bf16[256,1024]{1,0:T(8,128)(2,1)S(1)} %get-tuple-element.66), channel_id=1, source_target_pairs={{0,4},{1,5},{2,6},{3,7},{4,8},{5,9},{6,10},{7,11},{8,12},{9,13},{1... | collective-permute-start | bytes 1572872 | tf_op jit(solution)/shard_map/ppermute | solution.py:46
  78.0 11.1 %collective-permute-start.28 = (bf16[256,1024]{1,0:T(8,128)(2,1)S(1)}, bf16[256,1024]{1,0:T(8,128)(2,1)S(1)}, u32[]{:S(2)}, u32[]{:S(2)}) collective-permute-start(bf16[256,1024]{1,0:T(8,128)(2,1)S(1)} %get-tuple-element.65), channel_id=1, source_target_pairs={{0,4},{1,5},{2,6},{3,7},{4,8},{5,9},{6,10},{7,11},{8,12},{9,13},{1... | collective-permute-start | bytes 1572872 | tf_op jit(solution)/shard_map/ppermute | solution.py:46
  78.1 11.0 %collective-permute-start.30 = (bf16[256,1024]{1,0:T(8,128)(2,1)S(1)}, bf16[256,1024]{1,0:T(8,128)(2,1)S(1)}, u32[]{:S(2)}, u32[]{:S(2)}) collective-permute-start(bf16[256,1024]{1,0:T(8,128)(2,1)S(1)} %get-tuple-element.67), channel_id=1, source_target_pairs={{0,12},{1,13},{2,14},{3,15},{4,0},{5,1},{6,2},{7,3},{8,4},{9,5},{1... | collective-permute-start | bytes 1572872 | tf_op jit(solution)/shard_map/ppermute | solution.py:46
  89.3 7.1 %collective-permute-start.31 = (bf16[128,1024]{1,0:T(8,128)(2,1)S(1)}, bf16[128,1024]{1,0:T(8,128)(2,1)S(1)}, u32[]{:S(2)}, u32[]{:S(2)}) collective-permute-start(bf16[128,1024]{1,0:T(8,128)(2,1)S(1)} %get-tuple-element.68), channel_id=1, source_target_pairs={{0,2},{1,3},{2,0},{3,1},{4,6},{5,7},{6,4},{7,5},{8,10},{9,11},{10,... | collective-permute-start | bytes 786440 | tf_op jit(solution)/shard_map/ppermute | solution.py:50
  90.5 8.8 %collective-permute-start.32 = (bf16[128,1024]{1,0:T(8,128)(2,1)S(1)}, bf16[128,1024]{1,0:T(8,128)(2,1)S(1)}, u32[]{:S(2)}, u32[]{:S(2)}) collective-permute-start(bf16[128,1024]{1,0:T(8,128)(2,1)S(1)} %get-tuple-element.69), channel_id=1, source_target_pairs={{0,1},{1,2},{2,3},{3,0},{4,5},{5,6},{6,7},{7,4},{8,9},{9,10},{10,1... | collective-permute-start | bytes 786440 | tf_op jit(solution)/shard_map/ppermute | solution.py:50
  90.8 8.5 %collective-permute-start.33 = (bf16[128,1024]{1,0:T(8,128)(2,1)S(1)}, bf16[128,1024]{1,0:T(8,128)(2,1)S(1)}, u32[]{:S(2)}, u32[]{:S(2)}) collective-permute-start(bf16[128,1024]{1,0:T(8,128)(2,1)S(1)} %get-tuple-element.70), channel_id=1, source_target_pairs={{0,3},{1,0},{2,1},{3,2},{4,7},{5,4},{6,5},{7,6},{8,11},{9,8},{10,9... | collective-permute-start | bytes 786440 | tf_op jit(solution)/shard_map/ppermute | solution.py:50
  (10 other events, 38.8 us)

commit v4 on v3

--- a/solution.py
+++ b/solution.py
@@ -13,6 +13,7 @@
 MSG = SLOTS * SIDE + HEAD
 PIECE = RING * MSG
 OCC = RING * RING
+STEPS = (0, 2, 1, 3)
 DUMMY = OCC
 UNROLL = 4
 INFO = 32
@@ -192,7 +193,7 @@
 
 
 def turn_kernel(after, *refs):
-    ins, outs = refs[:RING], refs[RING:]
+    ins, outs = [refs[STEPS.index(d)] for d in range(RING)], refs[RING:]
     lanes = lax.broadcasted_iota(I32, (HEAD, SIDE), 1)
     heads = [r[SLOTS * SIDE :, :].astype(F32) for r in ins]
     for db in range(RING):
@@ -392,11 +393,11 @@
 
 
 def first_steps(parts):
-    return [parts[0]] + [send_first(parts[d], d) for d in (1, 2, 3)]
+    return [send_first(parts[d], d) if d else parts[d] for d in STEPS]
 
 
 def second_steps(parts):
-    return [parts[0]] + [send_second(parts[d], d) for d in (1, 2, 3)]
+    return [send_second(parts[d], d) if d else parts[d] for d in STEPS]
 
 
 def join(parts, after):

time: 101 us -> 100 us (0.990)
  starting transfers between devices: 51.2 us -> 47.9 us
  waiting for transfers between devices: 21.1 us -> 24.4 us
  Pallas kernels: 27.5 us -> 26.1 us
    ppermute x10, starting transfers between devices: 16.6 us -> 13.7 us  [send_core(): return lax.ppermute(v, 'row', CORE_PERM)]
    ppermute x12, waiting for transfers between devices: 8.33 us -> 10.7 us  [send_first(): return lax.ppermute(v, ('row', 'col'), plane_perm(step, False))]
    ppermute x9, starting transfers between devices: 12 us -> 10.6 us  [send_second(): return lax.ppermute(v, ('row', 'col'), plane_perm(step, True))]
  transfers between devices with their start and end apart: 34 -> 34, of which waited for: 12 -> 19; matrix products, arithmetic and copies ran while one was open for 0% -> 0% of each run, Pallas kernels for 22% -> 21%
where the time goes in v4:
time: 100 us; the launch traced here: 98.7 us
  starting transfers between devices  47.9 us (48%)
  Pallas kernels  26.1 us (26%)
  waiting for transfers between devices  24.4 us (24%)
    ppermute x12, starting transfers between devices, send_first(): return lax.ppermute(v, ('row', 'col'), plane_perm(step, False))  17.4 us
    ppermute x10, starting transfers between devices, send_core(): return lax.ppermute(v, 'row', CORE_PERM)  13.7 us
    pallas_call x3, Pallas kernels, accumulate(): pl.pallas_call(kernel, in_specs=[VMEM] * (len(old) + 1 + many), out_specs...  11.7 us
    ppermute x12, waiting for transfers between devices, send_first(): return lax.ppermute(v, ('row', 'col'), plane_perm(step, False))  10.7 us
    ppermute x9, starting transfers between devices, send_second(): return lax.ppermute(v, ('row', 'col'), plane_perm(step, True))  10.6 us
    pallas_call x4, Pallas kernels, finish(): pl.pallas_call(kernel, in_specs=[VMEM] * (2 + len(late)), out_specs=[VMEM...  6.8 us
    ppermute x9, waiting for transfers between devices, send_second(): return lax.ppermute(v, ('row', 'col'), plane_perm(step, True))  6.46 us
    ppermute x3, starting transfers between devices, send_y(): return lax.ppermute(v, 'row', row_perm(step))  6.18 us
  transfers between devices with their start and end apart: 34, of which 19 were waited for; matrix products, arithmetic and copies ran while one was open for 0% of the time, Pallas kernels for 21%

profile of v4, /device:TPU:1, one launch (start us, length us, event | category | flops | bytes accessed | tf_op | source)
XLA Modules:
  0.0 98.7 jit_solution(604672474984073836)
XLA Ops:
  1.6 4.5 %collective-permute-start = (bf16[1040,128]{1,0:T(8,128)(2,1)S(1)}, bf16[1040,128]{1,0:T(8,128)(2,1)S(1)}, u32[]{:S(2)}, u32[]{:S(2)}) collective-permute-start(bf16[1040,128]{1,0:T(8,128)(2,1)S(1)} %get-tuple-element.39), channel_id=1, source_target_pairs={{0,8},{1,9},{2,10},{3,11},{4,12},{5,13},{6,14},{7,15},{8,0},{9,1},... | collective-permute-start | bytes 798728 | tf_op jit(solution)/shard_map/ppermute | solution.py:47
  6.9 1.9 %collective-permute-start.2 = (bf16[1040,128]{1,0:T(8,128)(2,1)S(1)}, bf16[1040,128]{1,0:T(8,128)(2,1)S(1)}, u32[]{:S(2)}, u32[]{:S(2)}) collective-permute-start(bf16[1040,128]{1,0:T(8,128)(2,1)S(1)} %get-tuple-element.41), channel_id=1, source_target_pairs={{0,12},{1,13},{2,14},{3,15},{4,0},{5,1},{6,2},{7,3},{8,4},{9,5},{1... | collective-permute-start | bytes 798728 | tf_op jit(solution)/shard_map/ppermute | solution.py:47
  8.8 2.9 %collective-permute-start.12 = (bf16[2064,128]{1,0:T(8,128)(2,1)S(1)}, bf16[2064,128]{1,0:T(8,128)(2,1)S(1)}, u32[]{:S(2)}, u32[]{:S(2)}) collective-permute-start(bf16[2064,128]{1,0:T(8,128)(2,1)S(1)} %get-tuple-element.46), channel_id=1, source_target_pairs={{0,64},{16,80},{32,96},{48,112},{64,0},{80,16},{96,32},{112,48},{1... | collective-permute-start | bytes 1585160 | tf_op jit(solution)/shard_map/ppermute | solution.py:55
  11.7 3.4 %load.1.after.refs_0_.refs_1_.ints_ref = bf16[4096,1024]{1,0:T(8,128)(2,1)S(1)} custom-call(bf16[4096,1024]{1,0:T(8,128)(2,1)} %src.1), custom_call_target="tpu_custom_call" | custom-call | flops 1048576 | bytes 4096 | tf_op jit(solution)/shard_map/load/pallas_call | solution.py:445
  15.3 2.8 %collective-permute-start.3 = (bf16[1040,128]{1,0:T(8,128)(2,1)S(1)}, bf16[1040,128]{1,0:T(8,128)(2,1)S(1)}, u32[]{:S(2)}, u32[]{:S(2)}) collective-permute-start(bf16[1040,128]{1,0:T(8,128)(2,1)S(1)} %get-tuple-element.43), channel_id=1, source_target_pairs={{0,2},{1,3},{2,0},{3,1},{4,6},{5,7},{6,4},{7,5},{8,10},{9,11},{10,... | collective-permute-start | bytes 798728 | tf_op jit(solution)/shard_map/ppermute | solution.py:51
  18.4 2.8 %collective-permute-start.8 = (bf16[1040,128]{1,0:T(8,128)(2,1)S(1)}, bf16[1040,128]{1,0:T(8,128)(2,1)S(1)}, u32[]{:S(2)}, u32[]{:S(2)}) collective-permute-start(bf16[1040,128]{1,0:T(8,128)(2,1)S(1)} %get-tuple-element.42.after_ref), channel_id=1, source_target_pairs={{0,16},{16,0},{32,48},{48,32},{64,80},{80,64},{96,112},{112,96},{1... | collective-permute-start | bytes 798728 | tf_op jit(solution)/shard_map/ppermute | solution.py:59
  27.3 2.2 %collective-permute-start.9 = (bf16[1040,128]{1,0:T(8,128)(2,1)S(1)}, bf16[1040,128]{1,0:T(8,128)(2,1)S(1)}, u32[]{:S(2)}, u32[]{:S(2)}) collective-permute-start(bf16[1040,128]{1,0:T(8,128)(2,1)S(1)} %collective-permute-done.3), channel_id=1, source_target_pairs={{0,16},{16,0},{32,48},{48,32},{64,80},{80,64},{96,112},{112,96},{1... | collective-permute-start | bytes 798728 | tf_op jit(solution)/shard_map/ppermute | solution.py:59
  29.6 2.8 %collective-permute-start.7 = (bf16[4160,128]{1,0:T(8,128)(2,1)S(1)}, bf16[4160,128]{1,0:T(8,128)(2,1)S(1)}, u32[]{:S(2)}, u32[]{:S(2)}) collective-permute-start(bf16[4160,128]{1,0:T(8,128)(2,1)S(1)} %constant_dynamic-update-slice_fusion.refs_1_.after), channel_id=1, source_target_pairs={{0,96},{16,112},{32,0},{48,16},{64,32},{80,48},{96,64},{112,80},{1... | collective-permute-start | bytes 3194888 | tf_op jit(solution)/shard_map/ppermute | solution.py:55
  34.1 2.4 %collective-permute-start.10 = (bf16[1040,128]{1,0:T(8,128)(2,1)S(1)}, bf16[1040,128]{1,0:T(8,128)(2,1)S(1)}, u32[]{:S(2)}, u32[]{:S(2)}) collective-permute-start(bf16[1040,128]{1,0:T(8,128)(2,1)S(1)} %collective-permute-done.4), channel_id=1, source_target_pairs={{0,16},{16,0},{32,48},{48,32},{64,80},{80,64},{96,112},{112,96},{1... | collective-permute-start | bytes 798728 | tf_op jit(solution)/shard_map/ppermute | solution.py:59
  38.0 2.3 %collective-permute-start.18 = (bf16[1040,128]{1,0:T(8,128)(2,1)S(1)}, bf16[1040,128]{1,0:T(8,128)(2,1)S(1)}, u32[]{:S(2)}, u32[]{:S(2)}) collective-permute-start(bf16[1040,128]{1,0:T(8,128)(2,1)S(1)} %get-tuple-element.54), channel_id=1, source_target_pairs={{0,3},{1,0},{2,1},{3,2},{4,7},{5,4},{6,5},{7,6},{8,11},{9,8},{10,9... | collective-permute-start | bytes 798728 | tf_op jit(solution)/shard_map/ppermute | solution.py:51
  40.3 4.2 %accumulate.3.after_ref.refs_0_ = f32[2176,1024]{1,0:T(8,128)S(1)} custom-call(bf16[4096,1024]{1,0:T(8,128)(2,1)S(1)} %load.1.after.refs_0_.refs_1_.ints_ref, bf16[4160,128]{1,0:T(8,128)(2,1)S(1)} %constant_dynamic-update-slice_fusion.refs_1_.after, bf16[1040,128]{1,0:T(8,128)(2,1)S(1)} %collective-permute-done.8.refs_2_, ...), custom_call_target="tpu_custom_call" | custom-call | flops 1048576 | bytes 4096 | tf_op jit(solution)/shard_map/accumulate/pallas_call | solution.py:327
  44.6 2.0 %collective-permute-start.19 = (bf16[1040,128]{1,0:T(8,128)(2,1)S(1)}, bf16[1040,128]{1,0:T(8,128)(2,1)S(1)}, u32[]{:S(2)}, u32[]{:S(2)}) collective-permute-start(bf16[1040,128]{1,0:T(8,128)(2,1)S(1)} %join.1), channel_id=1, source_target_pairs={{0,16},{16,0},{32,48},{48,32},{64,80},{80,64},{96,112},{112,96},{1... | collective-permute-start | bytes 798728 | tf_op jit(solution)/shard_map/ppermute | solution.py:59
  49.9 3.8 %accumulate.4.refs_0_ = f32[2176,1024]{1,0:T(8,128)S(1)} custom-call(f32[2176,1024]{1,0:T(8,128)S(1)} %accumulate.3.after_ref.refs_0_, bf16[4096,1024]{1,0:T(8,128)(2,1)S(1)} %load.1.after.refs_0_.refs_1_.ints_ref, bf16[1040,128]{1,0:T(8,128)(2,1)S(1)} %get-tuple-element.51.refs_0_.refs_2_, ...), custom_call_target="tpu_custom_call", output_to_operand_aliasing={{}: (0, {})} | custom-call | flops 1048576 | bytes 4096 | tf_op jit(solution)/shard_map/accumulate/pallas_call | solution.py:327
  55.3 1.7 %collective-permute-done.6.refs_2_ = bf16[4160,128]{1,0:T(8,128)(2,1)S(1)} collective-permute-done((bf16[4160,128]{1,0:T(8,128)(2,1)S(1)}, bf16[4160,128]{1,0:T(8,128)(2,1)S(1)}, u32[]{:S(2)}, u32[]{:S(2)}) %collective-permute-start.6) | collective-permute-done | bytes 1064992 | tf_op jit(solution)/shard_map/ppermute | solution.py:55
  57.0 2.5 %collective-permute-start.23 = (bf16[4160,128]{1,0:T(8,128)(2,1)S(1)}, bf16[4160,128]{1,0:T(8,128)(2,1)S(1)}, u32[]{:S(2)}, u32[]{:S(2)}) collective-permute-start(bf16[4160,128]{1,0:T(8,128)(2,1)S(1)} %collective-permute-done.6.refs_2_), channel_id=1, source_target_pairs={{0,16},{16,0},{32,48},{48,32},{64,80},{80,64},{96,112},{112,96},{1... | collective-permute-start | bytes 3194888 | tf_op jit(solution)/shard_map/ppermute | solution.py:59
  59.5 3.8 %accumulate.5.total_in = f32[2176,1024]{1,0:T(8,128)S(1)} custom-call(f32[2176,1024]{1,0:T(8,128)S(1)} %accumulate.4.refs_0_, bf16[4096,1024]{1,0:T(8,128)(2,1)S(1)} %load.1.after.refs_0_.refs_1_.ints_ref, bf16[4160,128]{1,0:T(8,128)(2,1)S(1)} %collective-permute-done.6.refs_2_, ...), custom_call_target="tpu_custom_call", output_to_operand_aliasing={{}: (0, {})} | custom-call | flops 1048576 | bytes 4096 | tf_op jit(solution)/shard_map/accumulate/pallas_call | solution.py:327
  63.3 2.5 %finish.4 = (f32[2176,1024]{1,0:T(8,128)S(1)}, bf16[256,1024]{1,0:T(8,128)(2,1)S(1)}, bf16[256,1024]{1,0:T(8,128)(2,1)S(1)}, bf16[10496,128]{1,0:T(8,128)(2,1)S(1)}, s32[32,128]{1,0:T(8,128)S(1)}) custom-call(f32[2176,1024]{1,0:T(8,128)S(1)} %accumulate.5.total_in, ...), custom_call_target="tpu_custom_call", output_to_operand_aliasing={{0}: (0, {})} | custom-call | flops 2147483648 | bytes 4096 | tf_op jit(solution)/shard_map/finish/pallas_call | solution.py:360
  70.1 1.8 %collective-permute-start.25 = (bf16[256,1024]{1,0:T(8,128)(2,1)S(1)}, bf16[256,1024]{1,0:T(8,128)(2,1)S(1)}, u32[]{:S(2)}, u32[]{:S(2)}) collective-permute-start(bf16[256,1024]{1,0:T(8,128)(2,1)S(1)} %get-tuple-element.62), channel_id=1, source_target_pairs={{0,12},{1,13},{2,14},{3,15},{4,0},{5,1},{6,2},{7,3},{8,4},{9,5},{1... | collective-permute-start | bytes 1572872 | tf_op jit(solution)/shard_map/ppermute | solution.py:47
  73.3 2.1 %collective-permute-done.26.refs_0_ = bf16[256,1024]{1,0:T(8,128)(2,1)S(1)} collective-permute-done((bf16[256,1024]{1,0:T(8,128)(2,1)S(1)}, bf16[256,1024]{1,0:T(8,128)(2,1)S(1)}, u32[]{:S(2)}, u32[]{:S(2)}) %collective-permute-start.26) | collective-permute-done | bytes 524320 | tf_op jit(solution)/shard_map/ppermute | solution.py:47
  76.5 2.0 %collective-permute-start.30 = (bf16[256,1024]{1,0:T(8,128)(2,1)S(1)}, bf16[256,1024]{1,0:T(8,128)(2,1)S(1)}, u32[]{:S(2)}, u32[]{:S(2)}) collective-permute-start(bf16[256,1024]{1,0:T(8,128)(2,1)S(1)} %get-tuple-element.67), channel_id=1, source_target_pairs={{0,12},{1,13},{2,14},{3,15},{4,0},{5,1},{6,2},{7,3},{8,4},{9,5},{1... | collective-permute-start | bytes 1572872 | tf_op jit(solution)/shard_map/ppermute | solution.py:47
  81.4 5.6 %collective-permute-done.28.refs_2_.refs_1_ = bf16[256,1024]{1,0:T(8,128)(2,1)S(1)} collective-permute-done((bf16[256,1024]{1,0:T(8,128)(2,1)S(1)}, bf16[256,1024]{1,0:T(8,128)(2,1)S(1)}, u32[]{:S(2)}, u32[]{:S(2)}) %collective-permute-start.28) | collective-permute-done | bytes 524320 | tf_op jit(solution)/shard_map/ppermute | solution.py:47
  88.7 2.2 %collective-permute-start.32 = (bf16[128,1024]{1,0:T(8,128)(2,1)S(1)}, bf16[128,1024]{1,0:T(8,128)(2,1)S(1)}, u32[]{:S(2)}, u32[]{:S(2)}) collective-permute-start(bf16[128,1024]{1,0:T(8,128)(2,1)S(1)} %get-tuple-element.69), channel_id=1, source_target_pairs={{0,1},{1,2},{2,3},{3,0},{4,5},{5,6},{6,7},{7,4},{8,9},{9,10},{10,1... | collective-permute-start | bytes 786440 | tf_op jit(solution)/shard_map/ppermute | solution.py:51
  91.4 2.8 %collective-permute-done.31.refs_2_ = bf16[128,1024]{1,0:T(8,128)(2,1)S(1)} collective-permute-done((bf16[128,1024]{1,0:T(8,128)(2,1)S(1)}, bf16[128,1024]{1,0:T(8,128)(2,1)S(1)}, u32[]{:S(2)}, u32[]{:S(2)}) %collective-permute-start.31) | collective-permute-done | bytes 262176 | tf_op jit(solution)/shard_map/ppermute | solution.py:51
  94.2 3.0 %collective-permute-done.32.refs_3_ = bf16[128,1024]{1,0:T(8,128)(2,1)S(1)} collective-permute-done((bf16[128,1024]{1,0:T(8,128)(2,1)S(1)}, bf16[128,1024]{1,0:T(8,128)(2,1)S(1)}, u32[]{:S(2)}, u32[]{:S(2)}) %collective-permute-start.32) | collective-permute-done | bytes 262176 | tf_op jit(solution)/shard_map/ppermute | solution.py:51
  (64 shorter events, 30.6 us)
Async XLA Ops:
  1.6 13.5 %collective-permute-start = (bf16[1040,128]{1,0:T(8,128)(2,1)S(1)}, bf16[1040,128]{1,0:T(8,128)(2,1)S(1)}, u32[]{:S(2)}, u32[]{:S(2)}) collective-permute-start(bf16[1040,128]{1,0:T(8,128)(2,1)S(1)} %get-tuple-element.39), channel_id=1, source_target_pairs={{0,8},{1,9},{2,10},{3,11},{4,12},{5,13},{6,14},{7,15},{8,0},{9,1},... | collective-permute-start | bytes 798728 | tf_op jit(solution)/shard_map/ppermute | solution.py:47
  6.1 9.0 %collective-permute-start.1 = (bf16[1040,128]{1,0:T(8,128)(2,1)S(1)}, bf16[1040,128]{1,0:T(8,128)(2,1)S(1)}, u32[]{:S(2)}, u32[]{:S(2)}) collective-permute-start(bf16[1040,128]{1,0:T(8,128)(2,1)S(1)} %get-tuple-element.40), channel_id=1, source_target_pairs={{0,4},{1,5},{2,6},{3,7},{4,8},{5,9},{6,10},{7,11},{8,12},{9,13},{1... | collective-permute-start | bytes 798728 | tf_op jit(solution)/shard_map/ppermute | solution.py:47
  6.9 8.3 %collective-permute-start.2 = (bf16[1040,128]{1,0:T(8,128)(2,1)S(1)}, bf16[1040,128]{1,0:T(8,128)(2,1)S(1)}, u32[]{:S(2)}, u32[]{:S(2)}) collective-permute-start(bf16[1040,128]{1,0:T(8,128)(2,1)S(1)} %get-tuple-element.41), channel_id=1, source_target_pairs={{0,12},{1,13},{2,14},{3,15},{4,0},{5,1},{6,2},{7,3},{8,4},{9,5},{1... | collective-permute-start | bytes 798728 | tf_op jit(solution)/shard_map/ppermute | solution.py:47
  8.8 14.4 %collective-permute-start.12 = (bf16[2064,128]{1,0:T(8,128)(2,1)S(1)}, bf16[2064,128]{1,0:T(8,128)(2,1)S(1)}, u32[]{:S(2)}, u32[]{:S(2)}) collective-permute-start(bf16[2064,128]{1,0:T(8,128)(2,1)S(1)} %get-tuple-element.46), channel_id=1, source_target_pairs={{0,64},{16,80},{32,96},{48,112},{64,0},{80,16},{96,32},{112,48},{1... | collective-permute-start | bytes 1585160 | tf_op jit(solution)/shard_map/ppermute | solution.py:55
  15.3 9.1 %collective-permute-start.3 = (bf16[1040,128]{1,0:T(8,128)(2,1)S(1)}, bf16[1040,128]{1,0:T(8,128)(2,1)S(1)}, u32[]{:S(2)}, u32[]{:S(2)}) collective-permute-start(bf16[1040,128]{1,0:T(8,128)(2,1)S(1)} %get-tuple-element.43), channel_id=1, source_target_pairs={{0,2},{1,3},{2,0},{3,1},{4,6},{5,7},{6,4},{7,5},{8,10},{9,11},{10,... | collective-permute-start | bytes 798728 | tf_op jit(solution)/shard_map/ppermute | solution.py:51
  18.1 7.6 %collective-permute-start.4 = (bf16[1040,128]{1,0:T(8,128)(2,1)S(1)}, bf16[1040,128]{1,0:T(8,128)(2,1)S(1)}, u32[]{:S(2)}, u32[]{:S(2)}) collective-permute-start(bf16[1040,128]{1,0:T(8,128)(2,1)S(1)} %get-tuple-element.44), channel_id=1, source_target_pairs={{0,1},{1,2},{2,3},{3,0},{4,5},{5,6},{6,7},{7,4},{8,9},{9,10},{10,1... | collective-permute-start | bytes 798728 | tf_op jit(solution)/shard_map/ppermute | solution.py:51
  18.4 11.1 %collective-permute-start.8 = (bf16[1040,128]{1,0:T(8,128)(2,1)S(1)}, bf16[1040,128]{1,0:T(8,128)(2,1)S(1)}, u32[]{:S(2)}, u32[]{:S(2)}) collective-permute-start(bf16[1040,128]{1,0:T(8,128)(2,1)S(1)} %get-tuple-element.42.after_ref), channel_id=1, source_target_pairs={{0,16},{16,0},{32,48},{48,32},{64,80},{80,64},{96,112},{112,96},{1... | collective-permute-start | bytes 798728 | tf_op jit(solution)/shard_map/ppermute | solution.py:59
  24.3 8.0 %collective-permute-start.13 = (bf16[1040,128]{1,0:T(8,128)(2,1)S(1)}, bf16[1040,128]{1,0:T(8,128)(2,1)S(1)}, u32[]{:S(2)}, u32[]{:S(2)}) collective-permute-start(bf16[1040,128]{1,0:T(8,128)(2,1)S(1)} %get-tuple-element.48), channel_id=1, source_target_pairs={{0,8},{1,9},{2,10},{3,11},{4,12},{5,13},{6,14},{7,15},{8,0},{9,1},... | collective-permute-start | bytes 798728 | tf_op jit(solution)/shard_map/ppermute | solution.py:47
  24.4 9.7 %collective-permute-start.14 = (bf16[1040,128]{1,0:T(8,128)(2,1)S(1)}, bf16[1040,128]{1,0:T(8,128)(2,1)S(1)}, u32[]{:S(2)}, u32[]{:S(2)}) collective-permute-start(bf16[1040,128]{1,0:T(8,128)(2,1)S(1)} %get-tuple-element.49), channel_id=1, source_target_pairs={{0,4},{1,5},{2,6},{3,7},{4,8},{5,9},{6,10},{7,11},{8,12},{9,13},{1... | collective-permute-start | bytes 798728 | tf_op jit(solution)/shard_map/ppermute | solution.py:47
  25.7 10.8 %collective-permute-start.15 = (bf16[1040,128]{1,0:T(8,128)(2,1)S(1)}, bf16[1040,128]{1,0:T(8,128)(2,1)S(1)}, u32[]{:S(2)}, u32[]{:S(2)}) collective-permute-start(bf16[1040,128]{1,0:T(8,128)(2,1)S(1)} %get-tuple-element.50), channel_id=1, source_target_pairs={{0,12},{1,13},{2,14},{3,15},{4,0},{5,1},{6,2},{7,3},{8,4},{9,5},{1... | collective-permute-start | bytes 798728 | tf_op jit(solution)/shard_map/ppermute | solution.py:47
  27.3 9.3 %collective-permute-start.9 = (bf16[1040,128]{1,0:T(8,128)(2,1)S(1)}, bf16[1040,128]{1,0:T(8,128)(2,1)S(1)}, u32[]{:S(2)}, u32[]{:S(2)}) collective-permute-start(bf16[1040,128]{1,0:T(8,128)(2,1)S(1)} %collective-permute-done.3), channel_id=1, source_target_pairs={{0,16},{16,0},{32,48},{48,32},{64,80},{80,64},{96,112},{112,96},{1... | collective-permute-start | bytes 798728 | tf_op jit(solution)/shard_map/ppermute | solution.py:59
  29.6 25.7 %collective-permute-start.7 = (bf16[4160,128]{1,0:T(8,128)(2,1)S(1)}, bf16[4160,128]{1,0:T(8,128)(2,1)S(1)}, u32[]{:S(2)}, u32[]{:S(2)}) collective-permute-start(bf16[4160,128]{1,0:T(8,128)(2,1)S(1)} %constant_dynamic-update-slice_fusion.refs_1_.after), channel_id=1, source_target_pairs={{0,96},{16,112},{32,0},{48,16},{64,32},{80,48},{96,64},{112,80},{1... | collective-permute-start | bytes 3194888 | tf_op jit(solution)/shard_map/ppermute | solution.py:55
  32.4 24.6 %collective-permute-start.6 = (bf16[4160,128]{1,0:T(8,128)(2,1)S(1)}, bf16[4160,128]{1,0:T(8,128)(2,1)S(1)}, u32[]{:S(2)}, u32[]{:S(2)}) collective-permute-start(bf16[4160,128]{1,0:T(8,128)(2,1)S(1)} %constant_dynamic-update-slice_fusion.refs_1_.after), channel_id=1, source_target_pairs={{0,32},{16,48},{32,64},{48,80},{64,96},{80,112},{96,0},{112,16},{1... | collective-permute-start | bytes 3194888 | tf_op jit(solution)/shard_map/ppermute | solution.py:55
  36.6 8.0 %collective-permute-start.16 = (bf16[1040,128]{1,0:T(8,128)(2,1)S(1)}, bf16[1040,128]{1,0:T(8,128)(2,1)S(1)}, u32[]{:S(2)}, u32[]{:S(2)}) collective-permute-start(bf16[1040,128]{1,0:T(8,128)(2,1)S(1)} %get-tuple-element.52), channel_id=1, source_target_pairs={{0,2},{1,3},{2,0},{3,1},{4,6},{5,7},{6,4},{7,5},{8,10},{9,11},{10,... | collective-permute-start | bytes 798728 | tf_op jit(solution)/shard_map/ppermute | solution.py:51
  37.7 8.9 %collective-permute-start.17 = (bf16[1040,128]{1,0:T(8,128)(2,1)S(1)}, bf16[1040,128]{1,0:T(8,128)(2,1)S(1)}, u32[]{:S(2)}, u32[]{:S(2)}) collective-permute-start(bf16[1040,128]{1,0:T(8,128)(2,1)S(1)} %get-tuple-element.53), channel_id=1, source_target_pairs={{0,1},{1,2},{2,3},{3,0},{4,5},{5,6},{6,7},{7,4},{8,9},{9,10},{10,1... | collective-permute-start | bytes 798728 | tf_op jit(solution)/shard_map/ppermute | solution.py:51
  38.0 9.9 %collective-permute-start.18 = (bf16[1040,128]{1,0:T(8,128)(2,1)S(1)}, bf16[1040,128]{1,0:T(8,128)(2,1)S(1)}, u32[]{:S(2)}, u32[]{:S(2)}) collective-permute-start(bf16[1040,128]{1,0:T(8,128)(2,1)S(1)} %get-tuple-element.54), channel_id=1, source_target_pairs={{0,3},{1,0},{2,1},{3,2},{4,7},{5,4},{6,5},{7,6},{8,11},{9,8},{10,9... | collective-permute-start | bytes 798728 | tf_op jit(solution)/shard_map/ppermute | solution.py:51
  65.8 9.6 %collective-permute-start.26 = (bf16[256,1024]{1,0:T(8,128)(2,1)S(1)}, bf16[256,1024]{1,0:T(8,128)(2,1)S(1)}, u32[]{:S(2)}, u32[]{:S(2)}) collective-permute-start(bf16[256,1024]{1,0:T(8,128)(2,1)S(1)} %get-tuple-element.63), channel_id=1, source_target_pairs={{0,4},{1,5},{2,6},{3,7},{4,8},{5,9},{6,10},{7,11},{8,12},{9,13},{1... | collective-permute-start | bytes 1572872 | tf_op jit(solution)/shard_map/ppermute | solution.py:47
  67.2 8.3 %collective-permute-start.27 = (bf16[256,1024]{1,0:T(8,128)(2,1)S(1)}, bf16[256,1024]{1,0:T(8,128)(2,1)S(1)}, u32[]{:S(2)}, u32[]{:S(2)}) collective-permute-start(bf16[256,1024]{1,0:T(8,128)(2,1)S(1)} %get-tuple-element.64), channel_id=1, source_target_pairs={{0,12},{1,13},{2,14},{3,15},{4,0},{5,1},{6,2},{7,3},{8,4},{9,5},{1... | collective-permute-start | bytes 1572872 | tf_op jit(solution)/shard_map/ppermute | solution.py:47
  70.1 11.1 %collective-permute-start.25 = (bf16[256,1024]{1,0:T(8,128)(2,1)S(1)}, bf16[256,1024]{1,0:T(8,128)(2,1)S(1)}, u32[]{:S(2)}, u32[]{:S(2)}) collective-permute-start(bf16[256,1024]{1,0:T(8,128)(2,1)S(1)} %get-tuple-element.62), channel_id=1, source_target_pairs={{0,12},{1,13},{2,14},{3,15},{4,0},{5,1},{6,2},{7,3},{8,4},{9,5},{1... | collective-permute-start | bytes 1572872 | tf_op jit(solution)/shard_map/ppermute | solution.py:47
  71.9 9.5 %collective-permute-start.29 = (bf16[256,1024]{1,0:T(8,128)(2,1)S(1)}, bf16[256,1024]{1,0:T(8,128)(2,1)S(1)}, u32[]{:S(2)}, u32[]{:S(2)}) collective-permute-start(bf16[256,1024]{1,0:T(8,128)(2,1)S(1)} %get-tuple-element.66), channel_id=1, source_target_pairs={{0,4},{1,5},{2,6},{3,7},{4,8},{5,9},{6,10},{7,11},{8,12},{9,13},{1... | collective-permute-start | bytes 1572872 | tf_op jit(solution)/shard_map/ppermute | solution.py:47
  75.8 11.3 %collective-permute-start.28 = (bf16[256,1024]{1,0:T(8,128)(2,1)S(1)}, bf16[256,1024]{1,0:T(8,128)(2,1)S(1)}, u32[]{:S(2)}, u32[]{:S(2)}) collective-permute-start(bf16[256,1024]{1,0:T(8,128)(2,1)S(1)} %get-tuple-element.65), channel_id=1, source_target_pairs={{0,4},{1,5},{2,6},{3,7},{4,8},{5,9},{6,10},{7,11},{8,12},{9,13},{1... | collective-permute-start | bytes 1572872 | tf_op jit(solution)/shard_map/ppermute | solution.py:47
  76.5 10.6 %collective-permute-start.30 = (bf16[256,1024]{1,0:T(8,128)(2,1)S(1)}, bf16[256,1024]{1,0:T(8,128)(2,1)S(1)}, u32[]{:S(2)}, u32[]{:S(2)}) collective-permute-start(bf16[256,1024]{1,0:T(8,128)(2,1)S(1)} %get-tuple-element.67), channel_id=1, source_target_pairs={{0,12},{1,13},{2,14},{3,15},{4,0},{5,1},{6,2},{7,3},{8,4},{9,5},{1... | collective-permute-start | bytes 1572872 | tf_op jit(solution)/shard_map/ppermute | solution.py:47
  87.3 6.9 %collective-permute-start.31 = (bf16[128,1024]{1,0:T(8,128)(2,1)S(1)}, bf16[128,1024]{1,0:T(8,128)(2,1)S(1)}, u32[]{:S(2)}, u32[]{:S(2)}) collective-permute-start(bf16[128,1024]{1,0:T(8,128)(2,1)S(1)} %get-tuple-element.68), channel_id=1, source_target_pairs={{0,2},{1,3},{2,0},{3,1},{4,6},{5,7},{6,4},{7,5},{8,10},{9,11},{10,... | collective-permute-start | bytes 786440 | tf_op jit(solution)/shard_map/ppermute | solution.py:51
  88.7 8.4 %collective-permute-start.32 = (bf16[128,1024]{1,0:T(8,128)(2,1)S(1)}, bf16[128,1024]{1,0:T(8,128)(2,1)S(1)}, u32[]{:S(2)}, u32[]{:S(2)}) collective-permute-start(bf16[128,1024]{1,0:T(8,128)(2,1)S(1)} %get-tuple-element.69), channel_id=1, source_target_pairs={{0,1},{1,2},{2,3},{3,0},{4,5},{5,6},{6,7},{7,4},{8,9},{9,10},{10,1... | collective-permute-start | bytes 786440 | tf_op jit(solution)/shard_map/ppermute | solution.py:51
  (10 other events, 37.6 us)

commit v5 on v4

--- a/solution.py
+++ b/solution.py
@@ -467,10 +467,10 @@
     far = second_steps(far_turned)
     total = accumulate(None, ints, [own] + [send_core(v) for v in near])
     far_other = [send_core(v) for v in [join(far[:1], total)] + far[1:]]
-    total = accumulate(total, ints, far + far_other)
+    total, _, far = finish(total, ints, far + far_other, (0, 12), [], 2**20)
     up, down, total = lax.optimization_barrier((up, down, total))
     late = [send_core(up), send_core(down)]
-    total = accumulate(total, ints, [up, down])
+    total, _, middle = finish(total, ints, [up, down], (0, 12), [], 2**20)
 
     total, (two_ahead, two_behind), late = finish(total, ints, late, (0, 4), [(0, 2), (2, 2)], 2**31)
     from_behind, from_ahead = send_first(two_ahead, 1), send_first(two_behind, -1)
@@ -479,7 +479,8 @@
     total, _, late = finish(total, ints, late, (8, 12), [], 2**31)
     ahead, behind = fold(total, [from_behind, from_ahead], [(8, 2, [(0, 0)]), (10, 2, [(1, 0)])], BF16, pltpu.VMEM)
     got += [send_first(ahead, 1), send_first(behind, -1)]
-    total, _, late = finish(total, ints, late, (12, 16), [], 2**31)
+    for packed in (far, middle, late):
+        total, _, _ = finish(total, ints, packed, (12, 16), [], 2**31)
     outs = [(13, 1, [(0, 1), (2, 1)]), (14, 1, [(1, 0), (3, 0)]), (15, 1, [(1, 1), (3, 1)])]
     rest = fold(total, got, outs, BF16, pltpu.VMEM)
     last = [got[0], got[2]] + [send_second(rest[d - 1], d) for d in (2, 1, 3)]

time: 100 us -> 99.3 us (level)
  Pallas kernels: 26.1 us -> 28.5 us
  waiting for transfers between devices: 24.4 us -> 22.3 us
  starting transfers between devices: 47.9 us -> 46.9 us
    pallas_call x4 -> x8, Pallas kernels: 6.8 us -> 16.7 us  [finish(): pl.pallas_call(kernel, in_specs=[VMEM] * (2 + len(late)), out_specs=[VMEM...]
    pallas_call x3 -> x1, Pallas kernels: 11.7 us -> 4.19 us  [accumulate(): pl.pallas_call(kernel, in_specs=[VMEM] * (len(old) + 1 + many), out_specs...]
    ppermute x12, waiting for transfers between devices: 10.7 us -> 7.28 us  [send_first(): return lax.ppermute(v, ('row', 'col'), plane_perm(step, False))]
  transfers between devices with their start and end apart: 34 -> 34, of which waited for: 19 -> 16; matrix products, arithmetic and copies ran while one was open for 0% -> 0% of each run, Pallas kernels for 21% -> 24%
where the time goes in v5:
time: 99.3 us; the launch traced here: 98.1 us
  starting transfers between devices  46.9 us (47%)
  Pallas kernels  28.5 us (29%)
  waiting for transfers between devices  22.3 us (22%)
    ppermute x12, starting transfers between devices, send_first(): return lax.ppermute(v, ('row', 'col'), plane_perm(step, False))  17.1 us
    pallas_call x8, Pallas kernels, finish(): pl.pallas_call(kernel, in_specs=[VMEM] * (2 + len(late)), out_specs=[VMEM...  16.7 us
    ppermute x10, starting transfers between devices, send_core(): return lax.ppermute(v, 'row', CORE_PERM)  13.6 us
    ppermute x9, starting transfers between devices, send_second(): return lax.ppermute(v, ('row', 'col'), plane_perm(step, True))  10 us
    ppermute x12, waiting for transfers between devices, send_first(): return lax.ppermute(v, ('row', 'col'), plane_perm(step, False))  7.28 us
    ppermute x9, waiting for transfers between devices, send_second(): return lax.ppermute(v, ('row', 'col'), plane_perm(step, True))  6.45 us
    ppermute x3, starting transfers between devices, send_y(): return lax.ppermute(v, 'row', row_perm(step))  6.14 us
    ppermute x3, waiting for transfers between devices, send_y(): return lax.ppermute(v, 'row', row_perm(step))  4.99 us
  transfers between devices with their start and end apart: 34, of which 16 were waited for; matrix products, arithmetic and copies ran while one was open for 0% of the time, Pallas kernels for 24%

profile of v5, /device:TPU:1, one launch (start us, length us, event | category | flops | bytes accessed | tf_op | source)
XLA Modules:
  0.0 98.1 jit_solution(11236922147461390486)
XLA Ops:
  1.6 4.5 %collective-permute-start = (bf16[1040,128]{1,0:T(8,128)(2,1)S(1)}, bf16[1040,128]{1,0:T(8,128)(2,1)S(1)}, u32[]{:S(2)}, u32[]{:S(2)}) collective-permute-start(bf16[1040,128]{1,0:T(8,128)(2,1)S(1)} %get-tuple-element.45), channel_id=1, source_target_pairs={{0,8},{1,9},{2,10},{3,11},{4,12},{5,13},{6,14},{7,15},{8,0},{9,1},... | collective-permute-start | bytes 798728 | tf_op jit(solution)/shard_map/ppermute | solution.py:47
  6.9 1.9 %collective-permute-start.2 = (bf16[1040,128]{1,0:T(8,128)(2,1)S(1)}, bf16[1040,128]{1,0:T(8,128)(2,1)S(1)}, u32[]{:S(2)}, u32[]{:S(2)}) collective-permute-start(bf16[1040,128]{1,0:T(8,128)(2,1)S(1)} %get-tuple-element.47), channel_id=1, source_target_pairs={{0,12},{1,13},{2,14},{3,15},{4,0},{5,1},{6,2},{7,3},{8,4},{9,5},{1... | collective-permute-start | bytes 798728 | tf_op jit(solution)/shard_map/ppermute | solution.py:47
  8.8 2.9 %collective-permute-start.12 = (bf16[2064,128]{1,0:T(8,128)(2,1)S(1)}, bf16[2064,128]{1,0:T(8,128)(2,1)S(1)}, u32[]{:S(2)}, u32[]{:S(2)}) collective-permute-start(bf16[2064,128]{1,0:T(8,128)(2,1)S(1)} %get-tuple-element.52), channel_id=1, source_target_pairs={{0,64},{16,80},{32,96},{48,112},{64,0},{80,16},{96,32},{112,48},{1... | collective-permute-start | bytes 1585160 | tf_op jit(solution)/shard_map/ppermute | solution.py:55
  11.7 3.4 %load.1.after.refs_0_.ints_ref = bf16[4096,1024]{1,0:T(8,128)(2,1)S(1)} custom-call(bf16[4096,1024]{1,0:T(8,128)(2,1)} %src.1), custom_call_target="tpu_custom_call" | custom-call | flops 1048576 | bytes 4096 | tf_op jit(solution)/shard_map/load/pallas_call | solution.py:445
  15.3 2.8 %collective-permute-start.3 = (bf16[1040,128]{1,0:T(8,128)(2,1)S(1)}, bf16[1040,128]{1,0:T(8,128)(2,1)S(1)}, u32[]{:S(2)}, u32[]{:S(2)}) collective-permute-start(bf16[1040,128]{1,0:T(8,128)(2,1)S(1)} %get-tuple-element.49), channel_id=1, source_target_pairs={{0,2},{1,3},{2,0},{3,1},{4,6},{5,7},{6,4},{7,5},{8,10},{9,11},{10,... | collective-permute-start | bytes 798728 | tf_op jit(solution)/shard_map/ppermute | solution.py:51
  18.4 2.8 %collective-permute-start.8 = (bf16[1040,128]{1,0:T(8,128)(2,1)S(1)}, bf16[1040,128]{1,0:T(8,128)(2,1)S(1)}, u32[]{:S(2)}, u32[]{:S(2)}) collective-permute-start(bf16[1040,128]{1,0:T(8,128)(2,1)S(1)} %get-tuple-element.48.after_ref), channel_id=1, source_target_pairs={{0,16},{16,0},{32,48},{48,32},{64,80},{80,64},{96,112},{112,96},{1... | collective-permute-start | bytes 798728 | tf_op jit(solution)/shard_map/ppermute | solution.py:59
  27.4 2.2 %collective-permute-start.9 = (bf16[1040,128]{1,0:T(8,128)(2,1)S(1)}, bf16[1040,128]{1,0:T(8,128)(2,1)S(1)}, u32[]{:S(2)}, u32[]{:S(2)}) collective-permute-start(bf16[1040,128]{1,0:T(8,128)(2,1)S(1)} %collective-permute-done.3), channel_id=1, source_target_pairs={{0,16},{16,0},{32,48},{48,32},{64,80},{80,64},{96,112},{112,96},{1... | collective-permute-start | bytes 798728 | tf_op jit(solution)/shard_map/ppermute | solution.py:59
  29.6 2.8 %collective-permute-start.7 = (bf16[4160,128]{1,0:T(8,128)(2,1)S(1)}, bf16[4160,128]{1,0:T(8,128)(2,1)S(1)}, u32[]{:S(2)}, u32[]{:S(2)}) collective-permute-start(bf16[4160,128]{1,0:T(8,128)(2,1)S(1)} %constant_dynamic-update-slice_fusion.refs_1_.after), channel_id=1, source_target_pairs={{0,96},{16,112},{32,0},{48,16},{64,32},{80,48},{96,64},{112,80},{1... | collective-permute-start | bytes 3194888 | tf_op jit(solution)/shard_map/ppermute | solution.py:55
  34.1 2.4 %collective-permute-start.10 = (bf16[1040,128]{1,0:T(8,128)(2,1)S(1)}, bf16[1040,128]{1,0:T(8,128)(2,1)S(1)}, u32[]{:S(2)}, u32[]{:S(2)}) collective-permute-start(bf16[1040,128]{1,0:T(8,128)(2,1)S(1)} %collective-permute-done.4), channel_id=1, source_target_pairs={{0,16},{16,0},{32,48},{48,32},{64,80},{80,64},{96,112},{112,96},{1... | collective-permute-start | bytes 798728 | tf_op jit(solution)/shard_map/ppermute | solution.py:59
  38.1 2.3 %collective-permute-start.18 = (bf16[1040,128]{1,0:T(8,128)(2,1)S(1)}, bf16[1040,128]{1,0:T(8,128)(2,1)S(1)}, u32[]{:S(2)}, u32[]{:S(2)}) collective-permute-start(bf16[1040,128]{1,0:T(8,128)(2,1)S(1)} %get-tuple-element.60), channel_id=1, source_target_pairs={{0,3},{1,0},{2,1},{3,2},{4,7},{5,4},{6,5},{7,6},{8,11},{9,8},{10,9... | collective-permute-start | bytes 798728 | tf_op jit(solution)/shard_map/ppermute | solution.py:51
  40.4 4.2 %accumulate.1.after_ref.total_in = f32[2176,1024]{1,0:T(8,128)S(1)} custom-call(bf16[4096,1024]{1,0:T(8,128)(2,1)S(1)} %load.1.after.refs_0_.ints_ref, bf16[4160,128]{1,0:T(8,128)(2,1)S(1)} %constant_dynamic-update-slice_fusion.refs_1_.after, bf16[1040,128]{1,0:T(8,128)(2,1)S(1)} %collective-permute-done.8.refs_2_, ...), custom_call_target="tpu_custom_call" | custom-call | flops 1048576 | bytes 4096 | tf_op jit(solution)/shard_map/accumulate/pallas_call | solution.py:327
  44.6 1.9 %collective-permute-start.19 = (bf16[1040,128]{1,0:T(8,128)(2,1)S(1)}, bf16[1040,128]{1,0:T(8,128)(2,1)S(1)}, u32[]{:S(2)}, u32[]{:S(2)}) collective-permute-start(bf16[1040,128]{1,0:T(8,128)(2,1)S(1)} %join.1), channel_id=1, source_target_pairs={{0,16},{16,0},{32,48},{48,32},{64,80},{80,64},{96,112},{112,96},{1... | collective-permute-start | bytes 798728 | tf_op jit(solution)/shard_map/ppermute | solution.py:59
  49.9 3.3 %finish.8 = (f32[2176,1024]{1,0:T(8,128)S(1)}, bf16[10496,128]{1,0:T(8,128)(2,1)S(1)}, s32[32,128]{1,0:T(8,128)S(1)}) custom-call(f32[2176,1024]{1,0:T(8,128)S(1)} %accumulate.1.after_ref.total_in, bf16[4096,1024]{1,0:T(8,128)(2,1)S(1)} %load.1.after.refs_0_.ints_ref, ...), custom_call_target="tpu_custom_call", output_to_operand_aliasing={{0}: (0, {})} | custom-call | flops 1048576 | bytes 4096 | tf_op jit(solution)/shard_map/finish/pallas_call | solution.py:360
  53.2 2.0 %collective-permute-done.7.refs_1_ = bf16[4160,128]{1,0:T(8,128)(2,1)S(1)} collective-permute-done((bf16[4160,128]{1,0:T(8,128)(2,1)S(1)}, bf16[4160,128]{1,0:T(8,128)(2,1)S(1)}, u32[]{:S(2)}, u32[]{:S(2)}) %collective-permute-start.7) | collective-permute-done | bytes 1064992 | tf_op jit(solution)/shard_map/ppermute | solution.py:55
  57.0 2.5 %collective-permute-start.23 = (bf16[4160,128]{1,0:T(8,128)(2,1)S(1)}, bf16[4160,128]{1,0:T(8,128)(2,1)S(1)}, u32[]{:S(2)}, u32[]{:S(2)}) collective-permute-start(bf16[4160,128]{1,0:T(8,128)(2,1)S(1)} %collective-permute-done.6.refs_0_), channel_id=1, source_target_pairs={{0,16},{16,0},{32,48},{48,32},{64,80},{80,64},{96,112},{112,96},{1... | collective-permute-start | bytes 3194888 | tf_op jit(solution)/shard_map/ppermute | solution.py:59
  59.5 2.8 %finish.9 = (f32[2176,1024]{1,0:T(8,128)S(1)}, bf16[10496,128]{1,0:T(8,128)(2,1)S(1)}, s32[32,128]{1,0:T(8,128)S(1)}) custom-call(f32[2176,1024]{1,0:T(8,128)S(1)} %get-tuple-element.62.total_in, bf16[4096,1024]{1,0:T(8,128)(2,1)S(1)} %load.1.after.refs_0_.ints_ref, ...), custom_call_target="tpu_custom_call", output_to_operand_aliasing={{0}: (0, {})} | custom-call | flops 1048576 | bytes 4096 | tf_op jit(solution)/shard_map/finish/pallas_call | solution.py:360
  63.3 2.5 %finish.10 = (f32[2176,1024]{1,0:T(8,128)S(1)}, bf16[256,1024]{1,0:T(8,128)(2,1)S(1)}, bf16[256,1024]{1,0:T(8,128)(2,1)S(1)}, bf16[10496,128]{1,0:T(8,128)(2,1)S(1)}, s32[32,128]{1,0:T(8,128)S(1)}) custom-call(f32[2176,1024]{1,0:T(8,128)S(1)} %get-tuple-element.65.total_in, ...), custom_call_target="tpu_custom_call", output_to_operand_aliasing={{0}: (0, {})} | custom-call | flops 2147483648 | bytes 4096 | tf_op jit(solution)/shard_map/finish/pallas_call | solution.py:360
  68.6 2.0 %finish.11 = (f32[2176,1024]{1,0:T(8,128)S(1)}, bf16[256,1024]{1,0:T(8,128)(2,1)S(1)}, bf16[256,1024]{1,0:T(8,128)(2,1)S(1)}) custom-call(f32[2176,1024]{1,0:T(8,128)S(1)} %get-tuple-element.66.total_in, bf16[4096,1024]{1,0:T(8,128)(2,1)S(1)} %load.1.after.refs_0_.ints_ref, ...), custom_call_target="tpu_custom_call", output_to_operand_aliasing={{0}: (0, {})} | custom-call | flops 2147483648 | bytes 4096 | tf_op jit(solution)/shard_map/finish/pallas_call | solution.py:360
  73.5 1.9 %collective-permute-done.26.refs_0_ = bf16[256,1024]{1,0:T(8,128)(2,1)S(1)} collective-permute-done((bf16[256,1024]{1,0:T(8,128)(2,1)S(1)}, bf16[256,1024]{1,0:T(8,128)(2,1)S(1)}, u32[]{:S(2)}, u32[]{:S(2)}) %collective-permute-start.26) | collective-permute-done | bytes 524320 | tf_op jit(solution)/shard_map/ppermute | solution.py:47
  79.9 1.9 %finish.14.total_in = f32[2176,1024]{1,0:T(8,128)S(1)} custom-call(f32[2176,1024]{1,0:T(8,128)S(1)} %finish.13.total_in, bf16[4096,1024]{1,0:T(8,128)(2,1)S(1)} %load.1.after.refs_0_.ints_ref, bf16[10496,128]{1,0:T(8,128)(2,1)S(1)} %get-tuple-element.72.refs_0_, s32[32,128]{1,0:T(8,128)S(1)} %get-tuple-element.73.refs_1_), custom_call_target="tpu_custom_call", output_to_operand_aliasing={{}: (0, {})} | custom-call | flops 2147483648 | bytes 4096 | tf_op jit(solution)/shard_map/finish/pallas_call | solution.py:360
  83.2 3.8 %collective-permute-done.28.refs_2_.refs_1_ = bf16[256,1024]{1,0:T(8,128)(2,1)S(1)} collective-permute-done((bf16[256,1024]{1,0:T(8,128)(2,1)S(1)}, bf16[256,1024]{1,0:T(8,128)(2,1)S(1)}, u32[]{:S(2)}, u32[]{:S(2)}) %collective-permute-start.28) | collective-permute-done | bytes 524320 | tf_op jit(solution)/shard_map/ppermute | solution.py:47
  88.5 2.4 %collective-permute-start.33 = (bf16[128,1024]{1,0:T(8,128)(2,1)S(1)}, bf16[128,1024]{1,0:T(8,128)(2,1)S(1)}, u32[]{:S(2)}, u32[]{:S(2)}) collective-permute-start(bf16[128,1024]{1,0:T(8,128)(2,1)S(1)} %get-tuple-element.82), channel_id=1, source_target_pairs={{0,3},{1,0},{2,1},{3,2},{4,7},{5,4},{6,5},{7,6},{8,11},{9,8},{10,9... | collective-permute-start | bytes 786440 | tf_op jit(solution)/shard_map/ppermute | solution.py:51
  90.9 3.6 %collective-permute-done.31.refs_2_ = bf16[128,1024]{1,0:T(8,128)(2,1)S(1)} collective-permute-done((bf16[128,1024]{1,0:T(8,128)(2,1)S(1)}, bf16[128,1024]{1,0:T(8,128)(2,1)S(1)}, u32[]{:S(2)}, u32[]{:S(2)}) %collective-permute-start.31) | collective-permute-done | bytes 262176 | tf_op jit(solution)/shard_map/ppermute | solution.py:51
  94.4 2.8 %collective-permute-done.32.refs_3_ = bf16[128,1024]{1,0:T(8,128)(2,1)S(1)} collective-permute-done((bf16[128,1024]{1,0:T(8,128)(2,1)S(1)}, bf16[128,1024]{1,0:T(8,128)(2,1)S(1)}, u32[]{:S(2)}, u32[]{:S(2)}) %collective-permute-start.32) | collective-permute-done | bytes 262176 | tf_op jit(solution)/shard_map/ppermute | solution.py:51
  (66 shorter events, 32.2 us)
Async XLA Ops:
  1.6 13.5 %collective-permute-start = (bf16[1040,128]{1,0:T(8,128)(2,1)S(1)}, bf16[1040,128]{1,0:T(8,128)(2,1)S(1)}, u32[]{:S(2)}, u32[]{:S(2)}) collective-permute-start(bf16[1040,128]{1,0:T(8,128)(2,1)S(1)} %get-tuple-element.45), channel_id=1, source_target_pairs={{0,8},{1,9},{2,10},{3,11},{4,12},{5,13},{6,14},{7,15},{8,0},{9,1},... | collective-permute-start | bytes 798728 | tf_op jit(solution)/shard_map/ppermute | solution.py:47
  6.2 9.0 %collective-permute-start.1 = (bf16[1040,128]{1,0:T(8,128)(2,1)S(1)}, bf16[1040,128]{1,0:T(8,128)(2,1)S(1)}, u32[]{:S(2)}, u32[]{:S(2)}) collective-permute-start(bf16[1040,128]{1,0:T(8,128)(2,1)S(1)} %get-tuple-element.46), channel_id=1, source_target_pairs={{0,4},{1,5},{2,6},{3,7},{4,8},{5,9},{6,10},{7,11},{8,12},{9,13},{1... | collective-permute-start | bytes 798728 | tf_op jit(solution)/shard_map/ppermute | solution.py:47
  6.9 8.3 %collective-permute-start.2 = (bf16[1040,128]{1,0:T(8,128)(2,1)S(1)}, bf16[1040,128]{1,0:T(8,128)(2,1)S(1)}, u32[]{:S(2)}, u32[]{:S(2)}) collective-permute-start(bf16[1040,128]{1,0:T(8,128)(2,1)S(1)} %get-tuple-element.47), channel_id=1, source_target_pairs={{0,12},{1,13},{2,14},{3,15},{4,0},{5,1},{6,2},{7,3},{8,4},{9,5},{1... | collective-permute-start | bytes 798728 | tf_op jit(solution)/shard_map/ppermute | solution.py:47
  8.8 14.4 %collective-permute-start.12 = (bf16[2064,128]{1,0:T(8,128)(2,1)S(1)}, bf16[2064,128]{1,0:T(8,128)(2,1)S(1)}, u32[]{:S(2)}, u32[]{:S(2)}) collective-permute-start(bf16[2064,128]{1,0:T(8,128)(2,1)S(1)} %get-tuple-element.52), channel_id=1, source_target_pairs={{0,64},{16,80},{32,96},{48,112},{64,0},{80,16},{96,32},{112,48},{1... | collective-permute-start | bytes 1585160 | tf_op jit(solution)/shard_map/ppermute | solution.py:55
  15.3 9.2 %collective-permute-start.3 = (bf16[1040,128]{1,0:T(8,128)(2,1)S(1)}, bf16[1040,128]{1,0:T(8,128)(2,1)S(1)}, u32[]{:S(2)}, u32[]{:S(2)}) collective-permute-start(bf16[1040,128]{1,0:T(8,128)(2,1)S(1)} %get-tuple-element.49), channel_id=1, source_target_pairs={{0,2},{1,3},{2,0},{3,1},{4,6},{5,7},{6,4},{7,5},{8,10},{9,11},{10,... | collective-permute-start | bytes 798728 | tf_op jit(solution)/shard_map/ppermute | solution.py:51
  18.1 7.6 %collective-permute-start.4 = (bf16[1040,128]{1,0:T(8,128)(2,1)S(1)}, bf16[1040,128]{1,0:T(8,128)(2,1)S(1)}, u32[]{:S(2)}, u32[]{:S(2)}) collective-permute-start(bf16[1040,128]{1,0:T(8,128)(2,1)S(1)} %get-tuple-element.50), channel_id=1, source_target_pairs={{0,1},{1,2},{2,3},{3,0},{4,5},{5,6},{6,7},{7,4},{8,9},{9,10},{10,1... | collective-permute-start | bytes 798728 | tf_op jit(solution)/shard_map/ppermute | solution.py:51
  18.4 11.1 %collective-permute-start.8 = (bf16[1040,128]{1,0:T(8,128)(2,1)S(1)}, bf16[1040,128]{1,0:T(8,128)(2,1)S(1)}, u32[]{:S(2)}, u32[]{:S(2)}) collective-permute-start(bf16[1040,128]{1,0:T(8,128)(2,1)S(1)} %get-tuple-element.48.after_ref), channel_id=1, source_target_pairs={{0,16},{16,0},{32,48},{48,32},{64,80},{80,64},{96,112},{112,96},{1... | collective-permute-start | bytes 798728 | tf_op jit(solution)/shard_map/ppermute | solution.py:59
  24.3 8.0 %collective-permute-start.13 = (bf16[1040,128]{1,0:T(8,128)(2,1)S(1)}, bf16[1040,128]{1,0:T(8,128)(2,1)S(1)}, u32[]{:S(2)}, u32[]{:S(2)}) collective-permute-start(bf16[1040,128]{1,0:T(8,128)(2,1)S(1)} %get-tuple-element.54), channel_id=1, source_target_pairs={{0,8},{1,9},{2,10},{3,11},{4,12},{5,13},{6,14},{7,15},{8,0},{9,1},... | collective-permute-start | bytes 798728 | tf_op jit(solution)/shard_map/ppermute | solution.py:47
  24.4 9.7 %collective-permute-start.14 = (bf16[1040,128]{1,0:T(8,128)(2,1)S(1)}, bf16[1040,128]{1,0:T(8,128)(2,1)S(1)}, u32[]{:S(2)}, u32[]{:S(2)}) collective-permute-start(bf16[1040,128]{1,0:T(8,128)(2,1)S(1)} %get-tuple-element.55), channel_id=1, source_target_pairs={{0,4},{1,5},{2,6},{3,7},{4,8},{5,9},{6,10},{7,11},{8,12},{9,13},{1... | collective-permute-start | bytes 798728 | tf_op jit(solution)/shard_map/ppermute | solution.py:47
  25.7 10.8 %collective-permute-start.15 = (bf16[1040,128]{1,0:T(8,128)(2,1)S(1)}, bf16[1040,128]{1,0:T(8,128)(2,1)S(1)}, u32[]{:S(2)}, u32[]{:S(2)}) collective-permute-start(bf16[1040,128]{1,0:T(8,128)(2,1)S(1)} %get-tuple-element.56), channel_id=1, source_target_pairs={{0,12},{1,13},{2,14},{3,15},{4,0},{5,1},{6,2},{7,3},{8,4},{9,5},{1... | collective-permute-start | bytes 798728 | tf_op jit(solution)/shard_map/ppermute | solution.py:47
  27.4 9.3 %collective-permute-start.9 = (bf16[1040,128]{1,0:T(8,128)(2,1)S(1)}, bf16[1040,128]{1,0:T(8,128)(2,1)S(1)}, u32[]{:S(2)}, u32[]{:S(2)}) collective-permute-start(bf16[1040,128]{1,0:T(8,128)(2,1)S(1)} %collective-permute-done.3), channel_id=1, source_target_pairs={{0,16},{16,0},{32,48},{48,32},{64,80},{80,64},{96,112},{112,96},{1... | collective-permute-start | bytes 798728 | tf_op jit(solution)/shard_map/ppermute | solution.py:59
  29.6 25.7 %collective-permute-start.7 = (bf16[4160,128]{1,0:T(8,128)(2,1)S(1)}, bf16[4160,128]{1,0:T(8,128)(2,1)S(1)}, u32[]{:S(2)}, u32[]{:S(2)}) collective-permute-start(bf16[4160,128]{1,0:T(8,128)(2,1)S(1)} %constant_dynamic-update-slice_fusion.refs_1_.after), channel_id=1, source_target_pairs={{0,96},{16,112},{32,0},{48,16},{64,32},{80,48},{96,64},{112,80},{1... | collective-permute-start | bytes 3194888 | tf_op jit(solution)/shard_map/ppermute | solution.py:55
  32.4 24.6 %collective-permute-start.6 = (bf16[4160,128]{1,0:T(8,128)(2,1)S(1)}, bf16[4160,128]{1,0:T(8,128)(2,1)S(1)}, u32[]{:S(2)}, u32[]{:S(2)}) collective-permute-start(bf16[4160,128]{1,0:T(8,128)(2,1)S(1)} %constant_dynamic-update-slice_fusion.refs_1_.after), channel_id=1, source_target_pairs={{0,32},{16,48},{32,64},{48,80},{64,96},{80,112},{96,0},{112,16},{1... | collective-permute-start | bytes 3194888 | tf_op jit(solution)/shard_map/ppermute | solution.py:55
  36.6 8.0 %collective-permute-start.16 = (bf16[1040,128]{1,0:T(8,128)(2,1)S(1)}, bf16[1040,128]{1,0:T(8,128)(2,1)S(1)}, u32[]{:S(2)}, u32[]{:S(2)}) collective-permute-start(bf16[1040,128]{1,0:T(8,128)(2,1)S(1)} %get-tuple-element.58), channel_id=1, source_target_pairs={{0,2},{1,3},{2,0},{3,1},{4,6},{5,7},{6,4},{7,5},{8,10},{9,11},{10,... | collective-permute-start | bytes 798728 | tf_op jit(solution)/shard_map/ppermute | solution.py:51
  37.7 8.9 %collective-permute-start.17 = (bf16[1040,128]{1,0:T(8,128)(2,1)S(1)}, bf16[1040,128]{1,0:T(8,128)(2,1)S(1)}, u32[]{:S(2)}, u32[]{:S(2)}) collective-permute-start(bf16[1040,128]{1,0:T(8,128)(2,1)S(1)} %get-tuple-element.59), channel_id=1, source_target_pairs={{0,1},{1,2},{2,3},{3,0},{4,5},{5,6},{6,7},{7,4},{8,9},{9,10},{10,1... | collective-permute-start | bytes 798728 | tf_op jit(solution)/shard_map/ppermute | solution.py:51
  38.1 9.9 %collective-permute-start.18 = (bf16[1040,128]{1,0:T(8,128)(2,1)S(1)}, bf16[1040,128]{1,0:T(8,128)(2,1)S(1)}, u32[]{:S(2)}, u32[]{:S(2)}) collective-permute-start(bf16[1040,128]{1,0:T(8,128)(2,1)S(1)} %get-tuple-element.60), channel_id=1, source_target_pairs={{0,3},{1,0},{2,1},{3,2},{4,7},{5,4},{6,5},{7,6},{8,11},{9,8},{10,9... | collective-permute-start | bytes 798728 | tf_op jit(solution)/shard_map/ppermute | solution.py:51
  65.8 9.6 %collective-permute-start.26 = (bf16[256,1024]{1,0:T(8,128)(2,1)S(1)}, bf16[256,1024]{1,0:T(8,128)(2,1)S(1)}, u32[]{:S(2)}, u32[]{:S(2)}) collective-permute-start(bf16[256,1024]{1,0:T(8,128)(2,1)S(1)} %get-tuple-element.75), channel_id=1, source_target_pairs={{0,4},{1,5},{2,6},{3,7},{4,8},{5,9},{6,10},{7,11},{8,12},{9,13},{1... | collective-permute-start | bytes 1572872 | tf_op jit(solution)/shard_map/ppermute | solution.py:47
  67.3 8.3 %collective-permute-start.27 = (bf16[256,1024]{1,0:T(8,128)(2,1)S(1)}, bf16[256,1024]{1,0:T(8,128)(2,1)S(1)}, u32[]{:S(2)}, u32[]{:S(2)}) collective-permute-start(bf16[256,1024]{1,0:T(8,128)(2,1)S(1)} %get-tuple-element.76), channel_id=1, source_target_pairs={{0,12},{1,13},{2,14},{3,15},{4,0},{5,1},{6,2},{7,3},{8,4},{9,5},{1... | collective-permute-start | bytes 1572872 | tf_op jit(solution)/shard_map/ppermute | solution.py:47
  70.5 12.7 %collective-permute-start.25 = (bf16[256,1024]{1,0:T(8,128)(2,1)S(1)}, bf16[256,1024]{1,0:T(8,128)(2,1)S(1)}, u32[]{:S(2)}, u32[]{:S(2)}) collective-permute-start(bf16[256,1024]{1,0:T(8,128)(2,1)S(1)} %get-tuple-element.74), channel_id=1, source_target_pairs={{0,12},{1,13},{2,14},{3,15},{4,0},{5,1},{6,2},{7,3},{8,4},{9,5},{1... | collective-permute-start | bytes 1572872 | tf_op jit(solution)/shard_map/ppermute | solution.py:47
  71.9 11.3 %collective-permute-start.29 = (bf16[256,1024]{1,0:T(8,128)(2,1)S(1)}, bf16[256,1024]{1,0:T(8,128)(2,1)S(1)}, u32[]{:S(2)}, u32[]{:S(2)}) collective-permute-start(bf16[256,1024]{1,0:T(8,128)(2,1)S(1)} %get-tuple-element.78), channel_id=1, source_target_pairs={{0,4},{1,5},{2,6},{3,7},{4,8},{5,9},{6,10},{7,11},{8,12},{9,13},{1... | collective-permute-start | bytes 1572872 | tf_op jit(solution)/shard_map/ppermute | solution.py:47
  75.8 11.3 %collective-permute-start.28 = (bf16[256,1024]{1,0:T(8,128)(2,1)S(1)}, bf16[256,1024]{1,0:T(8,128)(2,1)S(1)}, u32[]{:S(2)}, u32[]{:S(2)}) collective-permute-start(bf16[256,1024]{1,0:T(8,128)(2,1)S(1)} %get-tuple-element.77), channel_id=1, source_target_pairs={{0,4},{1,5},{2,6},{3,7},{4,8},{5,9},{6,10},{7,11},{8,12},{9,13},{1... | collective-permute-start | bytes 1572872 | tf_op jit(solution)/shard_map/ppermute | solution.py:47
  76.9 10.1 %collective-permute-start.30 = (bf16[256,1024]{1,0:T(8,128)(2,1)S(1)}, bf16[256,1024]{1,0:T(8,128)(2,1)S(1)}, u32[]{:S(2)}, u32[]{:S(2)}) collective-permute-start(bf16[256,1024]{1,0:T(8,128)(2,1)S(1)} %get-tuple-element.79), channel_id=1, source_target_pairs={{0,12},{1,13},{2,14},{3,15},{4,0},{5,1},{6,2},{7,3},{8,4},{9,5},{1... | collective-permute-start | bytes 1572872 | tf_op jit(solution)/shard_map/ppermute | solution.py:47
  88.2 9.0 %collective-permute-start.32 = (bf16[128,1024]{1,0:T(8,128)(2,1)S(1)}, bf16[128,1024]{1,0:T(8,128)(2,1)S(1)}, u32[]{:S(2)}, u32[]{:S(2)}) collective-permute-start(bf16[128,1024]{1,0:T(8,128)(2,1)S(1)} %get-tuple-element.81), channel_id=1, source_target_pairs={{0,1},{1,2},{2,3},{3,0},{4,5},{5,6},{6,7},{7,4},{8,9},{9,10},{10,1... | collective-permute-start | bytes 786440 | tf_op jit(solution)/shard_map/ppermute | solution.py:51
  88.5 8.7 %collective-permute-start.33 = (bf16[128,1024]{1,0:T(8,128)(2,1)S(1)}, bf16[128,1024]{1,0:T(8,128)(2,1)S(1)}, u32[]{:S(2)}, u32[]{:S(2)}) collective-permute-start(bf16[128,1024]{1,0:T(8,128)(2,1)S(1)} %get-tuple-element.82), channel_id=1, source_target_pairs={{0,3},{1,0},{2,1},{3,2},{4,7},{5,4},{6,5},{7,6},{8,11},{9,8},{10,9... | collective-permute-start | bytes 786440 | tf_op jit(solution)/shard_map/ppermute | solution.py:51
  (10 other events, 37.0 us)
